TPU v7x, 32 devices: a whole 2x2x4 slice. The times are simulated.
32 devices in a mesh: ctx: 8 (over z, x), head: 4 (over y, core).
Axes of the slice: x: 2, y: 2, z: 4, core: 2. Of those that a mesh axis runs over, the one named last changes fastest.
Arguments:
- query: bfloat16 [4096, 4096], P('ctx', 'head'), may hold values from -6 to 6
- key: bfloat16 [4096, 4096], P('ctx', 'head'), may hold values from -6 to 6
- value: bfloat16 [4096, 4096], P('ctx', 'head'), may hold values from -1040 to 1040
- log_decay: float32 [32, 4096], P('head', 'ctx'), may hold values from -1.1 to 0
- doc_lengths: int32 [8], replicated, may hold values from 1 to 2048, 4096 in all
- tile_mask: int32 [32, 20], P('ctx'), may hold values 0 or 1
- gain: float32 [4096], P('head'), may hold values from 0.25 to 1.75
Outputs:
- attended: bfloat16 [4096, 4096], P('ctx', 'head')
Inputs may be any that keep to these rules, and one draw needn't show every extreme that they name: `doc_lengths`: the documents fill the stream in order and sum to 4096 positions; the longest has exactly 2048 positions. `tile_mask`: row r is a tile of queries; column j names key tile (r // 4 - 4) * 4 + j.
All inputs are finite; a program needn't handle non-finite values. No bound on the sum of `tile_mask` on one device may be relied on, other than what follows from the above.
Results may differ from a plain program's by a relative error of at most 0.005.
Values may be sent and summed in bfloat16 or wider, within the bound.
No kernel may reach another device: no remote copies, remote signals or barrier semaphores. Data moves between devices by JAX's collectives and lax.ppermute only.
A program may use at most 128 MiB of HBM per device.

v0:
```python
import math
from functools import partial

import jax
import jax.numpy as jnp
from jax import lax
from jax.experimental import pallas as pl
from jax.experimental.pallas import tpu as pltpu
from jax.sharding import PartitionSpec as P

D = 4096
BLK = 128
REACH = 4
EPSILON = 1e-06
NEG = -1e30
FAR_OFF = 1 << 30
LOG2E = math.log2(math.e)
PER_CHUNK = 2

NT = (((1,), (1,)), ((), ()))
TN = (((0,), (0,)), ((), ()))


def dot(a, b, dims):
    return lax.dot_general(a, b, dims, preferred_element_type=jnp.float32)


def params(mib=48):
    return pltpu.CompilerParams(vmem_limit_bytes=mib * 1024 * 1024)


def shifted(x, by):
    n = lax.axis_size("ctx")
    return lax.ppermute(x, "ctx", [(i, i + by) for i in range(n) if 0 <= i + by < n])


def even_to_odd(x):
    n = lax.axis_size("ctx")
    return lax.ppermute(x, "ctx", [(i, i + 1) for i in range(0, n - 1, 2)])


def odd_to_even(x):
    n = lax.axis_size("ctx")
    return lax.ppermute(x, "ctx", [(i, i - 1) for i in range(1, n, 2)])


def lane_column(block, lane):
    spots = lax.broadcasted_iota(jnp.int32, block.shape, 1)
    return jnp.sum(jnp.where(spots == lane, block, 0.0), axis=1, keepdims=True)


def masked_scores(keys, q, thr_ref, first):
    scores = dot(keys, q, NT)
    row = lax.broadcasted_iota(jnp.int32, (BLK, q.shape[0]), 0)
    parts = []
    for j in range(keys.shape[0] // BLK):
        ok = row >= thr_ref[first + j : first + j + 1, :]
        parts.append(jnp.where(ok, scores[j * BLK : (j + 1) * BLK], NEG))
    return parts


def softmax_of(parts, scale2):
    top = parts[0]
    for p in parts[1:]:
        top = jnp.maximum(top, p)
    top = jnp.max(top, axis=0, keepdims=True) * scale2
    weights = [jnp.exp2(p * scale2 - top) for p in parts]
    total = weights[0]
    for w in weights[1:]:
        total = total + w
    total = jnp.sum(total, axis=0, keepdims=True)
    return top, total, [w.astype(jnp.bfloat16) for w in weights]


def diag_kernel(scale2, divisor, q_ref, k_ref, v_ref, thr_ref, start_ref, cum_ref, cumc_ref, o_ref, top_ref, tot_ref, lin_ref):
    h = pl.program_id(0)
    q, k, v = q_ref[...], k_ref[...], v_ref[...]
    length = q.shape[0]
    scores = dot(k, q, NT)
    row = lax.broadcasted_iota(jnp.int32, (BLK, length), 0)
    col = lax.broadcasted_iota(jnp.int32, (BLK, length), 1)
    cum_row = cum_ref[pl.ds(h, 1), :]
    cum_col = lane_column(cumc_ref[...], h)
    soft, mix = [], []
    for j in range(length // BLK):
        s = scores[j * BLK : (j + 1) * BLK]
        causal = row <= col - j * BLK
        soft.append(jnp.where(causal & (row >= thr_ref[j : j + 1, :]), s, NEG))
        gap = cum_row - cum_col[j * BLK : (j + 1) * BLK]
        ok = causal & (row >= start_ref[0:1, :] - j * BLK)
        decay = jnp.exp(jnp.where(ok, gap, NEG))
        mix.append((s * decay * (1.0 / divisor)).astype(jnp.bfloat16))
    top, total, weights = softmax_of(soft, scale2)
    o_ref[...] = dot(v, jnp.concatenate(weights, axis=0), TN)
    lin_ref[...] = dot(v, jnp.concatenate(mix, axis=0), TN)
    top_ref[pl.ds(h, 1), :] = top
    tot_ref[pl.ds(h, 1), :] = total


def near_scores(q, k2, k1, thr_ref, scale2):
    n = k2.shape[0] // BLK
    parts = masked_scores(k2, q, thr_ref, 0) + masked_scores(k1, q, thr_ref, n)
    top, total, weights = softmax_of(parts, scale2)
    return top, total, jnp.concatenate(weights[:n], axis=0), jnp.concatenate(weights[n:], axis=0)


def far_kernel(scale2, chunk, q_ref, k2_ref, v2_ref, ka_ref, va_ref, kb_ref, vb_ref, thr_ref, w_ref, out_ref):
    h = pl.program_id(0) + chunk * PER_CHUNK
    k1 = ka_ref[...] + kb_ref[...]
    v1 = va_ref[...] + vb_ref[...]
    k2, v2 = k2_ref[...], v2_ref[...]
    length = k2.shape[0]
    top, total, p2, p1 = near_scores(q_ref[...], k2, k1, thr_ref, scale2)
    w = lane_column(w_ref[...], h)
    kw2 = (k2.astype(jnp.float32) * w[:length]).astype(jnp.bfloat16)
    kw1 = (k1.astype(jnp.float32) * w[length:]).astype(jnp.bfloat16)
    o = dot(v2, p2, TN) + dot(v1, p1, TN)
    state = dot(v2, kw2, TN) + dot(v1, kw1, TN)
    hd = o.shape[0]
    out_ref[0:hd, 0:length] = (o * (1.0 / total)).astype(jnp.bfloat16)
    out_ref[0:hd, length:] = state.astype(jnp.bfloat16)
    lse = top + jnp.log(total) * LOG2E
    hi = lse.astype(jnp.bfloat16)
    rest = lse - hi.astype(jnp.float32)
    mid = rest.astype(jnp.bfloat16)
    low = (rest - mid.astype(jnp.float32)).astype(jnp.bfloat16)
    spot = lax.broadcasted_iota(jnp.int32, (16, length), 0)
    zero = jnp.zeros((16, length), jnp.float32)
    stats = jnp.where(
        spot == 0,
        zero + hi.astype(jnp.float32),
        jnp.where(
            spot == 1,
            zero + mid.astype(jnp.float32),
            jnp.where(spot == 2, zero + low.astype(jnp.float32), jnp.where(spot == 3, zero + 1.0, zero)),
        ),
    )
    out_ref[hd:, 0:length] = stats.astype(jnp.bfloat16)
    out_ref[hd:, length:] = jnp.zeros((16, hd), jnp.bfloat16)


def near_kernel(
    scale2, chunk, q_ref, k2_ref, v2_ref, ka_ref, va_ref, kb_ref, vb_ref, thr_ref, pay_ref, coef_ref,
    od_ref, topd_ref, totd_ref, lind_ref, x_ref, on_ref, lse_ref,
):
    i = pl.program_id(0)
    h = i + chunk * PER_CHUNK
    q = q_ref[...]
    hd = q.shape[1]
    length = q.shape[0]
    k1 = ka_ref[...] + kb_ref[...]
    v1 = va_ref[...] + vb_ref[...]
    v2 = v2_ref[...]
    top, total, p2, p1 = near_scores(q, k2_ref[...], k1, thr_ref, scale2)
    o = dot(v2, p2, TN) + dot(v1, p1, TN)
    top_d = topd_ref[pl.ds(h, 1), :]
    new_top = jnp.maximum(top, top_d)
    a, b = jnp.exp2(top - new_top), jnp.exp2(top_d - new_top)
    total = total * a + totd_ref[pl.ds(h, 1), :] * b
    on = (o * a + od_ref[...] * b) * (1.0 / total)
    lin = lind_ref[...] + dot(pay_ref[0:hd, length:], q, NT) * coef_ref[pl.ds(h, 1), :]
    x_ref[...] = lin + on
    on_ref[...] = on
    lse_ref[pl.ds(i, 1), :] = new_top + jnp.log(total) * LOG2E


def merge_kernel(chunk, q_ref, pay_ref, coef_ref, x_ref, on_ref, lse_ref, mixed_ref, sq_ref):
    i = pl.program_id(0)
    h = i + chunk * PER_CHUNK
    q = q_ref[...]
    length, hd = q.shape
    stats = pay_ref[hd:, 0:length].astype(jnp.float32)
    lse_far = stats[0:1] + stats[1:2] + stats[2:3]
    far = pay_ref[0:hd, 0:length].astype(jnp.float32)
    share = 1.0 / (1.0 + jnp.exp2(jnp.minimum(lse_ref[pl.ds(i, 1), :] - lse_far, 120.0)))
    share = jnp.where((lse_far > 0.5 * NEG) & (stats[3:4] > 0.5), share, 0.0)
    lin = dot(pay_ref[0:hd, length:], q, NT) * coef_ref[pl.ds(h, 1), :]
    mixed = x_ref[...] + share * (far - on_ref[...]) + lin
    mixed_ref[...] = mixed

    @pl.when(i == 0)
    def _():
        sq_ref[...] = jnp.zeros_like(sq_ref)

    sq_ref[...] += jnp.sum(mixed * mixed, axis=0, keepdims=True)


def norm_kernel(chunks, *refs):
    mixed_refs, sq_ref, gain_ref, out_ref = refs[:chunks], refs[chunks], refs[chunks + 1], refs[chunks + 2]
    inverse = lax.rsqrt(jnp.sum(sq_ref[...], axis=0, keepdims=True) / D + EPSILON)
    col = 0
    for ref in mixed_refs:
        for i in range(ref.shape[0] // 128):
            part = (ref[i * 128 : (i + 1) * 128, :] * inverse).T
            out_ref[:, col : col + 128] = (part * gain_ref[:, col : col + 128]).astype(jnp.bfloat16)
            col += 128


def on_device(query, key, value, log_decay, doc_lengths, tile_mask, gain):
    length, features = query.shape
    heads = log_decay.shape[0]
    hd = features // heads
    tiles = length // BLK
    chunks = heads // PER_CHUNK
    width = PER_CHUNK * hd
    divisor = hd * math.sqrt(length)
    scale2 = LOG2E / math.sqrt(hd)
    place = lax.axis_index("ctx")
    f32, bf16 = jnp.float32, jnp.bfloat16

    kv = [
        jnp.concatenate([key[:, i * width : (i + 1) * width], value[:, i * width : (i + 1) * width]], axis=1)
        for i in range(chunks)
    ]
    two_back = [shifted(x, 2) for x in kv]
    from_even = [even_to_odd(x) for x in kv]
    q_far = shifted(query, -2)
    from_odd = [odd_to_even(x) for x in two_back]

    ends = jnp.cumsum(doc_lengths)
    begin = place * length

    def doc_start(pos):
        return jnp.max(jnp.where(ends[:, None] <= pos[None, :], ends[:, None], 0), axis=0)

    local = jnp.arange(length, dtype=jnp.int32)
    start = doc_start(begin + local) - begin
    entry = doc_start(jnp.reshape(begin - 1, (1,)))[0] - begin
    picked = jnp.repeat(tile_mask.T, BLK, axis=1) == 1
    own = jnp.arange(tiles)[:, None] == (local // BLK)[None, :]
    reach = (REACH + 1) * tiles
    bases = (jnp.arange(reach, dtype=jnp.int32) - REACH * tiles) * BLK
    keep = picked.at[REACH * tiles :].set(picked[REACH * tiles :] | own)
    thr = jnp.where(keep, start[None, :] - bases[:, None], FAR_OFF)
    thr_far = shifted(thr[: 2 * tiles], -2)
    thr_near = thr[2 * tiles : 4 * tiles]
    thr_own = thr[4 * tiles :]

    cum = jnp.cumsum(log_decay, axis=1)
    alive = (start < 0).astype(f32)
    coef = jnp.exp(cum) * alive[None, :] * (1.0 / divisor)
    gathered = lax.all_gather(log_decay, "ctx")
    before = lax.dynamic_slice_in_dim(
        jnp.concatenate([jnp.zeros((2,) + log_decay.shape, f32), gathered]), place, 2, 0
    )
    before = before.transpose(1, 0, 2).reshape(heads, 2 * length)
    back = jnp.cumsum(before[:, ::-1], axis=1)[:, ::-1]
    since = jnp.arange(-2 * length, 0, dtype=jnp.int32) >= entry
    weight = (jnp.exp(back - before) * since[None, :].astype(f32)).T
    through = jnp.exp(back[:, 0]) * (entry < -2 * length).astype(f32)
    coef_far = coef * through[:, None]

    whole = lambda *shape: pl.BlockSpec(shape, lambda h: (0,) * len(shape))
    head_cols = pl.BlockSpec((length, hd), lambda h: (0, h))
    head_rows = pl.BlockSpec((hd, length), lambda h: (h, 0))
    o_diag, top_diag, tot_diag, lin_diag = pl.pallas_call(
        partial(diag_kernel, scale2, divisor),
        grid=(heads,),
        in_specs=[head_cols] * 3
        + [whole(tiles, length), whole(1, length), whole(heads, length), whole(length, heads)],
        out_specs=[head_rows, whole(heads, length), whole(heads, length), head_rows],
        out_shape=[
            jax.ShapeDtypeStruct((features, length), f32),
            jax.ShapeDtypeStruct((heads, length), f32),
            jax.ShapeDtypeStruct((heads, length), f32),
            jax.ShapeDtypeStruct((features, length), f32),
        ],
        compiler_params=params(),
        cost_estimate=pl.CostEstimate(flops=6 * heads * length * length * hd, bytes_accessed=8 << 20, transcendentals=2 * heads * length * length),
        name="own_piece",
    )(query, key, value, thr_own, start[None, :], cum, cum.T)

    first = pl.BlockSpec((length, hd), lambda h: (0, h))
    second = pl.BlockSpec((length, hd), lambda h: (0, h + PER_CHUNK))
    pay_rows, pay_cols = hd + 16, length + hd
    pay_spec = pl.BlockSpec((pay_rows, pay_cols), lambda h: (h, 0))
    pair_cost = pl.CostEstimate(flops=8 * PER_CHUNK * length * length * hd, bytes_accessed=3 << 20, transcendentals=2 * PER_CHUNK * length * length)
    sent, merged_in = [], []
    for i in range(chunks):
        q_spec = pl.BlockSpec((length, hd), lambda h, i=i: (0, h + i * PER_CHUNK))
        row_spec = pl.BlockSpec((hd, length), lambda h, i=i: (h + i * PER_CHUNK, 0))
        kv_specs = [first, second] * 3
        kv_args = (two_back[i], two_back[i], from_even[i], from_even[i], from_odd[i], from_odd[i])
        pay = pl.pallas_call(
            partial(far_kernel, scale2, i),
            grid=(PER_CHUNK,),
            in_specs=[q_spec] + kv_specs + [whole(2 * tiles, length), whole(2 * length, heads)],
            out_specs=pay_spec,
            out_shape=jax.ShapeDtypeStruct((PER_CHUNK * pay_rows, pay_cols), bf16),
            compiler_params=params(),
            cost_estimate=pair_cost,
            name="far_pieces",
        )(q_far, *kv_args, thr_far, weight)
        sent.append(shifted(pay, 2))
        x, on, lse = pl.pallas_call(
            partial(near_kernel, scale2, i),
            grid=(PER_CHUNK,),
            in_specs=[q_spec]
            + kv_specs
            + [whole(2 * tiles, length), pay_spec, whole(heads, length), row_spec, whole(heads, length), whole(heads, length), row_spec],
            out_specs=[head_rows, head_rows, whole(PER_CHUNK, length)],
            out_shape=[
                jax.ShapeDtypeStruct((width, length), f32),
                jax.ShapeDtypeStruct((width, length), f32),
                jax.ShapeDtypeStruct((PER_CHUNK, length), f32),
            ],
            compiler_params=params(),
            cost_estimate=pair_cost,
            name="near_pieces",
        )(query, *kv_args, thr_near, pay, coef, o_diag, top_diag, tot_diag, lin_diag)
        merged_in.append((x, on, lse))
    mixed, squares = [], []
    for i in range(chunks):
        q_spec = pl.BlockSpec((length, hd), lambda h, i=i: (0, h + i * PER_CHUNK))
        m, s = pl.pallas_call(
            partial(merge_kernel, i),
            grid=(PER_CHUNK,),
            in_specs=[q_spec, pay_spec, whole(heads, length), head_rows, head_rows, whole(PER_CHUNK, length)],
            out_specs=[head_rows, whole(1, length)],
            out_shape=[jax.ShapeDtypeStruct((width, length), f32), jax.ShapeDtypeStruct((1, length), f32)],
            compiler_params=params(),
            cost_estimate=pl.CostEstimate(flops=1 << 26, bytes_accessed=2 << 20, transcendentals=1024),
            name="merge",
        )(query, sent[i], coef_far, *merged_in[i])
        mixed.append(m)
        squares.append(s)
    total = squares[0]
    for s in squares[1:]:
        total = total + s
    ranks = lax.axis_size("head")
    everyone = lax.all_gather(total.reshape(length // 128, 128), "head").reshape(ranks, length)
    return pl.pallas_call(
        partial(norm_kernel, chunks),
        out_shape=jax.ShapeDtypeStruct((length, features), bf16),
        compiler_params=params(),
        name="normalize",
    )(*mixed, everyone, gain[None, :])


def solution(mesh):
    placed = (
        P("ctx", "head"),
        P("ctx", "head"),
        P("ctx", "head"),
        P("head", "ctx"),
        P(),
        P("ctx", None),
        P("head"),
    )
    return jax.shard_map(on_device, mesh=mesh, in_specs=placed, out_specs=P("ctx", "head"), check_vma=False)
```

profile of v0, /device:TPU:3, one launch (start us, length us, event | category | flops | bytes accessed | tf_op | source)
XLA Modules:
  0.0 182.5 jit_solution(7169051885394105405)
XLA Ops:
  0.0 2.7 %fusion.12 = (bf16[512,256]{1,0:T(8,128)(2,1)S(1)}, bf16[512,256]{1,0:T(8,128)(2,1)}, bf16[512,256]{1,0:T(8,128)(2,1)S(1)}, bf16[512,256]{1,0:T(8,128)(2,1)}, bf...) fusion(bf16[512,1024]{1,0:T(8,128)(2,1)} %k_ref.1, ...), kind=kLoop, calls=%fused_computation.42 | loop fusion | bytes 4194304 | tf_op jit(solution)/shard_map/slice | solution.py:212
  2.7 0.8 pad_maximum_fusion
  3.5 3.2 %collective-permute-start.1 = (bf16[512,512]{1,0:T(8,128)(2,1)}, bf16[512,512]{1,0:T(8,128)(2,1)S(1)}, u32[]{:S(2)}, u32[]{:S(2)}) collective-permute-start(bf16[512,512]{1,0:T(8,128)(2,1)} %pad_maximum_fusion), channel_id=1, source_target_pairs={{0,8},{4,12},{8,16},{12,20},{16,24},{20,28},{1,9},{5,13},{9,17},{1... | collective-permute-start | bytes 1572872 | tf_op jit(solution)/shard_map/ppermute | solution.py:34
  6.8 1.3 collective-permute-start.2
  8.1 1.3 collective-permute-start
  9.4 0.1 copy.26
  9.6 0.1 broadcast_in_dim.44
  9.7 0.1 copy.27
  9.8 0.1 broadcast_bitcast_fusion
  9.9 0.2 broadcast_in_dim.46
  10.1 0.1 select_reduce_fusion
  10.2 0.1 subtract_select_fusion
  10.3 0.6 fusion.14
  10.9 1.3 collective-permute-start.4
  12.2 1.9 %pad_maximum_fusion.1 = bf16[512,512]{1,0:T(8,128)(2,1)} fusion(bf16[512,256]{1,0:T(8,128)(2,1)} %get-tuple-element.81, bf16[512,256]{1,0:T(8,128)(2,1)} %get-tuple-element.70), kind=kLoop, calls=%fused_computation.2 | loop fusion | flops 1048576 | bytes 1048576 | tf_op jit(solution)/shard_map/concatenate | solution.py:212
  14.1 5.4 %collective-permute-start.6 = (bf16[512,512]{1,0:T(8,128)(2,1)}, bf16[512,512]{1,0:T(8,128)(2,1)}, u32[]{:S(2)}, u32[]{:S(2)}) collective-permute-start(bf16[512,512]{1,0:T(8,128)(2,1)} %pad_maximum_fusion.1), channel_id=1, source_target_pairs={{0,8},{4,12},{8,16},{12,20},{16,24},{20,28},{1,9},{5,13},{9,17},{1... | collective-permute-start | bytes 1572872 | tf_op jit(solution)/shard_map/ppermute | solution.py:34
  19.5 34.1 %all-gather = f32[64,512]{1,0:T(8,128)} all-gather(f32[8,512]{1,0:T(8,128)S(1)} %copy-done.5), channel_id=2, replica_groups=mesh['ctx'=8,'head'=4] {'ctx'}, dimensions={0}, use_global_device_ids=true | all-gather | bytes 147456 | tf_op jit(solution)/shard_map/all_gather | solution.py:242
  53.6 2.8 %copy.28 = f32[8,8,512]{1,2,0:T(8,128)} copy(f32[8,8,512]{2,1,0:T(8,128)} %bitcast.44) | data formatting | bytes 262144 | tf_op jit(solution)/shard_map/all_gather | solution.py:242
  56.4 1.8 pad_dynamic-slice_fusion
  58.2 4.7 %rev.6 = f32[8,1024]{0,1:T(8,128)} reverse(f32[8,1024]{0,1:T(8,128)} %bitcast.40), dimensions={1} | reverse | bytes 65536 | tf_op jit(solution)/shard_map/rev | solution.py:247
  62.9 1.2 copy.29
  64.2 2.3 %reduce-window.15 = f32[8,8,128]{2,1,0:T(8,128)S(1)} reduce-window(f32[8,8,128]{2,1,0:T(8,128)S(1)} %copy.29, f32[]{:T(128)} %constant.82.clone.1), window={size=1x1x128 pad=0_0x0_0x127_0}, to_apply=%region_2.3 | reduce-window | flops 1040384 | bytes 65540 | tf_op jit(solution)/shard_map/reduce-window.1
  66.4 0.2 slice_reduce_fusion
  66.6 0.2 reduce-window.16
  66.8 1.1 reduce-window.19
  67.9 0.2 slice_reduce_fusion.1
  68.1 0.1 fusion
  68.2 1.9 %pad_maximum_fusion.2 = bf16[512,512]{1,0:T(8,128)(2,1)} fusion(bf16[512,256]{1,0:T(8,128)(2,1)} %get-tuple-element.79, bf16[512,256]{1,0:T(8,128)(2,1)} %get-tuple-element.72), kind=kLoop, calls=%fused_computation.3 | loop fusion | flops 1048576 | bytes 1048576 | tf_op jit(solution)/shard_map/concatenate | solution.py:212
  70.1 1.8 pad_maximum_fusion.3
  71.9 1.0 copy.30
  72.9 1.3 collective-permute-start.7
  74.2 2.1 %collective-permute-start.10 = (bf16[512,512]{1,0:T(8,128)(2,1)}, bf16[512,512]{1,0:T(8,128)(2,1)}, u32[]{:S(2)}, u32[]{:S(2)}) collective-permute-start(bf16[512,512]{1,0:T(8,128)(2,1)} %pad_maximum_fusion.2), channel_id=1, source_target_pairs={{0,8},{4,12},{8,16},{12,20},{16,24},{20,28},{1,9},{5,13},{9,17},{1... | collective-permute-start | bytes 1572872 | tf_op jit(solution)/shard_map/ppermute | solution.py:34
  76.3 3.2 %collective-permute-start.14 = (bf16[512,512]{1,0:T(8,128)(2,1)}, bf16[512,512]{1,0:T(8,128)(2,1)}, u32[]{:S(2)}, u32[]{:S(2)}) collective-permute-start(bf16[512,512]{1,0:T(8,128)(2,1)} %pad_maximum_fusion.3), channel_id=1, source_target_pairs={{0,8},{4,12},{8,16},{12,20},{16,24},{20,28},{1,9},{5,13},{9,17},{1... | collective-permute-start | bytes 1572872 | tf_op jit(solution)/shard_map/ppermute | solution.py:34
  79.5 0.6 fusion.8
  80.8 5.7 %collective-permute-start.3 = (bf16[512,512]{1,0:T(8,128)(2,1)S(1)}, bf16[512,512]{1,0:T(8,128)(2,1)}, u32[]{:S(2)}, u32[]{:S(2)}) collective-permute-start(bf16[512,512]{1,0:T(8,128)(2,1)S(1)} %collective-permute-done.1.k2_ref.v2_ref), channel_id=1, source_target_pairs={{4,0},{12,8},{20,16},{28,24},{5,1},{13,9},{21,17},{29,25},{6,2},{1... | collective-permute-start | bytes 1572872 | tf_op jit(solution)/shard_map/ppermute | solution.py:44
  86.5 0.7 fusion.11
  87.2 1.3 collective-permute-start.11
  88.5 5.6 %collective-permute-start.8 = (bf16[512,512]{1,0:T(8,128)(2,1)}, bf16[512,512]{1,0:T(8,128)(2,1)}, u32[]{:S(2)}, u32[]{:S(2)}) collective-permute-start(bf16[512,512]{1,0:T(8,128)(2,1)} %collective-permute-done.6.k2_ref.v2_ref), channel_id=1, source_target_pairs={{4,0},{12,8},{20,16},{28,24},{5,1},{13,9},{21,17},{29,25},{6,2},{1... | collective-permute-start | bytes 1572872 | tf_op jit(solution)/shard_map/ppermute | solution.py:44
  94.1 3.8 %collective-permute-start.12 = (bf16[512,512]{1,0:T(8,128)(2,1)}, bf16[512,512]{1,0:T(8,128)(2,1)}, u32[]{:S(2)}, u32[]{:S(2)}) collective-permute-start(bf16[512,512]{1,0:T(8,128)(2,1)} %collective-permute-done.10.k2_ref.v2_ref), channel_id=1, source_target_pairs={{4,0},{12,8},{20,16},{28,24},{5,1},{13,9},{21,17},{29,25},{6,2},{1... | collective-permute-start | bytes 1572872 | tf_op jit(solution)/shard_map/ppermute | solution.py:44
  98.0 4.7 %rev.7 = f32[8,1024]{0,1:T(8,128)} reverse(f32[8,1024]{0,1:T(8,128)} %bitcast.42), dimensions={1} | reverse | bytes 65536 | tf_op jit(solution)/shard_map/rev | solution.py:247
  102.7 0.7 slice.96.thr_ref
  103.5 0.1 copy.31.cumc_ref
  103.6 1.3 collective-permute-start.15
  104.9 4.0 %collective-permute-start.16 = (bf16[512,512]{1,0:T(8,128)(2,1)}, bf16[512,512]{1,0:T(8,128)(2,1)S(1)}, u32[]{:S(2)}, u32[]{:S(2)}) collective-permute-start(bf16[512,512]{1,0:T(8,128)(2,1)} %collective-permute-done.14.k2_ref.v2_ref), channel_id=1, source_target_pairs={{4,0},{12,8},{20,16},{28,24},{5,1},{13,9},{21,17},{29,25},{6,2},{1... | collective-permute-start | bytes 1572872 | tf_op jit(solution)/shard_map/ppermute | solution.py:44
  109.0 1.4 multiply_bitcast_fusion.w_ref
  110.4 3.8 %far_pieces.4.pay_ref = bf16[288,640]{1,0:T(8,128)(2,1)S(1)} custom-call(bf16[512,1024]{1,0:T(8,128)(2,1)S(1)} %collective-permute-done.q_ref, bf16[512,512]{1,0:T(8,128)(2,1)S(1)} %collective-permute-done.1.k2_ref.v2_ref, bf16[512,512]{1,0:T(8,128)(2,1)S(1)} %collective-permute-done.1.k2_ref.v2_ref, ...), custom_call_target="tpu_custom_call" | custom-call | flops 536870912 | bytes 3145728 | tf_op jit(solution)/shard_map/far_pieces/pallas_call | solution.py:284
  114.2 4.1 %collective-permute-start.5 = (bf16[288,640]{1,0:T(8,128)(2,1)S(1)}, bf16[288,640]{1,0:T(8,128)(2,1)S(1)}, u32[]{:S(2)}, u32[]{:S(2)}) collective-permute-start(bf16[288,640]{1,0:T(8,128)(2,1)S(1)} %far_pieces.4.pay_ref), channel_id=1, source_target_pairs={{0,8},{4,12},{8,16},{12,20},{16,24},{20,28},{1,9},{5,13},{9,17},{1... | collective-permute-start | bytes 1105928 | tf_op jit(solution)/shard_map/ppermute | solution.py:34
  118.4 4.0 %far_pieces.5.pay_ref = bf16[288,640]{1,0:T(8,128)(2,1)S(1)} custom-call(bf16[512,1024]{1,0:T(8,128)(2,1)S(1)} %collective-permute-done.q_ref, bf16[512,512]{1,0:T(8,128)(2,1)} %collective-permute-done.6.k2_ref.v2_ref, bf16[512,512]{1,0:T(8,128)(2,1)} %collective-permute-done.6.k2_ref.v2_ref, bf16[512,512]{1,0:T(8,128)(2,1)} %collective-permute-done.7.ka_ref.va_ref, ...), custom_call_target="tpu_custom_call" | custom-call | flops 536870912 | bytes 3145728 | tf_op jit(solution)/shard_map/far_pieces/pallas_call | solution.py:284
  122.4 2.1 %collective-permute-start.9 = (bf16[288,640]{1,0:T(8,128)(2,1)S(1)}, bf16[288,640]{1,0:T(8,128)(2,1)S(1)}, u32[]{:S(2)}, u32[]{:S(2)}) collective-permute-start(bf16[288,640]{1,0:T(8,128)(2,1)S(1)} %far_pieces.5.pay_ref), channel_id=1, source_target_pairs={{0,8},{4,12},{8,16},{12,20},{16,24},{20,28},{1,9},{5,13},{9,17},{1... | collective-permute-start | bytes 1105928 | tf_op jit(solution)/shard_map/ppermute | solution.py:34
  124.5 4.0 %far_pieces.6.pay_ref = bf16[288,640]{1,0:T(8,128)(2,1)S(1)} custom-call(bf16[512,1024]{1,0:T(8,128)(2,1)S(1)} %collective-permute-done.q_ref, bf16[512,512]{1,0:T(8,128)(2,1)} %collective-permute-done.10.k2_ref.v2_ref, bf16[512,512]{1,0:T(8,128)(2,1)} %collective-permute-done.10.k2_ref.v2_ref, bf16[512,512]{1,0:T(8,128)(2,1)} %collective-permute-done.11.ka_ref.va_ref, ...), custom_call_target="tpu_custom_call" | custom-call | flops 536870912 | bytes 3145728 | tf_op jit(solution)/shard_map/far_pieces/pallas_call | solution.py:284
  128.5 4.2 %collective-permute-start.13 = (bf16[288,640]{1,0:T(8,128)(2,1)S(1)}, bf16[288,640]{1,0:T(8,128)(2,1)S(1)}, u32[]{:S(2)}, u32[]{:S(2)}) collective-permute-start(bf16[288,640]{1,0:T(8,128)(2,1)S(1)} %far_pieces.6.pay_ref), channel_id=1, source_target_pairs={{0,8},{4,12},{8,16},{12,20},{16,24},{20,28},{1,9},{5,13},{9,17},{1... | collective-permute-start | bytes 1105928 | tf_op jit(solution)/shard_map/ppermute | solution.py:34
  132.8 3.7 %far_pieces.7.pay_ref = bf16[288,640]{1,0:T(8,128)(2,1)S(1)} custom-call(bf16[512,1024]{1,0:T(8,128)(2,1)S(1)} %collective-permute-done.q_ref, bf16[512,512]{1,0:T(8,128)(2,1)} %collective-permute-done.14.k2_ref.v2_ref, bf16[512,512]{1,0:T(8,128)(2,1)} %collective-permute-done.14.k2_ref.v2_ref, bf16[512,512]{1,0:T(8,128)(2,1)S(1)} %collective-permute-done.15.ka_ref.va_ref, ...), custom_call_target="tpu_custom_call" | custom-call | flops 536870912 | bytes 3145728 | tf_op jit(solution)/shard_map/far_pieces/pallas_call | solution.py:284
  136.5 2.1 %collective-permute-start.17 = (bf16[288,640]{1,0:T(8,128)(2,1)S(1)}, bf16[288,640]{1,0:T(8,128)(2,1)S(1)}, u32[]{:S(2)}, u32[]{:S(2)}) collective-permute-start(bf16[288,640]{1,0:T(8,128)(2,1)S(1)} %far_pieces.7.pay_ref), channel_id=1, source_target_pairs={{0,8},{4,12},{8,16},{12,20},{16,24},{20,28},{1,9},{5,13},{9,17},{1... | collective-permute-start | bytes 1105928 | tf_op jit(solution)/shard_map/ppermute | solution.py:34
  138.6 8.7 %own_piece.1 = (f32[1024,512]{1,0:T(8,128)S(1)}, f32[8,512]{1,0:T(8,128)S(1)}, f32[8,512]{1,0:T(8,128)S(1)}, f32[1024,512]{1,0:T(8,128)}) custom-call(bf16[512,1024]{1,0:T(8,128)(2,1)S(1)} %copy-done, bf16[512,1024]{1,0:T(8,128)(2,1)S(1)} %copy-done.1, bf16[512,1024]{1,0:T(8,128)(2,1)S(1)} %copy-done.2, s32[4,512]{1,0:T(4,128)S(1)} %slice.96.thr_ref, ...), custom_call_target="tpu_custom_call" | custom-call | flops 1610612736 | bytes 8388608 | tf_op jit(solution)/shard_map/own_piece/pallas_call | solution.py:256
  147.3 3.9 %near_pieces.4 = (f32[256,512]{1,0:T(8,128)S(1)}, f32[256,512]{1,0:T(8,128)S(1)}, f32[2,512]{1,0:T(2,128)S(1)}) custom-call(bf16[512,1024]{1,0:T(8,128)(2,1)S(1)} %copy-done, bf16[512,512]{1,0:T(8,128)(2,1)S(1)} %collective-permute-done.1.k2_ref.v2_ref, bf16[512,512]{1,0:T(8,128)(2,1)S(1)} %collective-permute-done.1.k2_ref.v2_ref, ...), custom_call_target="tpu_custom_call" | custom-call | flops 536870912 | bytes 3145728 | tf_op jit(solution)/shard_map/near_pieces/pallas_call | solution.py:295
  151.2 4.0 %near_pieces.5 = (f32[256,512]{1,0:T(8,128)S(1)}, f32[256,512]{1,0:T(8,128)S(1)}, f32[2,512]{1,0:T(2,128)S(1)}) custom-call(bf16[512,1024]{1,0:T(8,128)(2,1)S(1)} %copy-done, bf16[512,512]{1,0:T(8,128)(2,1)} %collective-permute-done.6.k2_ref.v2_ref, bf16[512,512]{1,0:T(8,128)(2,1)} %collective-permute-done.6.k2_ref.v2_ref, ...), custom_call_target="tpu_custom_call" | custom-call | flops 536870912 | bytes 3145728 | tf_op jit(solution)/shard_map/near_pieces/pallas_call | solution.py:295
  155.2 4.0 %near_pieces.6 = (f32[256,512]{1,0:T(8,128)S(1)}, f32[256,512]{1,0:T(8,128)S(1)}, f32[2,512]{1,0:T(2,128)S(1)}) custom-call(bf16[512,1024]{1,0:T(8,128)(2,1)S(1)} %copy-done, bf16[512,512]{1,0:T(8,128)(2,1)} %collective-permute-done.10.k2_ref.v2_ref, bf16[512,512]{1,0:T(8,128)(2,1)} %collective-permute-done.10.k2_ref.v2_ref, ...), custom_call_target="tpu_custom_call" | custom-call | flops 536870912 | bytes 3145728 | tf_op jit(solution)/shard_map/near_pieces/pallas_call | solution.py:295
  159.3 3.8 %near_pieces.7 = (f32[256,512]{1,0:T(8,128)S(1)}, f32[256,512]{1,0:T(8,128)S(1)}, f32[2,512]{1,0:T(2,128)S(1)}) custom-call(bf16[512,1024]{1,0:T(8,128)(2,1)S(1)} %copy-done, bf16[512,512]{1,0:T(8,128)(2,1)} %collective-permute-done.14.k2_ref.v2_ref, bf16[512,512]{1,0:T(8,128)(2,1)} %collective-permute-done.14.k2_ref.v2_ref, ...), custom_call_target="tpu_custom_call" | custom-call | flops 536870912 | bytes 3145728 | tf_op jit(solution)/shard_map/near_pieces/pallas_call | solution.py:295
  163.2 0.6 merge.4
  163.7 0.6 merge.5
  164.3 0.6 merge.6
  164.9 0.6 merge.7
  165.5 15.4 %all_gather.11 = f32[4,4,128]{2,1,0:T(4,128)S(1)} all-gather(f32[1,4,128]{2,1,0:T(4,128)S(1)} %bitcast.50), channel_id=1, replica_groups=mesh['ctx'=8,'head'=4] {'head'}, dimensions={0}, use_global_device_ids=true | all-gather | bytes 10240 | tf_op jit(solution)/shard_map/all_gather | solution.py:331
  180.9 1.6 normalize.1
  (51 shorter events, 0.5 us)
Async XLA Ops:
  0.0 8.1 %copy-start = (bf16[512,1024]{1,0:T(8,128)(2,1)S(1)}, bf16[512,1024]{1,0:T(8,128)(2,1)}, u32[]{:S(2)}) copy-start(bf16[512,1024]{1,0:T(8,128)(2,1)} %q_ref.17) | copy-start | bytes 3145732
  0.0 9.4 %copy-start.6 = (s32[4,20]{1,0:T(4,128)S(1)}, s32[4,20]{1,0:T(4,128)}, u32[]{:S(2)}) copy-start(s32[4,20]{1,0:T(4,128)} %param.14) | copy-start | bytes 964
  0.0 9.9 %copy-start.7 = (s32[8]{0:T(128)S(1)}, s32[8]{0:T(128)}, u32[]{:S(2)}) copy-start(s32[8]{0:T(128)} %param.13) | copy-start | bytes 100
  2.7 16.8 %copy-start.5 = (f32[8,512]{1,0:T(8,128)S(1)}, f32[8,512]{1,0:T(8,128)}, u32[]{:S(2)}) copy-start(f32[8,512]{1,0:T(8,128)} %param.12) | copy-start | bytes 49156
  3.5 70.7 %collective-permute-start.1 = (bf16[512,512]{1,0:T(8,128)(2,1)}, bf16[512,512]{1,0:T(8,128)(2,1)S(1)}, u32[]{:S(2)}, u32[]{:S(2)}) collective-permute-start(bf16[512,512]{1,0:T(8,128)(2,1)} %pad_maximum_fusion), channel_id=1, source_target_pairs={{0,8},{4,12},{8,16},{12,20},{16,24},{20,28},{1,9},{5,13},{9,17},{1... | collective-permute-start | bytes 1572872 | tf_op jit(solution)/shard_map/ppermute | solution.py:34
  6.8 69.6 %collective-permute-start.2 = (bf16[512,512]{1,0:T(8,128)(2,1)}, bf16[512,512]{1,0:T(8,128)(2,1)S(1)}, u32[]{:S(2)}, u32[]{:S(2)}) collective-permute-start(bf16[512,512]{1,0:T(8,128)(2,1)} %pad_maximum_fusion), channel_id=1, source_target_pairs={{0,4},{8,12},{16,20},{24,28},{1,5},{9,13},{17,21},{25,29},{2,6},{1... | collective-permute-start | bytes 1572872 | tf_op jit(solution)/shard_map/ppermute | solution.py:39
  8.1 95.5 %collective-permute-start = (bf16[512,1024]{1,0:T(8,128)(2,1)S(1)}, bf16[512,1024]{1,0:T(8,128)(2,1)S(1)}, u32[]{:S(2)}, u32[]{:S(2)}) collective-permute-start(bf16[512,1024]{1,0:T(8,128)(2,1)S(1)} %copy-done), channel_id=1, source_target_pairs={{8,0},{12,4},{16,8},{20,12},{24,16},{28,20},{9,1},{13,5},{17,9},{2... | collective-permute-start | bytes 3145736 | tf_op jit(solution)/shard_map/ppermute | solution.py:34
  10.3 0.6 copy-start.4
  10.9 62.0 %collective-permute-start.4 = (s32[8,512]{1,0:T(8,128)}, s32[8,512]{1,0:T(8,128)S(1)}, u32[]{:S(2)}, u32[]{:S(2)}) collective-permute-start(s32[8,512]{1,0:T(8,128)} %get-tuple-element.78), channel_id=1, source_target_pairs={{8,0},{12,4},{16,8},{20,12},{24,16},{28,20},{9,1},{13,5},{17,9},{2... | collective-permute-start | bytes 49160 | tf_op jit(solution)/shard_map/ppermute | solution.py:34
  14.1 66.7 %collective-permute-start.6 = (bf16[512,512]{1,0:T(8,128)(2,1)}, bf16[512,512]{1,0:T(8,128)(2,1)}, u32[]{:S(2)}, u32[]{:S(2)}) collective-permute-start(bf16[512,512]{1,0:T(8,128)(2,1)} %pad_maximum_fusion.1), channel_id=1, source_target_pairs={{0,8},{4,12},{8,16},{12,20},{16,24},{20,28},{1,9},{5,13},{9,17},{1... | collective-permute-start | bytes 1572872 | tf_op jit(solution)/shard_map/ppermute | solution.py:34
  72.9 14.3 %collective-permute-start.7 = (bf16[512,512]{1,0:T(8,128)(2,1)}, bf16[512,512]{1,0:T(8,128)(2,1)}, u32[]{:S(2)}, u32[]{:S(2)}) collective-permute-start(bf16[512,512]{1,0:T(8,128)(2,1)} %pad_maximum_fusion.1), channel_id=1, source_target_pairs={{0,4},{8,12},{16,20},{24,28},{1,5},{9,13},{17,21},{25,29},{2,6},{1... | collective-permute-start | bytes 1572872 | tf_op jit(solution)/shard_map/ppermute | solution.py:39
  74.2 14.3 %collective-permute-start.10 = (bf16[512,512]{1,0:T(8,128)(2,1)}, bf16[512,512]{1,0:T(8,128)(2,1)}, u32[]{:S(2)}, u32[]{:S(2)}) collective-permute-start(bf16[512,512]{1,0:T(8,128)(2,1)} %pad_maximum_fusion.2), channel_id=1, source_target_pairs={{0,8},{4,12},{8,16},{12,20},{16,24},{20,28},{1,9},{5,13},{9,17},{1... | collective-permute-start | bytes 1572872 | tf_op jit(solution)/shard_map/ppermute | solution.py:34
  76.3 17.8 %collective-permute-start.14 = (bf16[512,512]{1,0:T(8,128)(2,1)}, bf16[512,512]{1,0:T(8,128)(2,1)}, u32[]{:S(2)}, u32[]{:S(2)}) collective-permute-start(bf16[512,512]{1,0:T(8,128)(2,1)} %pad_maximum_fusion.3), channel_id=1, source_target_pairs={{0,8},{4,12},{8,16},{12,20},{16,24},{20,28},{1,9},{5,13},{9,17},{1... | collective-permute-start | bytes 1572872 | tf_op jit(solution)/shard_map/ppermute | solution.py:34
  80.8 24.1 %collective-permute-start.3 = (bf16[512,512]{1,0:T(8,128)(2,1)S(1)}, bf16[512,512]{1,0:T(8,128)(2,1)}, u32[]{:S(2)}, u32[]{:S(2)}) collective-permute-start(bf16[512,512]{1,0:T(8,128)(2,1)S(1)} %collective-permute-done.1.k2_ref.v2_ref), channel_id=1, source_target_pairs={{4,0},{12,8},{20,16},{28,24},{5,1},{13,9},{21,17},{29,25},{6,2},{1... | collective-permute-start | bytes 1572872 | tf_op jit(solution)/shard_map/ppermute | solution.py:44
  87.2 35.1 %collective-permute-start.11 = (bf16[512,512]{1,0:T(8,128)(2,1)}, bf16[512,512]{1,0:T(8,128)(2,1)}, u32[]{:S(2)}, u32[]{:S(2)}) collective-permute-start(bf16[512,512]{1,0:T(8,128)(2,1)} %pad_maximum_fusion.2), channel_id=1, source_target_pairs={{0,4},{8,12},{16,20},{24,28},{1,5},{9,13},{17,21},{25,29},{2,6},{1... | collective-permute-start | bytes 1572872 | tf_op jit(solution)/shard_map/ppermute | solution.py:39
  88.5 25.7 %collective-permute-start.8 = (bf16[512,512]{1,0:T(8,128)(2,1)}, bf16[512,512]{1,0:T(8,128)(2,1)}, u32[]{:S(2)}, u32[]{:S(2)}) collective-permute-start(bf16[512,512]{1,0:T(8,128)(2,1)} %collective-permute-done.6.k2_ref.v2_ref), channel_id=1, source_target_pairs={{4,0},{12,8},{20,16},{28,24},{5,1},{13,9},{21,17},{29,25},{6,2},{1... | collective-permute-start | bytes 1572872 | tf_op jit(solution)/shard_map/ppermute | solution.py:44
  94.1 30.3 %collective-permute-start.12 = (bf16[512,512]{1,0:T(8,128)(2,1)}, bf16[512,512]{1,0:T(8,128)(2,1)}, u32[]{:S(2)}, u32[]{:S(2)}) collective-permute-start(bf16[512,512]{1,0:T(8,128)(2,1)} %collective-permute-done.10.k2_ref.v2_ref), channel_id=1, source_target_pairs={{4,0},{12,8},{20,16},{28,24},{5,1},{13,9},{21,17},{29,25},{6,2},{1... | collective-permute-start | bytes 1572872 | tf_op jit(solution)/shard_map/ppermute | solution.py:44
  103.6 29.2 %collective-permute-start.15 = (bf16[512,512]{1,0:T(8,128)(2,1)}, bf16[512,512]{1,0:T(8,128)(2,1)S(1)}, u32[]{:S(2)}, u32[]{:S(2)}) collective-permute-start(bf16[512,512]{1,0:T(8,128)(2,1)} %pad_maximum_fusion.3), channel_id=1, source_target_pairs={{0,4},{8,12},{16,20},{24,28},{1,5},{9,13},{17,21},{25,29},{2,6},{1... | collective-permute-start | bytes 1572872 | tf_op jit(solution)/shard_map/ppermute | solution.py:39
  104.9 27.9 %collective-permute-start.16 = (bf16[512,512]{1,0:T(8,128)(2,1)}, bf16[512,512]{1,0:T(8,128)(2,1)S(1)}, u32[]{:S(2)}, u32[]{:S(2)}) collective-permute-start(bf16[512,512]{1,0:T(8,128)(2,1)} %collective-permute-done.14.k2_ref.v2_ref), channel_id=1, source_target_pairs={{4,0},{12,8},{20,16},{28,24},{5,1},{13,9},{21,17},{29,25},{6,2},{1... | collective-permute-start | bytes 1572872 | tf_op jit(solution)/shard_map/ppermute | solution.py:44
  114.2 48.9 %collective-permute-start.5 = (bf16[288,640]{1,0:T(8,128)(2,1)S(1)}, bf16[288,640]{1,0:T(8,128)(2,1)S(1)}, u32[]{:S(2)}, u32[]{:S(2)}) collective-permute-start(bf16[288,640]{1,0:T(8,128)(2,1)S(1)} %far_pieces.4.pay_ref), channel_id=1, source_target_pairs={{0,8},{4,12},{8,16},{12,20},{16,24},{20,28},{1,9},{5,13},{9,17},{1... | collective-permute-start | bytes 1105928 | tf_op jit(solution)/shard_map/ppermute | solution.py:34
  122.4 41.4 %collective-permute-start.9 = (bf16[288,640]{1,0:T(8,128)(2,1)S(1)}, bf16[288,640]{1,0:T(8,128)(2,1)S(1)}, u32[]{:S(2)}, u32[]{:S(2)}) collective-permute-start(bf16[288,640]{1,0:T(8,128)(2,1)S(1)} %far_pieces.5.pay_ref), channel_id=1, source_target_pairs={{0,8},{4,12},{8,16},{12,20},{16,24},{20,28},{1,9},{5,13},{9,17},{1... | collective-permute-start | bytes 1105928 | tf_op jit(solution)/shard_map/ppermute | solution.py:34
  128.5 10.1 %copy-start.1 = (bf16[512,1024]{1,0:T(8,128)(2,1)S(1)}, bf16[512,1024]{1,0:T(8,128)(2,1)}, u32[]{:S(2)}) copy-start(bf16[512,1024]{1,0:T(8,128)(2,1)} %k_ref.1) | copy-start | bytes 3145732
  128.5 10.1 %copy-start.2 = (bf16[512,1024]{1,0:T(8,128)(2,1)S(1)}, bf16[512,1024]{1,0:T(8,128)(2,1)}, u32[]{:S(2)}) copy-start(bf16[512,1024]{1,0:T(8,128)(2,1)} %v_ref.1) | copy-start | bytes 3145732
  128.5 35.8 %collective-permute-start.13 = (bf16[288,640]{1,0:T(8,128)(2,1)S(1)}, bf16[288,640]{1,0:T(8,128)(2,1)S(1)}, u32[]{:S(2)}, u32[]{:S(2)}) collective-permute-start(bf16[288,640]{1,0:T(8,128)(2,1)S(1)} %far_pieces.6.pay_ref), channel_id=1, source_target_pairs={{0,8},{4,12},{8,16},{12,20},{16,24},{20,28},{1,9},{5,13},{9,17},{1... | collective-permute-start | bytes 1105928 | tf_op jit(solution)/shard_map/ppermute | solution.py:34
  136.5 28.4 %collective-permute-start.17 = (bf16[288,640]{1,0:T(8,128)(2,1)S(1)}, bf16[288,640]{1,0:T(8,128)(2,1)S(1)}, u32[]{:S(2)}, u32[]{:S(2)}) collective-permute-start(bf16[288,640]{1,0:T(8,128)(2,1)S(1)} %far_pieces.7.pay_ref), channel_id=1, source_target_pairs={{0,8},{4,12},{8,16},{12,20},{16,24},{20,28},{1,9},{5,13},{9,17},{1... | collective-permute-start | bytes 1105928 | tf_op jit(solution)/shard_map/ppermute | solution.py:34
  164.3 16.6 %copy-start.3 = (f32[1024]{0:T(1024)S(1)}, f32[1024]{0:T(1024)}, u32[]{:S(2)}) copy-start(f32[1024]{0:T(1024)} %param.15) | copy-start | bytes 12292
where the time goes:
time: 184 us; the launch traced here: 182 us
  starting transfers between devices  53.3 us (29%)
  blocking collectives  49.4 us (27%)
  Pallas kernels  43.9 us (24%)
  local copies, waits for them, and re-layouts  21.3 us (12%)
  other arithmetic  13.4 us (7%)
    all_gather x1, blocking collectives, on_device(): gathered = lax.all_gather(log_decay, 'ctx')  34.1 us
    ppermute x10, starting transfers between devices, shifted(): lax.ppermute(x, 'ctx', [(i, i + by) for i in range(n) if 0 <= i + by < n])  29.1 us
    ppermute x4, starting transfers between devices, odd_to_even(): return lax.ppermute(x, 'ctx', [(i, i - 1) for i in range(1, n, 2)])  19.1 us
    pallas_call x4, Pallas kernels, on_device(): pl.pallas_call(partial(near_kernel, scale2, i), grid=(PER_CHUNK,), in_spe...  15.8 us
    pallas_call x4, Pallas kernels, on_device(): pl.pallas_call(partial(far_kernel, scale2, i), grid=(PER_CHUNK,), in_spec...  15.5 us
    all_gather x1, blocking collectives, on_device(): lax.all_gather(total.reshape(length // 128, 128), 'head')  15.4 us
    rev x2, local copies, waits for them, and re-layouts, on_device(): back = jnp.cumsum(before[:, ::-1], axis=1)[:, ::-1]  9.47 us
    pallas_call x1, Pallas kernels, on_device(): pl.pallas_call(partial(diag_kernel, scale2, divisor), grid=(heads,), in_s...  8.68 us
  transfers between devices with their start and end apart: 18, of which 0 were waited for; matrix products, arithmetic and copies ran while one was open for 17% of the time, Pallas kernels for 23%

commit v1 on v0

v1 whole, which is shorter than its diff:
```python
import math
from functools import partial

import jax
import jax.numpy as jnp
from jax import lax
from jax.experimental import pallas as pl
from jax.experimental.pallas import tpu as pltpu
from jax.sharding import PartitionSpec as P

D = 4096
BLK = 128
REACH = 4
EPSILON = 1e-06
NEG = -1e30
FAR_OFF = 1 << 30
LOG2E = math.log2(math.e)
PER_CHUNK = 2

NT = (((1,), (1,)), ((), ()))
TN = (((0,), (0,)), ((), ()))


def dot(a, b, dims):
    return lax.dot_general(a, b, dims, preferred_element_type=jnp.float32)


def params(mib=48):
    return pltpu.CompilerParams(vmem_limit_bytes=mib * 1024 * 1024)


def shifted(x, by):
    n = lax.axis_size("ctx")
    return lax.ppermute(x, "ctx", [(i, i + by) for i in range(n) if 0 <= i + by < n])


def even_to_odd(x):
    n = lax.axis_size("ctx")
    return lax.ppermute(x, "ctx", [(i, i + 1) for i in range(0, n - 1, 2)])


def odd_to_even(x):
    n = lax.axis_size("ctx")
    return lax.ppermute(x, "ctx", [(i, i - 1) for i in range(1, n, 2)])


def split3(x):
    hi = x.astype(jnp.bfloat16)
    rest = x - hi.astype(jnp.float32)
    mid = rest.astype(jnp.bfloat16)
    low = (rest - mid.astype(jnp.float32)).astype(jnp.bfloat16)
    return hi.astype(jnp.float32), mid.astype(jnp.float32), low.astype(jnp.float32)


def join3(rows, first):
    return rows[first : first + 1] + rows[first + 1 : first + 2] + rows[first + 2 : first + 3]


def stack_rows(rows, count, length):
    spot = lax.broadcasted_iota(jnp.int32, (count, length), 0)
    out = jnp.zeros((count, length), jnp.float32)
    for i, r in enumerate(rows):
        out = jnp.where(spot == i, r, out)
    return out


def lane_column(block, lane):
    spots = lax.broadcasted_iota(jnp.int32, block.shape, 1)
    return jnp.sum(jnp.where(spots == lane, block, 0.0), axis=1, keepdims=True)


def softmax_of(parts, scale2):
    top = parts[0]
    for p in parts[1:]:
        top = jnp.maximum(top, p)
    top = jnp.max(top, axis=0, keepdims=True) * scale2
    weights = [jnp.exp2(p * scale2 - top) for p in parts]
    total = weights[0]
    for w in weights[1:]:
        total = total + w
    total = jnp.sum(total, axis=0, keepdims=True)
    return top, total, [w.astype(jnp.bfloat16) for w in weights]


def prep_kernel(divisor, place_ref, docs_ref, mask_ref, ld_ref, k_ref, v_ref, thr_ref, start_ref, cum_ref, cumt_ref, coef_ref, dec_ref, entry_ref, pay_ref, token_ref):
    heads, length = ld_ref.shape
    tiles = length // BLK
    begin = place_ref[0] * length
    f32, bf16 = jnp.float32, jnp.bfloat16
    parts = jnp.concatenate(split3(ld_ref[...]), axis=0).astype(bf16)
    u = lax.broadcasted_iota(jnp.int32, (length, length), 0)
    t = lax.broadcasted_iota(jnp.int32, (length, length), 1)
    ones = jnp.where(u <= t, 1.0, 0.0).astype(bf16)
    sums = lax.dot_general(parts, ones, (((1,), (0,)), ((), ())), preferred_element_type=f32)
    cum = sums[:heads] + sums[heads : 2 * heads] + sums[2 * heads :]
    cum_ref[...] = cum
    cumt_ref[...] = jnp.concatenate([cum, jnp.zeros((BLK - heads, length), f32)], axis=0).T
    pos = begin + lax.broadcasted_iota(jnp.int32, (8, length), 1)
    start = jnp.zeros((8, length), jnp.int32)
    end = jnp.int32(0)
    entry = jnp.int32(0)
    for d in range(docs_ref.shape[0]):
        end = end + docs_ref[d]
        start = jnp.where(pos >= end, end, start)
        entry = jnp.where(begin - 1 >= end, end, entry)
    start = start - begin
    start_ref[...] = start
    entry_ref[0] = entry - begin
    coef_ref[...] = jnp.exp(cum) * jnp.where(start[:1] < 0, 1.0 / divisor, 0.0)
    tile_of = lax.broadcasted_iota(jnp.int32, (1, length), 1) // BLK
    reach = mask_ref.shape[1]
    for j in range(reach):
        keep = tile_of < 0
        for i in range(tiles):
            here = mask_ref[i, j] == 1
            if j == REACH * tiles + i:
                here = here | True
            keep = keep | ((tile_of == i) & here)
        base = (j - REACH * tiles) * BLK
        thr_ref[j : j + 1, :] = jnp.where(keep, start[:1] - base, FAR_OFF)
    last = cum[:, length - 1 :]
    chunks = heads // PER_CHUNK
    decs = []
    for c in range(chunks):
        rows = []
        for h in range(c * PER_CHUNK, (c + 1) * PER_CHUNK):
            rows += list(split3(last[h : h + 1] - cum[h : h + 1]))
        for h in range(c * PER_CHUNK, (c + 1) * PER_CHUNK):
            rows += list(split3(last[h : h + 1] + jnp.zeros((1, length), f32)))
        decs.append(stack_rows(rows, 16, length).astype(bf16))
        dec_ref[c * 16 : (c + 1) * 16, :] = decs[-1]
    half = k_ref.shape[1]
    pay_ref[0:length, 0:half] = k_ref[...]
    pay_ref[0:length, half:] = v_ref[...]
    pay_ref[length:, :] = decs[0]
    token_ref[...] = jnp.zeros_like(token_ref)


def pack_kernel(token_in, k_ref, v_ref, dec_ref, *refs):
    pays, token_ref = refs[:-1], refs[-1]
    length = k_ref.shape[0]
    half = PER_CHUNK * 128
    for c, pay in enumerate(pays, 1):
        pay[0:length, 0:half] = k_ref[:, c * half : (c + 1) * half]
        pay[0:length, half:] = v_ref[:, c * half : (c + 1) * half]
        pay[length:, :] = dec_ref[c * 16 : (c + 1) * 16, :]
    token_ref[...] = jnp.zeros_like(token_ref)


def own_kernel(scale2, divisor, base, token_in, q_ref, k_ref, v_ref, thr_ref, start_ref, cum_ref, cumt_ref, o_ref, top_ref, tot_ref, lin_ref, token_ref):
    i = pl.program_id(0)
    h = i + base
    q, k, v = q_ref[...], k_ref[...], v_ref[...]
    length = q.shape[0]
    scores = dot(k, q, NT)
    row = lax.broadcasted_iota(jnp.int32, (BLK, length), 0)
    col = lax.broadcasted_iota(jnp.int32, (BLK, length), 1)
    cum_row = cum_ref[pl.ds(h, 1), :]
    cum_col = lane_column(cumt_ref[...], h)
    soft, mix = [], []
    for j in range(length // BLK):
        s = scores[j * BLK : (j + 1) * BLK]
        causal = row <= col - j * BLK
        soft.append(jnp.where(causal & (row >= thr_ref[j : j + 1, :]), s, NEG))
        gap = cum_row - cum_col[j * BLK : (j + 1) * BLK]
        ok = causal & (row >= start_ref[0:1, :] - j * BLK)
        decay = jnp.exp(jnp.where(ok, gap, NEG))
        mix.append((s * decay * (1.0 / divisor)).astype(jnp.bfloat16))
    top, total, weights = softmax_of(soft, scale2)
    o_ref[...] = dot(v, jnp.concatenate(weights, axis=0), TN)
    lin_ref[...] = dot(v, jnp.concatenate(mix, axis=0), TN)
    top_ref[pl.ds(i, 1), :] = top
    tot_ref[pl.ds(i, 1), :] = total
    token_ref[...] = jnp.zeros_like(token_ref)


class Pieces:
    def __init__(self, two, even, odd, entry):
        self.two, self.even, self.odd, self.entry = two, even, odd, entry
        self.length = two.shape[0] - 16
        rows2 = two[self.length :, :].astype(jnp.float32)
        rows1 = (even[self.length :, :] + odd[self.length :, :]).astype(jnp.float32)
        n = PER_CHUNK
        self.tot1 = [join3(rows1, 3 * n + 3 * i) for i in range(n)]
        self.tot2 = [join3(rows2, 3 * n + 3 * i) for i in range(n)]
        after1 = [join3(rows1, 3 * i) for i in range(n)]
        after2 = [join3(rows2, 3 * i) + self.tot1[i] for i in range(n)]
        col = lax.broadcasted_iota(jnp.int32, (1, self.length), 1)
        w1 = [jnp.where(col - self.length >= entry, jnp.exp(x), 0.0) for x in after1]
        w2 = [jnp.where(col - 2 * self.length >= entry, jnp.exp(x), 0.0) for x in after2]
        self.weight = stack_rows(w1 + w2, BLK, self.length).T

    def keys(self, i):
        cols = slice(i * 128, (i + 1) * 128)
        return self.two[0 : self.length, cols], self.even[0 : self.length, cols] + self.odd[0 : self.length, cols]

    def values(self, i):
        lo = (PER_CHUNK + i) * 128
        cols = slice(lo, lo + 128)
        return self.two[0 : self.length, cols], self.even[0 : self.length, cols] + self.odd[0 : self.length, cols]

    def attend(self, i, q, thr_ref, scale2):
        tiles = self.length // BLK
        k2, k1 = self.keys(i)
        v2, v1 = self.values(i)
        row = lax.broadcasted_iota(jnp.int32, (BLK, q.shape[0]), 0)
        parts = []
        for first, keys in ((0, k2), (tiles, k1)):
            scores = dot(keys, q, NT)
            for j in range(tiles):
                ok = row >= thr_ref[first + j : first + j + 1, :]
                parts.append(jnp.where(ok, scores[j * BLK : (j + 1) * BLK], NEG))
        top, total, weights = softmax_of(parts, scale2)
        o = dot(v2, jnp.concatenate(weights[:tiles], axis=0), TN) + dot(v1, jnp.concatenate(weights[tiles:], axis=0), TN)
        n = PER_CHUNK
        kw1 = (k1.astype(jnp.float32) * self.weight[:, i : i + 1]).astype(jnp.bfloat16)
        kw2 = (k2.astype(jnp.float32) * self.weight[:, n + i : n + i + 1]).astype(jnp.bfloat16)
        state = dot(v2, kw2, TN) + dot(v1, kw1, TN)
        return top, total, o, state.astype(jnp.bfloat16)


def far_kernel(scale2, groups, *refs):
    token_in, entry_ref, q_ref, thr_ref = refs[:4]
    out_ref, token_ref = refs[-2:]
    n = 0
    for g in range(groups):
        two, even, odd = refs[4 + 3 * g : 7 + 3 * g]
        p = Pieces(two, even, odd, entry_ref[0])
        length = p.length
        for i in range(PER_CHUNK):
            top, total, o, state = p.attend(i, q_ref[:, n * 128 : (n + 1) * 128], thr_ref, scale2)
            r = n * 144
            out_ref[r : r + 128, 0:length] = (o * (1.0 / total)).astype(jnp.bfloat16)
            out_ref[r : r + 128, length:] = state
            lse = top + jnp.log(total) * LOG2E
            stats = stack_rows(list(split3(lse)) + [jnp.ones_like(lse)], 16, length)
            out_ref[r + 128 : r + 144, 0:length] = stats.astype(jnp.bfloat16)
            out_ref[r + 128 : r + 144, length:] = jnp.zeros((16, 128), jnp.bfloat16)
            n += 1
    token_ref[...] = jnp.zeros_like(token_ref)


def near_kernel(scale2, chunk, base, token_in, entry_ref, q_ref, thr_ref, coef_ref, two, even, odd, od_ref, topd_ref, totd_ref, lind_ref, x_ref, on_ref, st_ref, token_ref):
    p = Pieces(two, even, odd, entry_ref[0])
    length = p.length
    lses, coefs = [], []
    for i in range(PER_CHUNK):
        h = chunk * PER_CHUNK + i
        q = q_ref[:, i * 128 : (i + 1) * 128]
        rows = slice(i * 128, (i + 1) * 128)
        top, total, o, state = p.attend(i, q, thr_ref, scale2)
        top_d = topd_ref[h - base : h - base + 1, :]
        new_top = jnp.maximum(top, top_d)
        a, b = jnp.exp2(top - new_top), jnp.exp2(top_d - new_top)
        total = total * a + totd_ref[h - base : h - base + 1, :] * b
        inv = 1.0 / total
        on = o * (a * inv) + od_ref[rows, :] * (b * inv)
        coef = coef_ref[h : h + 1, :]
        x_ref[rows, :] = lind_ref[rows, :] + dot(state, q, NT) * coef + on
        on_ref[rows, :] = on
        lses.append(new_top + jnp.log(total) * LOG2E)
        through = jnp.where(entry_ref[0] < -2 * length, jnp.exp(p.tot1[i] + p.tot2[i]), 0.0)
        coefs.append(coef * through)
    st_ref[...] = stack_rows(lses + coefs, 8, length)
    token_ref[...] = jnp.zeros_like(token_ref)


def merge_kernel(groups, token_in, q_ref, pay_ref, *refs):
    mixed_ref, sq_ref, token_ref = refs[-3:]
    squares = None
    n = 0
    for g in range(groups):
        x_ref, on_ref, st_ref = refs[3 * g : 3 * g + 3]
        for i in range(PER_CHUNK):
            q = q_ref[:, n * 128 : (n + 1) * 128]
            length = q.shape[0]
            r = n * 144
            rows = slice(i * 128, (i + 1) * 128)
            stats = pay_ref[r + 128 : r + 144, 0:length].astype(jnp.float32)
            lse_far = join3(stats, 0)
            far = pay_ref[r : r + 128, 0:length].astype(jnp.float32)
            share = 1.0 / (1.0 + jnp.exp2(jnp.minimum(st_ref[i : i + 1, :] - lse_far, 120.0)))
            share = jnp.where((lse_far > 0.5 * NEG) & (stats[3:4] > 0.5), share, 0.0)
            lin = dot(pay_ref[r : r + 128, length:], q, NT) * st_ref[PER_CHUNK + i : PER_CHUNK + i + 1, :]
            mixed = x_ref[rows, :] + share * (far - on_ref[rows, :]) + lin
            mixed_ref[n * 128 : (n + 1) * 128, :] = mixed
            part = jnp.sum(mixed * mixed, axis=0, keepdims=True)
            squares = part if squares is None else squares + part
            n += 1
    sq_ref[...] = squares
    token_ref[...] = jnp.zeros_like(token_ref)


def norm_kernel(parts, *refs):
    mixed_refs, sq_ref, gain_ref, out_ref = refs[:parts], refs[parts], refs[parts + 1], refs[parts + 2]
    inverse = lax.rsqrt(jnp.sum(sq_ref[...], axis=0, keepdims=True) / D + EPSILON)
    col = 0
    for ref in mixed_refs:
        for i in range(ref.shape[0] // 128):
            part = (ref[i * 128 : (i + 1) * 128, :] * inverse).T
            out_ref[:, col : col + 128] = (part * gain_ref[:, col : col + 128]).astype(jnp.bfloat16)
            col += 128


def on_device(query, key, value, log_decay, doc_lengths, tile_mask, gain):
    length, features = query.shape
    heads = log_decay.shape[0]
    hd = features // heads
    tiles = length // BLK
    chunks = heads // PER_CHUNK
    width = PER_CHUNK * hd
    divisor = hd * math.sqrt(length)
    scale2 = LOG2E / math.sqrt(hd)
    place = lax.axis_index("ctx").astype(jnp.int32).reshape(1)
    f32, bf16 = jnp.float32, jnp.bfloat16
    shape = jax.ShapeDtypeStruct
    token_shape = shape((8, 128), f32)
    smem = pl.BlockSpec(memory_space=pltpu.SMEM)
    vmem = pl.BlockSpec(memory_space=pltpu.VMEM)
    loose = pl.BlockSpec(memory_space=pl.ANY)

    def cost(us):
        return pl.CostEstimate(flops=0, bytes_accessed=int(us * 3.69e6), transcendentals=0)

    def cols(first, count):
        return pl.BlockSpec((length, count), lambda *_: (0, first))

    q_far = shifted(query, -2)
    kv_rows = length + 16
    thr, start, cum, cum_t, coef, dec, entry, pay0, token = pl.pallas_call(
        partial(prep_kernel, divisor),
        grid=(1,),
        in_specs=[smem, smem, smem, vmem, cols(0, width), cols(0, width)],
        out_specs=[vmem] * 6 + [smem] + [vmem] * 2,
        out_shape=[
            shape(((REACH + 1) * tiles, length), jnp.int32),
            shape((8, length), jnp.int32),
            shape((heads, length), f32),
            shape((length, BLK), f32),
            shape((heads, length), f32),
            shape((16 * chunks, length), bf16),
            shape((1,), jnp.int32),
            shape((kv_rows, 2 * width), bf16),
            token_shape,
        ],
        compiler_params=params(),
        cost_estimate=cost(2),
        name="prep",
    )(place, doc_lengths, tile_mask, log_decay, key, value)
    packed = pl.pallas_call(
        pack_kernel,
        in_specs=[loose] + [vmem] * 3,
        out_specs=[vmem] * chunks,
        out_shape=[shape((kv_rows, 2 * width), bf16)] * (chunks - 1) + [token_shape],
        compiler_params=params(),
        cost_estimate=cost(3),
        name="pack",
    )(token, key, value, dec)
    token = packed[-1]
    kv = [pay0] + list(packed[:-1])
    two_back, from_even, from_odd = [], [], []
    for x in kv:
        two_back.append(shifted(x, 2))
        from_even.append(even_to_odd(x))
    thr_far = shifted(thr[: 2 * tiles], -2)
    thr_near = thr[2 * tiles : 4 * tiles]
    thr_own = thr[4 * tiles :]
    for x in two_back:
        from_odd.append(odd_to_even(x))

    half = max(PER_CHUNK, heads // 2)
    own = []
    for base in range(0, heads, half):
        whole = lambda *s: pl.BlockSpec(s, lambda h: (0,) * len(s))
        head_cols = pl.BlockSpec((length, hd), lambda h, base=base: (0, h + base))
        head_rows = pl.BlockSpec((hd, length), lambda h: (h, 0))
        *result, token = pl.pallas_call(
            partial(own_kernel, scale2, divisor, base),
            grid=(half,),
            in_specs=[loose]
            + [head_cols] * 3
            + [whole(tiles, length), whole(8, length), whole(heads, length), whole(length, BLK)],
            out_specs=[head_rows, whole(half, length), whole(half, length), head_rows, whole(8, 128)],
            out_shape=[
                shape((half * hd, length), f32),
                shape((half, length), f32),
                shape((half, length), f32),
                shape((half * hd, length), f32),
                token_shape,
            ],
            compiler_params=params(),
            cost_estimate=cost(half * 1.1),
            name="own_piece",
        )(token, query, key, value, thr_own, start, cum, cum_t)
        own.append((base, result))

    def near(c, token):
        base, (o_d, top_d, tot_d, lin_d) = own[c * PER_CHUNK // half]
        rows = pl.BlockSpec((width, length), lambda *_: (c - base // PER_CHUNK, 0))
        x, on, st, token = pl.pallas_call(
            partial(near_kernel, scale2, c, base),
            grid=(1,),
            in_specs=[loose, smem, cols(c, width), vmem, vmem, vmem, vmem, vmem, rows, vmem, vmem, rows],
            out_specs=[vmem] * 4,
            out_shape=[shape((width, length), f32), shape((width, length), f32), shape((8, length), f32), token_shape],
            compiler_params=params(),
            cost_estimate=cost(4),
            name="near_pieces",
        )(token, entry, query, thr_near, coef, two_back[c], from_even[c], from_odd[c], o_d, top_d, tot_d, lin_d)
        return (x, on, st), token

    def far(first, groups, token):
        args = []
        for c in range(first, first + groups):
            args += [two_back[c], from_even[c], from_odd[c]]
        pay, token = pl.pallas_call(
            partial(far_kernel, scale2, groups),
            grid=(1,),
            in_specs=[loose, smem, cols(first // groups, groups * width), vmem] + [vmem] * len(args),
            out_specs=[vmem] * 2,
            out_shape=[shape((groups * PER_CHUNK * 144, length + hd), bf16), token_shape],
            compiler_params=params(),
            cost_estimate=cost(4 * groups),
            name="far_pieces",
        )(token, entry, q_far, thr_far, *args)
        return shifted(pay, 2), token

    def merge(first, groups, pay, parts, token):
        args = []
        for c in range(first, first + groups):
            args += list(parts[c])
        return pl.pallas_call(
            partial(merge_kernel, groups),
            grid=(1,),
            in_specs=[loose, cols(first // groups, groups * width), vmem] + [vmem] * len(args),
            out_specs=[vmem] * 3,
            out_shape=[shape((groups * width, length), f32), shape((1, length), f32), token_shape],
            compiler_params=params(),
            cost_estimate=cost(1.5 * groups),
            name="merge",
        )(token, query, pay, *args)

    plan = [(0, chunks // 2)] + [(c, 1) for c in range(chunks // 2, chunks)]
    parts, pays = {}, []
    for first, groups in plan:
        if first == 0:
            for c in range(groups):
                parts[c], token = near(c, token)
            pay, token = far(first, groups, token)
        else:
            pay, token = far(first, groups, token)
            parts[first], token = near(first, token)
        pays.append(pay)
    mixed, total = [], None
    for (first, groups), pay in zip(plan, pays):
        m, s, token = merge(first, groups, pay, parts, token)
        mixed.append(m)
        total = s if total is None else total + s
    ranks = lax.axis_size("head")
    everyone = lax.all_gather(total.reshape(length // 128, 128), "head").reshape(ranks, length)
    return pl.pallas_call(
        partial(norm_kernel, len(mixed)),
        out_shape=shape((length, features), bf16),
        compiler_params=params(),
        name="normalize",
    )(*mixed, everyone, gain[None, :])


def solution(mesh):
    placed = (
        P("ctx", "head"),
        P("ctx", "head"),
        P("ctx", "head"),
        P("head", "ctx"),
        P(),
        P("ctx", None),
        P("head"),
    )
    return jax.shard_map(on_device, mesh=mesh, in_specs=placed, out_specs=P("ctx", "head"), check_vma=False)
```

time: 184 us -> 133 us (0.72)
  blocking collectives: 49.4 us -> 8.25 us
  waiting for transfers between devices: 0.05 us -> 29.9 us
  other arithmetic: 13.4 us -> 0.01 us
  starting transfers between devices: 53.3 us -> 42.4 us
  local copies, waits for them, and re-layouts: 21.3 us -> 11.3 us
  Pallas kernels: 43.9 us -> 38.7 us
    all_gather x1 -> x0, blocking collectives: 34.1 us -> none  [on_device(): gathered = lax.all_gather(log_decay, 'ctx')]
    ppermute x10 -> x9, waiting for transfers between devices: 0.03 us -> 28.7 us  [shifted(): lax.ppermute(x, 'ctx', [(i, i + by) for i in range(n) if 0 <= i + by < n])]
    unnamed x20 -> x65, local copies, waits for them, and re-layouts: 0.15 us -> 11.3 us
    rev x2 -> x0, local copies, waits for them, and re-layouts: 9.47 us -> none  [on_device(): back = jnp.cumsum(before[:, ::-1], axis=1)[:, ::-1]]
    ppermute x4, starting transfers between devices: 19.1 us -> 10.4 us  [odd_to_even(): return lax.ppermute(x, 'ctx', [(i, i - 1) for i in range(1, n, 2)])]
    all_gather x1, blocking collectives: 15.4 us -> 8.25 us  [on_device(): lax.all_gather(total.reshape(length // 128, 128), 'head')]
    concatenate x4 -> x0, other arithmetic: 6.37 us -> none  [on_device(): jnp.concatenate([key[:, i * width:(i + 1) * width], value[:, i * width:(i...]
    pallas_call x14 -> x15, Pallas kernels: 43.9 us -> 38.7 us  [the longest x4 13.8 us: near(): pl.pallas_call(partial(near_kernel, scale2, c, base), grid=(1,), in_specs...]
  transfers between devices with their start and end apart: 18 -> 17, of which waited for: 0 -> 7; matrix products, arithmetic and copies ran while one was open for 17% -> 0% of each run, Pallas kernels for 23% -> 27%
where the time goes in v1:
time: 133 us; the launch traced here: 131 us
  starting transfers between devices  42.4 us (32%)
  Pallas kernels  38.7 us (29%)
  waiting for transfers between devices  29.9 us (22%)
  local copies, waits for them, and re-layouts  11.3 us (8%)
  blocking collectives  8.25 us (6%)
    ppermute x9, waiting for transfers between devices, shifted(): lax.ppermute(x, 'ctx', [(i, i + by) for i in range(n) if 0 <= i + by < n])  28.7 us
    ppermute x9, starting transfers between devices, shifted(): lax.ppermute(x, 'ctx', [(i, i + by) for i in range(n) if 0 <= i + by < n])  26.8 us
    pallas_call x4, Pallas kernels, near(): pl.pallas_call(partial(near_kernel, scale2, c, base), grid=(1,), in_specs...  13.8 us
    pallas_call x3, Pallas kernels, far(): pl.pallas_call(partial(far_kernel, scale2, groups), grid=(1,), in_specs=[...  11.3 us
    unnamed x65, local copies, waits for them, and re-layouts  11.3 us
    ppermute x4, starting transfers between devices, odd_to_even(): return lax.ppermute(x, 'ctx', [(i, i - 1) for i in range(1, n, 2)])  10.4 us
    all_gather x1, blocking collectives, on_device(): lax.all_gather(total.reshape(length // 128, 128), 'head')  8.25 us
    pallas_call x2, Pallas kernels, on_device(): pl.pallas_call(partial(own_kernel, scale2, divisor, base), grid=(half,),...  7.96 us
  transfers between devices with their start and end apart: 17, of which 7 were waited for; matrix products, arithmetic and copies ran while one was open for 0% of the time, Pallas kernels for 27%

profile of v1, /device:TPU:3, one launch (start us, length us, event | category | flops | bytes accessed | tf_op | source)
XLA Modules:
  0.0 131.1 jit_solution(5933435266083822757)
XLA Ops:
  0.0 0.7 copy-done.30
  0.7 1.2 copy-done.1
  1.9 1.2 copy-done.3
  3.1 0.7 copy-done.28
  3.9 1.2 prep.1
  5.1 3.2 %collective-permute-start = (bf16[528,512]{1,0:T(8,128)(2,1)S(1)}, bf16[528,512]{1,0:T(8,128)(2,1)S(1)}, u32[]{:S(2)}, u32[]{:S(2)}) collective-permute-start(bf16[528,512]{1,0:T(8,128)(2,1)S(1)} %get-tuple-element.69), channel_id=1, source_target_pairs={{0,8},{4,12},{8,16},{12,20},{16,24},{20,28},{1,9},{5,13},{9,17},{1... | collective-permute-start | bytes 1622024 | tf_op jit(solution)/shard_map/ppermute | solution.py:34
  8.3 1.3 collective-permute-start.1
  9.6 0.0 copy-start
  9.6 1.1 pack.1
  10.8 3.2 %collective-permute-start.3 = (bf16[528,512]{1,0:T(8,128)(2,1)S(1)}, bf16[528,512]{1,0:T(8,128)(2,1)S(1)}, u32[]{:S(2)}, u32[]{:S(2)}) collective-permute-start(bf16[528,512]{1,0:T(8,128)(2,1)S(1)} %get-tuple-element.75), channel_id=1, source_target_pairs={{0,8},{4,12},{8,16},{12,20},{16,24},{20,28},{1,9},{5,13},{9,17},{1... | collective-permute-start | bytes 1622024 | tf_op jit(solution)/shard_map/ppermute | solution.py:34
  14.0 1.3 collective-permute-start.4
  15.3 1.3 collective-permute-start.7
  16.6 3.5 %collective-permute-done.7.refs_3_ = s32[8,512]{1,0:T(8,128)S(1)} collective-permute-done((s32[8,512]{1,0:T(8,128)S(1)}, s32[8,512]{1,0:T(8,128)S(1)}, u32[]{:S(2)}, u32[]{:S(2)}) %collective-permute-start.7) | collective-permute-done | bytes 16416 | tf_op jit(solution)/shard_map/ppermute | solution.py:34
  20.1 1.3 collective-permute-start.6
  21.4 0.0 collective-permute-done.two.refs_4_
  21.4 4.0 %collective-permute-start.8 = (bf16[528,512]{1,0:T(8,128)(2,1)}, bf16[528,512]{1,0:T(8,128)(2,1)S(1)}, u32[]{:S(2)}, u32[]{:S(2)}) collective-permute-start(bf16[528,512]{1,0:T(8,128)(2,1)} %get-tuple-element.78), channel_id=1, source_target_pairs={{0,8},{4,12},{8,16},{12,20},{16,24},{20,28},{1,9},{5,13},{9,17},{1... | collective-permute-start | bytes 1622024 | tf_op jit(solution)/shard_map/ppermute | solution.py:34
  25.4 0.0 collective-permute-done.1.even.refs_5_
  25.4 0.8 copy-done.7
  26.2 3.2 %collective-permute-start.11 = (bf16[528,512]{1,0:T(8,128)(2,1)}, bf16[528,512]{1,0:T(8,128)(2,1)S(1)}, u32[]{:S(2)}, u32[]{:S(2)}) collective-permute-start(bf16[528,512]{1,0:T(8,128)(2,1)} %get-tuple-element.85), channel_id=1, source_target_pairs={{0,8},{4,12},{8,16},{12,20},{16,24},{20,28},{1,9},{5,13},{9,17},{1... | collective-permute-start | bytes 1622024 | tf_op jit(solution)/shard_map/ppermute | solution.py:34
  29.4 1.4 %collective-permute-done.3.two.refs_7_ = bf16[528,512]{1,0:T(8,128)(2,1)S(1)} collective-permute-done((bf16[528,512]{1,0:T(8,128)(2,1)S(1)}, bf16[528,512]{1,0:T(8,128)(2,1)S(1)}, u32[]{:S(2)}, u32[]{:S(2)}) %collective-permute-start.3) | collective-permute-done | bytes 540704 | tf_op jit(solution)/shard_map/ppermute | solution.py:34
  30.8 2.7 %collective-permute-start.2 = (bf16[528,512]{1,0:T(8,128)(2,1)S(1)}, bf16[528,512]{1,0:T(8,128)(2,1)S(1)}, u32[]{:S(2)}, u32[]{:S(2)}) collective-permute-start(bf16[528,512]{1,0:T(8,128)(2,1)S(1)} %collective-permute-done.two.refs_4_), channel_id=1, source_target_pairs={{4,0},{12,8},{20,16},{28,24},{5,1},{13,9},{21,17},{29,25},{6,2},{1... | collective-permute-start | bytes 1622024 | tf_op jit(solution)/shard_map/ppermute | solution.py:44
  33.5 1.1 collective-permute-done.4.even.refs_8_
  34.6 0.8 copy-done.12
  35.4 1.3 %collective-permute-start.5 = (bf16[528,512]{1,0:T(8,128)(2,1)S(1)}, bf16[528,512]{1,0:T(8,128)(2,1)S(1)}, u32[]{:S(2)}, u32[]{:S(2)}) collective-permute-start(bf16[528,512]{1,0:T(8,128)(2,1)S(1)} %collective-permute-done.3.two.refs_7_), channel_id=1, source_target_pairs={{4,0},{12,8},{20,16},{28,24},{5,1},{13,9},{21,17},{29,25},{6,2},{1... | collective-permute-start | bytes 1622024 | tf_op jit(solution)/shard_map/ppermute | solution.py:44
  36.7 0.8 copy-done.10
  37.5 4.9 %collective-permute-done.8.refs_4_.two = bf16[528,512]{1,0:T(8,128)(2,1)S(1)} collective-permute-done((bf16[528,512]{1,0:T(8,128)(2,1)}, bf16[528,512]{1,0:T(8,128)(2,1)S(1)}, u32[]{:S(2)}, u32[]{:S(2)}) %collective-permute-start.8) | collective-permute-done | bytes 540704 | tf_op jit(solution)/shard_map/ppermute | solution.py:34
  42.5 1.3 collective-permute-start.9
  43.8 10.3 %collective-permute-done.11.refs_4_.two = bf16[528,512]{1,0:T(8,128)(2,1)S(1)} collective-permute-done((bf16[528,512]{1,0:T(8,128)(2,1)}, bf16[528,512]{1,0:T(8,128)(2,1)S(1)}, u32[]{:S(2)}, u32[]{:S(2)}) %collective-permute-start.11) | collective-permute-done | bytes 540704 | tf_op jit(solution)/shard_map/ppermute | solution.py:34
  54.1 2.2 %collective-permute-start.10 = (bf16[528,512]{1,0:T(8,128)(2,1)S(1)}, bf16[528,512]{1,0:T(8,128)(2,1)S(1)}, u32[]{:S(2)}, u32[]{:S(2)}) collective-permute-start(bf16[528,512]{1,0:T(8,128)(2,1)S(1)} %collective-permute-done.8.refs_4_.two), channel_id=1, source_target_pairs={{4,0},{12,8},{20,16},{28,24},{5,1},{13,9},{21,17},{29,25},{6,2},{1... | collective-permute-start | bytes 1622024 | tf_op jit(solution)/shard_map/ppermute | solution.py:44
  56.2 0.0 collective-permute-done.2.odd.refs_6_
  56.3 1.3 collective-permute-start.12
  57.6 0.0 collective-permute-done.5.odd.refs_9_
  57.6 4.2 %collective-permute-start.13 = (bf16[528,512]{1,0:T(8,128)(2,1)S(1)}, bf16[528,512]{1,0:T(8,128)(2,1)S(1)}, u32[]{:S(2)}, u32[]{:S(2)}) collective-permute-start(bf16[528,512]{1,0:T(8,128)(2,1)S(1)} %collective-permute-done.11.refs_4_.two), channel_id=1, source_target_pairs={{4,0},{12,8},{20,16},{28,24},{5,1},{13,9},{21,17},{29,25},{6,2},{1... | collective-permute-start | bytes 1622024 | tf_op jit(solution)/shard_map/ppermute | solution.py:44
  61.8 4.0 %own_piece.2 = (f32[512,512]{1,0:T(8,128)S(1)}, f32[4,512]{1,0:T(4,128)S(1)}, f32[4,512]{1,0:T(4,128)S(1)}, f32[512,512]{1,0:T(8,128)S(1)}, f32[8,128]{1,0:T(8,128)S(1)}) custom-call(f32[8,128]{1,0:T(8,128)S(1)} %get-tuple-element.60.token_in, bf16[512,1024]{1,0:T(8,128)(2,1)S(1)} %copy-done, bf16[512,1024]{1,0:T(8,128)(2,1)S(1)} %copy-done.2, ...), custom_call_target="tpu_custom_call" | custom-call | bytes 16236000 | tf_op jit(solution)/shard_map/own_piece/pallas_call | solution.py:377
  65.9 4.0 %own_piece.3 = (f32[512,512]{1,0:T(8,128)S(1)}, f32[4,512]{1,0:T(4,128)S(1)}, f32[4,512]{1,0:T(4,128)S(1)}, f32[512,512]{1,0:T(8,128)S(1)}, f32[8,128]{1,0:T(8,128)S(1)}) custom-call(f32[8,128]{1,0:T(8,128)S(1)} %get-tuple-element.65.token_in, bf16[512,1024]{1,0:T(8,128)(2,1)S(1)} %copy-done, bf16[512,1024]{1,0:T(8,128)(2,1)S(1)} %copy-done.2, ...), custom_call_target="tpu_custom_call" | custom-call | bytes 16236000 | tf_op jit(solution)/shard_map/own_piece/pallas_call | solution.py:377
  69.9 3.5 %near_pieces.4 = (f32[256,512]{1,0:T(8,128)S(1)}, f32[256,512]{1,0:T(8,128)S(1)}, f32[8,512]{1,0:T(8,128)S(1)}, f32[8,128]{1,0:T(8,128)S(1)}) custom-call(f32[8,128]{1,0:T(8,128)S(1)} %get-tuple-element.66.token_in, s32[1]{0:T(128)} %get-tuple-element.67.entry_ref.refs_1_, bf16[512,1024]{1,0:T(8,128)(2,1)S(1)} %copy-done, ...), custom_call_target="tpu_custom_call" | custom-call | bytes 14760000 | tf_op jit(solution)/shard_map/near_pieces/pallas_call | solution.py:400
  73.4 0.8 copy-done.20
  74.2 0.8 copy-done.22
  75.0 1.0 copy-done.18
  76.0 3.5 %near_pieces.5 = (f32[256,512]{1,0:T(8,128)S(1)}, f32[256,512]{1,0:T(8,128)S(1)}, f32[8,512]{1,0:T(8,128)S(1)}, f32[8,128]{1,0:T(8,128)S(1)}) custom-call(f32[8,128]{1,0:T(8,128)S(1)} %get-tuple-element.74.token_in, s32[1]{0:T(128)} %get-tuple-element.67.entry_ref.refs_1_, bf16[512,1024]{1,0:T(8,128)(2,1)S(1)} %copy-done, ...), custom_call_target="tpu_custom_call" | custom-call | bytes 14760000 | tf_op jit(solution)/shard_map/near_pieces/pallas_call | solution.py:400
  79.6 0.8 copy-done.24
  80.4 0.8 copy-done.26
  81.2 0.0 collective-permute-done.6.refs_2_
  81.2 5.3 %far_pieces.3 = (bf16[576,640]{1,0:T(8,128)(2,1)S(1)}, f32[8,128]{1,0:T(8,128)S(1)}) custom-call(f32[8,128]{1,0:T(8,128)S(1)} %get-tuple-element.76.refs_0_, s32[1]{0:T(128)} %get-tuple-element.67.entry_ref.refs_1_, bf16[512,1024]{1,0:T(8,128)(2,1)S(1)} %collective-permute-done.6.refs_2_, s32[8,512]{1,0:T(8,128)S(1)} %collective-permute-done.7.refs_3_, ...), custom_call_target="tpu_custom_call" | custom-call | bytes 29520000 | tf_op jit(solution)/shard_map/far_pieces/pallas_call | solution.py:416
  86.5 4.3 %collective-permute-start.14 = (bf16[576,640]{1,0:T(8,128)(2,1)S(1)}, bf16[576,640]{1,0:T(8,128)(2,1)S(1)}, u32[]{:S(2)}, u32[]{:S(2)}) collective-permute-start(bf16[576,640]{1,0:T(8,128)(2,1)S(1)} %get-tuple-element.88), channel_id=1, source_target_pairs={{0,8},{4,12},{8,16},{12,20},{16,24},{20,28},{1,9},{5,13},{9,17},{1... | collective-permute-start | bytes 2211848 | tf_op jit(solution)/shard_map/ppermute | solution.py:34
  90.8 0.0 collective-permute-done.9.refs_5_.even
  90.8 0.0 collective-permute-done.10.refs_6_.odd
  90.8 3.0 %far_pieces.4 = (bf16[288,640]{1,0:T(8,128)(2,1)S(1)}, f32[8,128]{1,0:T(8,128)S(1)}) custom-call(f32[8,128]{1,0:T(8,128)S(1)} %get-tuple-element.77.refs_0_, s32[1]{0:T(128)} %get-tuple-element.67.entry_ref.refs_1_, bf16[512,1024]{1,0:T(8,128)(2,1)S(1)} %collective-permute-done.6.refs_2_, s32[8,512]{1,0:T(8,128)S(1)} %collective-permute-done.7.refs_3_, ...), custom_call_target="tpu_custom_call" | custom-call | bytes 14760000 | tf_op jit(solution)/shard_map/far_pieces/pallas_call | solution.py:416
  93.8 3.2 %collective-permute-start.15 = (bf16[288,640]{1,0:T(8,128)(2,1)S(1)}, bf16[288,640]{1,0:T(8,128)(2,1)S(1)}, u32[]{:S(2)}, u32[]{:S(2)}) collective-permute-start(bf16[288,640]{1,0:T(8,128)(2,1)S(1)} %get-tuple-element.97), channel_id=1, source_target_pairs={{0,8},{4,12},{8,16},{12,20},{16,24},{20,28},{1,9},{5,13},{9,17},{1... | collective-permute-start | bytes 1105928 | tf_op jit(solution)/shard_map/ppermute | solution.py:34
  97.0 3.3 %near_pieces.6 = (f32[256,512]{1,0:T(8,128)S(1)}, f32[256,512]{1,0:T(8,128)S(1)}, f32[8,512]{1,0:T(8,128)S(1)}, f32[8,128]{1,0:T(8,128)S(1)}) custom-call(f32[8,128]{1,0:T(8,128)S(1)} %get-tuple-element.79.token_in, s32[1]{0:T(128)} %get-tuple-element.67.entry_ref.refs_1_, bf16[512,1024]{1,0:T(8,128)(2,1)S(1)} %copy-done, ...), custom_call_target="tpu_custom_call" | custom-call | bytes 14760000 | tf_op jit(solution)/shard_map/near_pieces/pallas_call | solution.py:400
  100.3 0.0 collective-permute-done.12.refs_5_.even
  100.3 0.0 collective-permute-done.13.refs_6_.odd
  100.3 3.0 %far_pieces.5 = (bf16[288,640]{1,0:T(8,128)(2,1)S(1)}, f32[8,128]{1,0:T(8,128)S(1)}) custom-call(f32[8,128]{1,0:T(8,128)S(1)} %get-tuple-element.84.refs_0_, s32[1]{0:T(128)} %get-tuple-element.67.entry_ref.refs_1_, bf16[512,1024]{1,0:T(8,128)(2,1)S(1)} %collective-permute-done.6.refs_2_, s32[8,512]{1,0:T(8,128)S(1)} %collective-permute-done.7.refs_3_, ...), custom_call_target="tpu_custom_call" | custom-call | bytes 14760000 | tf_op jit(solution)/shard_map/far_pieces/pallas_call | solution.py:416
  103.4 3.2 %collective-permute-start.16 = (bf16[288,640]{1,0:T(8,128)(2,1)S(1)}, bf16[288,640]{1,0:T(8,128)(2,1)S(1)}, u32[]{:S(2)}, u32[]{:S(2)}) collective-permute-start(bf16[288,640]{1,0:T(8,128)(2,1)S(1)} %get-tuple-element.103), channel_id=1, source_target_pairs={{0,8},{4,12},{8,16},{12,20},{16,24},{20,28},{1,9},{5,13},{9,17},{1... | collective-permute-start | bytes 1105928 | tf_op jit(solution)/shard_map/ppermute | solution.py:34
  106.6 3.5 %near_pieces.7 = (f32[256,512]{1,0:T(8,128)S(1)}, f32[256,512]{1,0:T(8,128)S(1)}, f32[8,512]{1,0:T(8,128)S(1)}, f32[8,128]{1,0:T(8,128)S(1)}) custom-call(f32[8,128]{1,0:T(8,128)S(1)} %get-tuple-element.86.token_in, s32[1]{0:T(128)} %get-tuple-element.67.entry_ref.refs_1_, bf16[512,1024]{1,0:T(8,128)(2,1)S(1)} %copy-done, ...), custom_call_target="tpu_custom_call" | custom-call | bytes 14760000 | tf_op jit(solution)/shard_map/near_pieces/pallas_call | solution.py:400
  110.1 0.0 collective-permute-done.14.pay_ref
  110.2 0.5 merge.3
  110.7 1.1 collective-permute-done.15.pay_ref
  111.8 0.3 merge.4
  112.1 7.6 %collective-permute-done.16.pay_ref = bf16[288,640]{1,0:T(8,128)(2,1)S(1)} collective-permute-done((bf16[288,640]{1,0:T(8,128)(2,1)S(1)}, bf16[288,640]{1,0:T(8,128)(2,1)S(1)}, u32[]{:S(2)}, u32[]{:S(2)}) %collective-permute-start.16) | collective-permute-done | bytes 368672 | tf_op jit(solution)/shard_map/ppermute | solution.py:34
  119.7 0.9 merge.5
  120.6 8.2 %all_gather.3 = f32[4,4,128]{2,1,0:T(4,128)S(1)} all-gather(f32[1,4,128]{2,1,0:T(4,128)S(1)} %bitcast.10), channel_id=1, replica_groups=mesh['ctx'=8,'head'=4] {'head'}, dimensions={0}, use_global_device_ids=true | all-gather | bytes 10240 | tf_op jit(solution)/shard_map/all_gather | solution.py:460
  128.8 0.7 copy-done.29
  129.5 1.6 %normalize.1 = bf16[512,1024]{1,0:T(8,128)(2,1)} custom-call(f32[512,512]{1,0:T(8,128)S(1)} %get-tuple-element.95.refs_0_, f32[256,512]{1,0:T(8,128)S(1)} %get-tuple-element.101.refs_1_, f32[256,512]{1,0:T(8,128)S(1)} %get-tuple-element.107.refs_2_, f32[4,512]{1,0:T(4,128)S(1)} %bitcast.7, f32[1,1024]{1,0:T(1,128)S(1)} %bitcast.8), custom_call_target="tpu_custom_call" | custom-call | tf_op jit(solution)/shard_map/normalize/pallas_call | solution.py:461
  (54 shorter events, 0.1 us)
Async XLA Ops:
  0.0 0.7 copy-start.30
  0.0 0.7 copy-start.31
  0.7 1.2 copy-start.1
  1.9 1.2 copy-start.3
  3.1 0.7 copy-start.28
  3.9 5.8 %copy-start.2 = (bf16[512,1024]{1,0:T(8,128)(2,1)S(1)}, bf16[512,1024]{1,0:T(8,128)(2,1)}, u32[]{:S(2)}) copy-start(bf16[512,1024]{1,0:T(8,128)(2,1)} %k_ref.7) | copy-start | bytes 3145732
  3.9 5.8 %copy-start.4 = (bf16[512,1024]{1,0:T(8,128)(2,1)S(1)}, bf16[512,1024]{1,0:T(8,128)(2,1)}, u32[]{:S(2)}) copy-start(bf16[512,1024]{1,0:T(8,128)(2,1)} %v_ref.7) | copy-start | bytes 3145732
  5.1 16.3 %collective-permute-start = (bf16[528,512]{1,0:T(8,128)(2,1)S(1)}, bf16[528,512]{1,0:T(8,128)(2,1)S(1)}, u32[]{:S(2)}, u32[]{:S(2)}) collective-permute-start(bf16[528,512]{1,0:T(8,128)(2,1)S(1)} %get-tuple-element.69), channel_id=1, source_target_pairs={{0,8},{4,12},{8,16},{12,20},{16,24},{20,28},{1,9},{5,13},{9,17},{1... | collective-permute-start | bytes 1622024 | tf_op jit(solution)/shard_map/ppermute | solution.py:34
  8.3 17.1 %collective-permute-start.1 = (bf16[528,512]{1,0:T(8,128)(2,1)S(1)}, bf16[528,512]{1,0:T(8,128)(2,1)S(1)}, u32[]{:S(2)}, u32[]{:S(2)}) collective-permute-start(bf16[528,512]{1,0:T(8,128)(2,1)S(1)} %get-tuple-element.69), channel_id=1, source_target_pairs={{0,4},{8,12},{16,20},{24,28},{1,5},{9,13},{17,21},{25,29},{2,6},{1... | collective-permute-start | bytes 1622024 | tf_op jit(solution)/shard_map/ppermute | solution.py:39
  9.6 10.4 %copy-start = (bf16[512,1024]{1,0:T(8,128)(2,1)S(1)}, bf16[512,1024]{1,0:T(8,128)(2,1)}, u32[]{:S(2)}) copy-start(bf16[512,1024]{1,0:T(8,128)(2,1)} %q_ref.17) | copy-start | bytes 3145732
  10.8 20.0 %collective-permute-start.3 = (bf16[528,512]{1,0:T(8,128)(2,1)S(1)}, bf16[528,512]{1,0:T(8,128)(2,1)S(1)}, u32[]{:S(2)}, u32[]{:S(2)}) collective-permute-start(bf16[528,512]{1,0:T(8,128)(2,1)S(1)} %get-tuple-element.75), channel_id=1, source_target_pairs={{0,8},{4,12},{8,16},{12,20},{16,24},{20,28},{1,9},{5,13},{9,17},{1... | collective-permute-start | bytes 1622024 | tf_op jit(solution)/shard_map/ppermute | solution.py:34
  14.0 20.6 %collective-permute-start.4 = (bf16[528,512]{1,0:T(8,128)(2,1)S(1)}, bf16[528,512]{1,0:T(8,128)(2,1)S(1)}, u32[]{:S(2)}, u32[]{:S(2)}) collective-permute-start(bf16[528,512]{1,0:T(8,128)(2,1)S(1)} %get-tuple-element.75), channel_id=1, source_target_pairs={{0,4},{8,12},{16,20},{24,28},{1,5},{9,13},{17,21},{25,29},{2,6},{1... | collective-permute-start | bytes 1622024 | tf_op jit(solution)/shard_map/ppermute | solution.py:39
  15.3 4.8 %collective-permute-start.7 = (s32[8,512]{1,0:T(8,128)S(1)}, s32[8,512]{1,0:T(8,128)S(1)}, u32[]{:S(2)}, u32[]{:S(2)}) collective-permute-start(s32[8,512]{1,0:T(8,128)S(1)} %get-tuple-element.111), channel_id=1, source_target_pairs={{8,0},{12,4},{16,8},{20,12},{24,16},{28,20},{9,1},{13,5},{17,9},{2... | collective-permute-start | bytes 49160 | tf_op jit(solution)/shard_map/ppermute | solution.py:34
  20.1 61.1 %collective-permute-start.6 = (bf16[512,1024]{1,0:T(8,128)(2,1)S(1)}, bf16[512,1024]{1,0:T(8,128)(2,1)S(1)}, u32[]{:S(2)}, u32[]{:S(2)}) collective-permute-start(bf16[512,1024]{1,0:T(8,128)(2,1)S(1)} %copy-done), channel_id=1, source_target_pairs={{8,0},{12,4},{16,8},{20,12},{24,16},{28,20},{9,1},{13,5},{17,9},{2... | collective-permute-start | bytes 3145736 | tf_op jit(solution)/shard_map/ppermute | solution.py:34
  21.4 48.5 %copy-start.5 = (bf16[528,512]{1,0:T(8,128)(2,1)}, bf16[528,512]{1,0:T(8,128)(2,1)S(1)}, u32[]{:S(2)}) copy-start(bf16[528,512]{1,0:T(8,128)(2,1)S(1)} %collective-permute-done.two.refs_4_) | copy-start | bytes 1622020
  21.4 21.1 %collective-permute-start.8 = (bf16[528,512]{1,0:T(8,128)(2,1)}, bf16[528,512]{1,0:T(8,128)(2,1)S(1)}, u32[]{:S(2)}, u32[]{:S(2)}) collective-permute-start(bf16[528,512]{1,0:T(8,128)(2,1)} %get-tuple-element.78), channel_id=1, source_target_pairs={{0,8},{4,12},{8,16},{12,20},{16,24},{20,28},{1,9},{5,13},{9,17},{1... | collective-permute-start | bytes 1622024 | tf_op jit(solution)/shard_map/ppermute | solution.py:34
  25.4 0.8 copy-start.7
  26.2 27.8 %collective-permute-start.11 = (bf16[528,512]{1,0:T(8,128)(2,1)}, bf16[528,512]{1,0:T(8,128)(2,1)S(1)}, u32[]{:S(2)}, u32[]{:S(2)}) collective-permute-start(bf16[528,512]{1,0:T(8,128)(2,1)} %get-tuple-element.85), channel_id=1, source_target_pairs={{0,8},{4,12},{8,16},{12,20},{16,24},{20,28},{1,9},{5,13},{9,17},{1... | collective-permute-start | bytes 1622024 | tf_op jit(solution)/shard_map/ppermute | solution.py:34
  30.8 25.5 %collective-permute-start.2 = (bf16[528,512]{1,0:T(8,128)(2,1)S(1)}, bf16[528,512]{1,0:T(8,128)(2,1)S(1)}, u32[]{:S(2)}, u32[]{:S(2)}) collective-permute-start(bf16[528,512]{1,0:T(8,128)(2,1)S(1)} %collective-permute-done.two.refs_4_), channel_id=1, source_target_pairs={{4,0},{12,8},{20,16},{28,24},{5,1},{13,9},{21,17},{29,25},{6,2},{1... | collective-permute-start | bytes 1622024 | tf_op jit(solution)/shard_map/ppermute | solution.py:44
  34.6 0.8 copy-start.12
  35.4 22.2 %collective-permute-start.5 = (bf16[528,512]{1,0:T(8,128)(2,1)S(1)}, bf16[528,512]{1,0:T(8,128)(2,1)S(1)}, u32[]{:S(2)}, u32[]{:S(2)}) collective-permute-start(bf16[528,512]{1,0:T(8,128)(2,1)S(1)} %collective-permute-done.3.two.refs_7_), channel_id=1, source_target_pairs={{4,0},{12,8},{20,16},{28,24},{5,1},{13,9},{21,17},{29,25},{6,2},{1... | collective-permute-start | bytes 1622024 | tf_op jit(solution)/shard_map/ppermute | solution.py:44
  36.7 0.8 copy-start.10
  42.5 48.3 %collective-permute-start.9 = (bf16[528,512]{1,0:T(8,128)(2,1)}, bf16[528,512]{1,0:T(8,128)(2,1)S(1)}, u32[]{:S(2)}, u32[]{:S(2)}) collective-permute-start(bf16[528,512]{1,0:T(8,128)(2,1)} %get-tuple-element.78), channel_id=1, source_target_pairs={{0,4},{8,12},{16,20},{24,28},{1,5},{9,13},{17,21},{25,29},{2,6},{1... | collective-permute-start | bytes 1622024 | tf_op jit(solution)/shard_map/ppermute | solution.py:39
  54.1 36.7 %collective-permute-start.10 = (bf16[528,512]{1,0:T(8,128)(2,1)S(1)}, bf16[528,512]{1,0:T(8,128)(2,1)S(1)}, u32[]{:S(2)}, u32[]{:S(2)}) collective-permute-start(bf16[528,512]{1,0:T(8,128)(2,1)S(1)} %collective-permute-done.8.refs_4_.two), channel_id=1, source_target_pairs={{4,0},{12,8},{20,16},{28,24},{5,1},{13,9},{21,17},{29,25},{6,2},{1... | collective-permute-start | bytes 1622024 | tf_op jit(solution)/shard_map/ppermute | solution.py:44
  56.3 9.6 %copy-start.14 = (bf16[528,512]{1,0:T(8,128)(2,1)}, bf16[528,512]{1,0:T(8,128)(2,1)S(1)}, u32[]{:S(2)}) copy-start(bf16[528,512]{1,0:T(8,128)(2,1)S(1)} %collective-permute-done.2.odd.refs_6_) | copy-start | bytes 1622020
  56.3 44.1 %collective-permute-start.12 = (bf16[528,512]{1,0:T(8,128)(2,1)}, bf16[528,512]{1,0:T(8,128)(2,1)S(1)}, u32[]{:S(2)}, u32[]{:S(2)}) collective-permute-start(bf16[528,512]{1,0:T(8,128)(2,1)} %get-tuple-element.85), channel_id=1, source_target_pairs={{0,4},{8,12},{16,20},{24,28},{1,5},{9,13},{17,21},{25,29},{2,6},{1... | collective-permute-start | bytes 1622024 | tf_op jit(solution)/shard_map/ppermute | solution.py:39
  57.6 8.3 %copy-start.17 = (bf16[528,512]{1,0:T(8,128)(2,1)}, bf16[528,512]{1,0:T(8,128)(2,1)S(1)}, u32[]{:S(2)}) copy-start(bf16[528,512]{1,0:T(8,128)(2,1)S(1)} %collective-permute-done.5.odd.refs_9_) | copy-start | bytes 1622020
  57.6 42.7 %collective-permute-start.13 = (bf16[528,512]{1,0:T(8,128)(2,1)S(1)}, bf16[528,512]{1,0:T(8,128)(2,1)S(1)}, u32[]{:S(2)}, u32[]{:S(2)}) collective-permute-start(bf16[528,512]{1,0:T(8,128)(2,1)S(1)} %collective-permute-done.11.refs_4_.two), channel_id=1, source_target_pairs={{4,0},{12,8},{20,16},{28,24},{5,1},{13,9},{21,17},{29,25},{6,2},{1... | collective-permute-start | bytes 1622024 | tf_op jit(solution)/shard_map/ppermute | solution.py:44
  65.8 4.0 %copy-start.8 = (bf16[528,512]{1,0:T(8,128)(2,1)S(1)}, bf16[528,512]{1,0:T(8,128)(2,1)}, u32[]{:S(2)}) copy-start(bf16[528,512]{1,0:T(8,128)(2,1)} %copy-done.7) | copy-start | bytes 1622020
  65.9 4.0 %copy-start.15 = (bf16[528,512]{1,0:T(8,128)(2,1)S(1)}, bf16[528,512]{1,0:T(8,128)(2,1)}, u32[]{:S(2)}) copy-start(bf16[528,512]{1,0:T(8,128)(2,1)} %copy-done.14) | copy-start | bytes 1622020
  69.9 5.1 %copy-start.11 = (bf16[528,512]{1,0:T(8,128)(2,1)S(1)}, bf16[528,512]{1,0:T(8,128)(2,1)}, u32[]{:S(2)}) copy-start(bf16[528,512]{1,0:T(8,128)(2,1)} %copy-done.10) | copy-start | bytes 1622020
  69.9 5.1 %copy-start.13 = (bf16[528,512]{1,0:T(8,128)(2,1)S(1)}, bf16[528,512]{1,0:T(8,128)(2,1)}, u32[]{:S(2)}) copy-start(bf16[528,512]{1,0:T(8,128)(2,1)} %copy-done.12) | copy-start | bytes 1622020
  73.4 0.8 copy-start.20
  74.2 0.8 copy-start.22
  75.0 1.0 copy-start.18
  76.0 5.2 %copy-start.6 = (bf16[528,512]{1,0:T(8,128)(2,1)S(1)}, bf16[528,512]{1,0:T(8,128)(2,1)}, u32[]{:S(2)}) copy-start(bf16[528,512]{1,0:T(8,128)(2,1)} %copy-done.5) | copy-start | bytes 1622020
  76.0 5.2 %copy-start.9 = (bf16[528,512]{1,0:T(8,128)(2,1)S(1)}, bf16[528,512]{1,0:T(8,128)(2,1)}, u32[]{:S(2)}) copy-start(bf16[528,512]{1,0:T(8,128)(2,1)} %copy-done.7) | copy-start | bytes 1622020
  76.0 5.2 %copy-start.16 = (bf16[528,512]{1,0:T(8,128)(2,1)S(1)}, bf16[528,512]{1,0:T(8,128)(2,1)}, u32[]{:S(2)}) copy-start(bf16[528,512]{1,0:T(8,128)(2,1)} %copy-done.14) | copy-start | bytes 1622020
  76.0 5.2 %copy-start.19 = (bf16[528,512]{1,0:T(8,128)(2,1)S(1)}, bf16[528,512]{1,0:T(8,128)(2,1)}, u32[]{:S(2)}) copy-start(bf16[528,512]{1,0:T(8,128)(2,1)} %copy-done.17) | copy-start | bytes 1622020
  79.6 0.8 copy-start.24
  80.4 0.8 copy-start.26
  86.5 23.6 %collective-permute-start.14 = (bf16[576,640]{1,0:T(8,128)(2,1)S(1)}, bf16[576,640]{1,0:T(8,128)(2,1)S(1)}, u32[]{:S(2)}, u32[]{:S(2)}) collective-permute-start(bf16[576,640]{1,0:T(8,128)(2,1)S(1)} %get-tuple-element.88), channel_id=1, source_target_pairs={{0,8},{4,12},{8,16},{12,20},{16,24},{20,28},{1,9},{5,13},{9,17},{1... | collective-permute-start | bytes 2211848 | tf_op jit(solution)/shard_map/ppermute | solution.py:34
  93.8 18.0 %collective-permute-start.15 = (bf16[288,640]{1,0:T(8,128)(2,1)S(1)}, bf16[288,640]{1,0:T(8,128)(2,1)S(1)}, u32[]{:S(2)}, u32[]{:S(2)}) collective-permute-start(bf16[288,640]{1,0:T(8,128)(2,1)S(1)} %get-tuple-element.97), channel_id=1, source_target_pairs={{0,8},{4,12},{8,16},{12,20},{16,24},{20,28},{1,9},{5,13},{9,17},{1... | collective-permute-start | bytes 1105928 | tf_op jit(solution)/shard_map/ppermute | solution.py:34
  103.4 16.3 %collective-permute-start.16 = (bf16[288,640]{1,0:T(8,128)(2,1)S(1)}, bf16[288,640]{1,0:T(8,128)(2,1)S(1)}, u32[]{:S(2)}, u32[]{:S(2)}) collective-permute-start(bf16[288,640]{1,0:T(8,128)(2,1)S(1)} %get-tuple-element.103), channel_id=1, source_target_pairs={{0,8},{4,12},{8,16},{12,20},{16,24},{20,28},{1,9},{5,13},{9,17},{1... | collective-permute-start | bytes 1105928 | tf_op jit(solution)/shard_map/ppermute | solution.py:34
  106.6 3.6 %copy-start.21 = (f32[256,512]{1,0:T(8,128)S(1)}, f32[256,512]{1,0:T(8,128)}, u32[]{:S(2)}) copy-start(f32[256,512]{1,0:T(8,128)} %copy-done.20) | copy-start | bytes 1572868
  106.6 3.6 %copy-start.23 = (f32[256,512]{1,0:T(8,128)S(1)}, f32[256,512]{1,0:T(8,128)}, u32[]{:S(2)}) copy-start(f32[256,512]{1,0:T(8,128)} %copy-done.22) | copy-start | bytes 1572868
  106.6 3.6 %copy-start.25 = (f32[256,512]{1,0:T(8,128)S(1)}, f32[256,512]{1,0:T(8,128)}, u32[]{:S(2)}) copy-start(f32[256,512]{1,0:T(8,128)} %copy-done.24) | copy-start | bytes 1572868
  106.6 3.6 %copy-start.27 = (f32[256,512]{1,0:T(8,128)S(1)}, f32[256,512]{1,0:T(8,128)}, u32[]{:S(2)}) copy-start(f32[256,512]{1,0:T(8,128)} %copy-done.26) | copy-start | bytes 1572868
  128.8 0.7 copy-start.29

commit v2 on v1

v2 whole, which is shorter than its diff:
```python
import math
from functools import partial

import jax
import jax.numpy as jnp
from jax import lax
from jax.experimental import pallas as pl
from jax.experimental.pallas import tpu as pltpu
from jax.sharding import PartitionSpec as P

D = 4096
BLK = 128
REACH = 4
EPSILON = 1e-06
NEG = -1e30
FAR_OFF = 1 << 30
LOG2E = math.log2(math.e)

NT = (((1,), (1,)), ((), ()))
TN = (((0,), (0,)), ((), ()))
NN = (((1,), (0,)), ((), ()))


def dot(a, b, dims):
    return lax.dot_general(a, b, dims, preferred_element_type=jnp.float32)


def params(mib=24):
    return pltpu.CompilerParams(vmem_limit_bytes=mib * 1024 * 1024)


def shifted(x, by):
    n = lax.axis_size("ctx")
    return lax.ppermute(x, "ctx", [(i, i + by) for i in range(n) if 0 <= i + by < n])


def even_to_odd(x):
    n = lax.axis_size("ctx")
    return lax.ppermute(x, "ctx", [(i, i + 1) for i in range(0, n - 1, 2)])


def odd_to_even(x):
    n = lax.axis_size("ctx")
    return lax.ppermute(x, "ctx", [(i, i - 1) for i in range(1, n, 2)])


def split3(x):
    hi = x.astype(jnp.bfloat16)
    rest = x - hi.astype(jnp.float32)
    mid = rest.astype(jnp.bfloat16)
    low = (rest - mid.astype(jnp.float32)).astype(jnp.bfloat16)
    return hi.astype(jnp.float32), mid.astype(jnp.float32), low.astype(jnp.float32)


def split2(x):
    return split3(x)[:2]


def join2(rows, first):
    return rows[first : first + 1] + rows[first + 1 : first + 2]


def join3(rows, first):
    return rows[first : first + 1] + rows[first + 1 : first + 2] + rows[first + 2 : first + 3]


def stack_rows(rows, count, length):
    spot = lax.broadcasted_iota(jnp.int32, (count, length), 0)
    out = jnp.zeros((count, length), jnp.float32)
    for i, r in enumerate(rows):
        out = jnp.where(spot == i, r, out)
    return out


def softmax_of(parts, scale2):
    top = parts[0]
    for p in parts[1:]:
        top = jnp.maximum(top, p)
    top = jnp.max(top, axis=0, keepdims=True) * scale2
    weights = [jnp.exp2(p * scale2 - top) for p in parts]
    total = weights[0]
    for w in weights[1:]:
        total = total + w
    total = jnp.sum(total, axis=0, keepdims=True)
    return top, total, [w.astype(jnp.bfloat16) for w in weights]


def pick(rows, index):
    spot = lax.broadcasted_iota(jnp.int32, rows.shape, 0)
    return jnp.sum(jnp.where(spot == index, rows, 0.0), axis=0, keepdims=True)


def fetch(pay_ref, k_hbm, v_hbm, source, half, sems, first, at=0):
    length = k_hbm.shape[0]
    copies = []
    for i, hbm in enumerate((k_hbm, v_hbm)):
        lo = at + i * half
        target = pay_ref.at[0:length, lo : lo + half]
        copies.append(pltpu.make_async_copy(hbm.at[:, source : source + half], target, sems.at[first + i]))
        copies[-1].start()
    return copies


def fill(pay_ref, dec, length, dec_row):
    pay_ref[dec_row : dec_row + 16, 0:length] = dec
    if pay_ref.shape[1] > length:
        pay_ref[dec_row : dec_row + 16, length:] = jnp.zeros((16, pay_ref.shape[1] - length), jnp.bfloat16)


def prep_kernel(
    divisor, sizes, docs_ref, mask_ref, ld_ref, k_ref, v_ref,
    thr_ref, start_ref, ahead_ref, entry_ref, keep_ref, cum_ref, cumt_ref, coef_ref, dec_ref, pay_ref, token_ref, sems,
):
    heads, length = ld_ref.shape
    copies = fetch(pay_ref, k_ref, v_ref, 0, sizes[0] * 128, sems, 0)
    tiles = length // BLK
    begin = lax.axis_index("ctx").astype(jnp.int32) * length
    f32, bf16 = jnp.float32, jnp.bfloat16
    parts = jnp.concatenate(split3(ld_ref[...]), axis=0).astype(bf16)
    u = lax.broadcasted_iota(jnp.int32, (length, length), 0)
    t = lax.broadcasted_iota(jnp.int32, (length, length), 1)
    ones = jnp.where(u <= t, 1.0, 0.0).astype(bf16)
    sums = dot(parts, ones, NN)
    cum = sums[:heads] + sums[heads : 2 * heads] + sums[2 * heads :]
    cum_ref[...] = cum
    cumt_ref[...] = jnp.concatenate([cum, jnp.zeros((BLK - heads, length), f32)], axis=0).T
    pos = begin + lax.broadcasted_iota(jnp.int32, (8, length), 1)
    start = jnp.zeros((8, length), jnp.int32)
    ahead = jnp.zeros((8, length), jnp.int32)
    entry = jnp.zeros((8, length), jnp.int32)
    end = jnp.zeros((1, 1), jnp.int32)
    for d in range(docs_ref.shape[1]):
        end = end + docs_ref[:, d : d + 1]
        start = jnp.where(pos >= end, end, start)
        ahead = jnp.where(pos + 2 * length >= end, end, ahead)
        entry = jnp.where(begin - 1 >= end, end, entry)
    start = start - begin
    start_ref[...] = start
    ahead_ref[...] = ahead - (begin + 2 * length)
    entry_ref[...] = entry - begin
    coef_ref[...] = jnp.exp(cum) * jnp.where(start[:1] < 0, 1.0 / divisor, 0.0)
    reach = mask_ref.shape[1]
    tile_row = lax.broadcasted_iota(jnp.int32, (reach, length), 0)
    tile_of = lax.broadcasted_iota(jnp.int32, (reach, length), 1) // BLK
    spread = (lax.broadcasted_iota(jnp.int32, (tiles, length), 1) // BLK == lax.broadcasted_iota(jnp.int32, (tiles, length), 0))
    picked = dot(mask_ref[...].astype(f32).astype(bf16), jnp.where(spread, 1.0, 0.0).astype(bf16), TN)
    keep = (picked > 0.5) | (tile_row == REACH * tiles + tile_of)
    base = (tile_row - REACH * tiles) * BLK
    thr_ref[...] = jnp.where(keep, start[:1] - base, FAR_OFF)
    kept = jnp.where(picked > 0.5, 1.0, 0.0)
    keep_ref[...] = kept[0:16].astype(bf16)
    last = cum[:, length - 1 :]
    first = 0
    for c, n in enumerate(sizes):
        rows = []
        for h in range(first, first + n):
            rows += list(split2(last[h : h + 1] - cum[h : h + 1]))
        for h in range(first, first + n):
            rows += list(split2(last[h : h + 1] + jnp.zeros((1, length), f32)))
        dec = stack_rows(rows, 16, length).astype(bf16)
        dec_ref[c * 16 : (c + 1) * 16, :] = dec
        if c == 0:
            fill(pay_ref, dec, length, length)
        first += n
    token_ref[...] = jnp.zeros_like(token_ref)
    for copy in copies:
        copy.wait()


def pack_kernel(sizes, width1, token_in, q_ref, keep_ref, k_ref, v_ref, dec_ref, one_ref, both_ref, qpay_ref, token_ref, sems):
    length, features = q_ref.shape
    first, second = sizes[0] * 128, (sizes[0] + sizes[1]) * 128
    copies = fetch(one_ref, k_ref, v_ref, first, sizes[1] * 128, sems, 0)
    copies.append(pltpu.make_async_copy(q_ref, qpay_ref.at[0:length, :], sems.at[6]))
    copies[-1].start()
    copies += fetch(both_ref, k_ref, v_ref, first, sizes[1] * 128, sems, 2)
    copies += fetch(both_ref, k_ref, v_ref, second, sizes[2] * 128, sems, 4, width1)
    fill(one_ref, dec_ref[16:32, :], length, length)
    fill(both_ref, dec_ref[16:32, :], length, length)
    fill(both_ref, dec_ref[32:48, :], length, length + 16)
    qpay_ref[length:, 0:length] = keep_ref[...]
    if features > length:
        qpay_ref[length:, length:] = jnp.zeros((16, features - length), jnp.bfloat16)
    token_ref[...] = jnp.zeros_like(token_ref)
    for copy in copies:
        copy.wait()


def pack_last_kernel(sizes, token_in, k_ref, v_ref, dec_ref, pay_ref, token_ref, sems):
    length = k_ref.shape[0]
    copies = fetch(pay_ref, k_ref, v_ref, (sizes[0] + sizes[1]) * 128, sizes[2] * 128, sems, 0)
    fill(pay_ref, dec_ref[...], length, length)
    token_ref[...] = jnp.zeros_like(token_ref)
    for copy in copies:
        copy.wait()


def gate_kernel(token_in, x_in, x_out):
    pass


def own_kernel(scale2, divisor, n, base, q_hbm, k_hbm, v_hbm, thr_ref, start_ref, cum_ref, cumt_ref, o_ref, top_ref, tot_ref, lin_ref, token_ref, held, sems):
    length = q_hbm.shape[0]
    tiles = length // BLK
    own = REACH * tiles
    copies = []
    for i in range(n):
        h = base + i
        for part, hbm in enumerate((q_hbm, k_hbm, v_hbm)):
            source = hbm.at[:, h * 128 : (h + 1) * 128]
            copies.append(pltpu.make_async_copy(source, held.at[3 * i + part], sems.at[3 * i + part]))
            copies[-1].start()
    row = lax.broadcasted_iota(jnp.int32, (BLK, length), 0)
    col = lax.broadcasted_iota(jnp.int32, (BLK, length), 1)
    for i in range(n):
        h = base + i
        for copy in copies[3 * i : 3 * i + 3]:
            copy.wait()
        q, k, v = held[3 * i], held[3 * i + 1], held[3 * i + 2]
        scores = dot(k, q, NT)
        cum_row = cum_ref[h : h + 1, :]
        soft, mix = [], []
        for j in range(tiles):
            s = scores[j * BLK : (j + 1) * BLK]
            causal = row <= col - j * BLK
            soft.append(jnp.where(causal & (row >= thr_ref[own + j : own + j + 1, :]), s, NEG))
            gap = cum_row - cumt_ref[j * BLK : (j + 1) * BLK, h : h + 1]
            ok = causal & (row >= start_ref[0:1, :] - j * BLK)
            decay = jnp.exp(jnp.where(ok, gap, NEG))
            mix.append((s * decay * (1.0 / divisor)).astype(jnp.bfloat16))
        top, total, weights = softmax_of(soft, scale2)
        rows = slice(i * 128, (i + 1) * 128)
        o_ref[rows, :] = dot(v, jnp.concatenate(weights, axis=0), TN)
        lin_ref[rows, :] = dot(v, jnp.concatenate(mix, axis=0), TN)
        top_ref[i : i + 1, :] = top
        tot_ref[i : i + 1, :] = total
    token_ref[...] = jnp.zeros_like(token_ref)


class Pieces:
    def __init__(self, n, two, even, odd, entry, even_at, even_dec):
        self.n, self.two, self.even, self.odd, self.even_at = n, two, even, odd, even_at
        length = self.length = odd.shape[0] - 16
        rows2 = two[length:, 0:length].astype(jnp.float32)
        rows1 = (even[even_dec : even_dec + 16, 0:length] + odd[length:, 0:length]).astype(jnp.float32)
        self.tot1 = [join2(rows1, 2 * n + 2 * i) for i in range(n)]
        self.tot2 = [join2(rows2, 2 * n + 2 * i) for i in range(n)]
        after1 = [join2(rows1, 2 * i) for i in range(n)]
        after2 = [join2(rows2, 2 * i) + self.tot1[i] for i in range(n)]
        col = lax.broadcasted_iota(jnp.int32, (1, length), 1)
        w1 = [jnp.where(col - length >= entry, jnp.exp(x), 0.0) for x in after1]
        w2 = [jnp.where(col - 2 * length >= entry, jnp.exp(x), 0.0) for x in after2]
        self.weight = stack_rows(w1 + w2, BLK, length).T

    def part(self, index):
        cols = slice(index * 128, (index + 1) * 128)
        at = slice(self.even_at + index * 128, self.even_at + (index + 1) * 128)
        return self.two[0 : self.length, cols], self.even[0 : self.length, at] + self.odd[0 : self.length, cols]

    def attend(self, i, q, thr, scale2):
        tiles = self.length // BLK
        k2, k1 = self.part(i)
        v2, v1 = self.part(self.n + i)
        row = lax.broadcasted_iota(jnp.int32, (BLK, q.shape[0]), 0)
        parts = []
        for first, keys in ((0, k2), (tiles, k1)):
            scores = dot(keys, q, NT)
            for j in range(tiles):
                ok = row >= thr[first + j : first + j + 1]
                parts.append(jnp.where(ok, scores[j * BLK : (j + 1) * BLK], NEG))
        top, total, weights = softmax_of(parts, scale2)
        o = dot(v2, jnp.concatenate(weights[:tiles], axis=0), TN) + dot(v1, jnp.concatenate(weights[tiles:], axis=0), TN)
        n = self.n
        kw1 = (k1.astype(jnp.float32) * self.weight[:, i : i + 1]).astype(jnp.bfloat16)
        kw2 = (k2.astype(jnp.float32) * self.weight[:, n + i : n + i + 1]).astype(jnp.bfloat16)
        state = dot(v2, kw2, TN) + dot(v1, kw1, TN)
        return top, total, o, state.astype(jnp.bfloat16)


def far_kernel(scale2, n, even_at, even_dec, token_in, entry_ref, q_ref, keep_ref, ahead_ref, two, even, odd, out_ref, token_ref):
    p = Pieces(n, two, even, odd, entry_ref[0:1, :], even_at, even_dec)
    length = p.length
    keep = keep_ref[...].astype(jnp.float32)
    tiles = length // BLK
    thr = []
    for j in range(2 * tiles):
        base = (j - REACH * tiles) * BLK
        thr.append(jnp.where(keep[j : j + 1] > 0.5, ahead_ref[0:1, :] - base, FAR_OFF))
    thr = jnp.concatenate(thr, axis=0)
    for i in range(n):
        top, total, o, state = p.attend(i, q_ref[0:length, i * 128 : (i + 1) * 128], thr, scale2)
        r = i * 144
        out_ref[r : r + 128, 0:length] = (o * (1.0 / total)).astype(jnp.bfloat16)
        out_ref[r : r + 128, length:] = state
        lse = top + jnp.log(total) * LOG2E
        stats = stack_rows(list(split3(lse)) + [jnp.ones_like(lse)], 16, length)
        out_ref[r + 128 : r + 144, 0:length] = stats.astype(jnp.bfloat16)
        out_ref[r + 128 : r + 144, length:] = jnp.zeros((16, 128), jnp.bfloat16)
    token_ref[...] = jnp.zeros_like(token_ref)


def near_kernel(
    scale2, n, first, even_at, even_dec, token_in, entry_ref, q_ref, thr_ref, coef_ref, two, even, odd, od_ref, topd_ref, totd_ref, lind_ref,
    x_ref, on_ref, st_ref, token_ref,
):
    entry = entry_ref[0:1, :]
    p = Pieces(n, two, even, odd, entry, even_at, even_dec)
    length = p.length
    lses, coefs = [], []
    thr = thr_ref[...]
    for i in range(n):
        q = q_ref[:, i * 128 : (i + 1) * 128]
        rows = slice(i * 128, (i + 1) * 128)
        top, total, o, state = p.attend(i, q, thr, scale2)
        top_d = topd_ref[i : i + 1, :]
        new_top = jnp.maximum(top, top_d)
        a, b = jnp.exp2(top - new_top), jnp.exp2(top_d - new_top)
        total = total * a + totd_ref[i : i + 1, :] * b
        inv = 1.0 / total
        on = o * (a * inv) + od_ref[rows, :] * (b * inv)
        coef = coef_ref[first + i : first + i + 1, :]
        x_ref[rows, :] = lind_ref[rows, :] + dot(state, q, NT) * coef + on
        on_ref[rows, :] = on
        lses.append(new_top + jnp.log(total) * LOG2E)
        through = jnp.where(entry < -2 * length, jnp.exp(p.tot1[i] + p.tot2[i]), 0.0)
        coefs.append(coef * through)
    st_ref[...] = stack_rows(lses + coefs, 8, length)
    token_ref[...] = jnp.zeros_like(token_ref)


def merge_kernel(n, token_in, q_ref, pay_ref, x_ref, on_ref, st_ref, mixed_ref, sq_ref, token_ref):
    squares = None
    length = q_ref.shape[0]
    for i in range(n):
        q = q_ref[:, i * 128 : (i + 1) * 128]
        rows = slice(i * 128, (i + 1) * 128)
        r = i * 144
        stats = pay_ref[r + 128 : r + 144, 0:length].astype(jnp.float32)
        lse_far = join3(stats, 0)
        far = pay_ref[r : r + 128, 0:length].astype(jnp.float32)
        share = 1.0 / (1.0 + jnp.exp2(jnp.minimum(st_ref[i : i + 1, :] - lse_far, 120.0)))
        share = jnp.where((lse_far > 0.5 * NEG) & (stats[3:4] > 0.5), share, 0.0)
        lin = dot(pay_ref[r : r + 128, length:], q, NT) * st_ref[n + i : n + i + 1, :]
        mixed = x_ref[rows, :] + share * (far - on_ref[rows, :]) + lin
        mixed_ref[rows, :] = mixed
        part = jnp.sum(mixed * mixed, axis=0, keepdims=True)
        squares = part if squares is None else squares + part
    sq_ref[...] = squares
    token_ref[...] = jnp.zeros_like(token_ref)


def norm_kernel(parts, *refs):
    mixed_refs, sq_ref, gain_ref, out_ref = refs[:parts], refs[parts], refs[parts + 1], refs[parts + 2]
    inverse = lax.rsqrt(jnp.sum(sq_ref[...], axis=0, keepdims=True) / D + EPSILON)
    col = 0
    for ref in mixed_refs:
        for i in range(ref.shape[0] // 128):
            part = (ref[i * 128 : (i + 1) * 128, :] * inverse).T
            out_ref[:, col : col + 128] = (part * gain_ref[:, col : col + 128]).astype(jnp.bfloat16)
            col += 128


def on_device(query, key, value, log_decay, doc_lengths, tile_mask, gain):
    length, features = query.shape
    heads = log_decay.shape[0]
    hd = features // heads
    tiles = length // BLK
    sizes = [(heads + 2) // 3, (heads + 1) // 3, heads // 3]
    firsts = [sum(sizes[:c]) for c in range(len(sizes))]
    divisor = hd * math.sqrt(length)
    scale2 = LOG2E / math.sqrt(hd)
    f32, bf16 = jnp.float32, jnp.bfloat16
    shape = jax.ShapeDtypeStruct
    loose = pl.BlockSpec(memory_space=pl.ANY)
    hbm = pl.BlockSpec(memory_space=pltpu.HBM)
    dma = pltpu.SemaphoreType.DMA

    def whole(x):
        return pl.BlockSpec(x.shape, lambda *_: (0,) * len(x.shape))

    def cols(c, rows=length):
        return pl.BlockSpec((rows, sizes[c] * hd), lambda *_: (0, firsts[c] // sizes[c]))

    def run(kernel, name, us, specs, args, outs, scratch=()):
        outs = outs + [shape((8, 128), f32)]
        out_specs = [whole(o) for o in outs]
        return pl.pallas_call(
            kernel,
            grid=(1,),
            in_specs=specs,
            out_specs=out_specs,
            out_shape=outs,
            scratch_shapes=scratch,
            compiler_params=params(),
            cost_estimate=pl.CostEstimate(flops=0, bytes_accessed=int(us * 3.69e6), transcendentals=0),
            name=name,
        )(*args)

    def pay_shape(c):
        return shape((length + 16, max(length, 2 * sizes[c] * hd)), bf16)

    docs = doc_lengths[None, :]
    outs = [
        shape(((REACH + 1) * tiles, length), jnp.int32),
        shape((8, length), jnp.int32),
        shape((8, length), jnp.int32),
        shape((8, length), jnp.int32),
        shape((16, length), bf16),
        shape((heads, length), f32),
        shape((length, BLK), f32),
        shape((heads, length), f32),
        shape((16 * len(sizes), length), bf16),
        pay_shape(0),
    ]
    thr, start, ahead, entry, keep, cum, cum_t, coef, dec, pay0, token = run(
        partial(prep_kernel, divisor, sizes),
        "prep",
        2,
        [whole(docs), whole(tile_mask), whole(log_decay), hbm, hbm],
        (docs, tile_mask, log_decay, key, value),
        outs,
        [dma((2,))],
    )
    thr_near = pl.BlockSpec((2 * tiles, length), lambda *_: (1, 0))

    def own(c, token, *after):
        n, first = sizes[c], firsts[c]
        outs = [shape((n * hd, length), f32), shape((n, length), f32), shape((n, length), f32), shape((n * hd, length), f32)]

        def kernel(*refs):
            own_kernel(scale2, divisor, n, first, *refs[len(after) + 1 :])

        *result, token = run(
            kernel,
            "own_piece",
            n * 0.8,
            [loose] * (len(after) + 1) + [hbm] * 3 + [whole(thr), whole(start), whole(cum), whole(cum_t)],
            (*after, token, query, key, value, thr, start, cum, cum_t),
            outs,
            [pltpu.VMEM((3 * n, length, hd), bf16), dma((3 * n,))],
        )
        return result, token

    width1 = pay_shape(1).shape[1]

    def kv(c):
        return two_back[c], from_even[min(c, 1)], from_odd[c]

    def even_place(c):
        return (0, length) if c < 2 else (width1, length + 16)

    def near(c, token):
        n = sizes[c]
        args = (*kv(c), *diag[c])
        x, on, st, token = run(
            partial(near_kernel, scale2, n, firsts[c], *even_place(c)),
            "near_pieces",
            1.8 * n,
            [loose, whole(entry), cols(c), thr_near, whole(coef)] + [whole(a) for a in args],
            (token, entry, query, thr, coef, *args),
            [shape((n * hd, length), f32), shape((n * hd, length), f32), shape((8, length), f32)],
        )
        return (x, on, st), token

    def far(c, token):
        n = sizes[c]
        kept = pl.BlockSpec((16, length), lambda *_: (length // 16, 0))
        pay, token = run(
            partial(far_kernel, scale2, n, *even_place(c)),
            "far_pieces",
            1.5 * n,
            [loose, whole(entry), cols(c), kept, whole(ahead)] + [whole(a) for a in kv(c)],
            (token, entry, q_far, q_far, ahead, *kv(c)),
            [shape((n * (hd + 16), length + hd), bf16)],
        )
        return shifted(pay, 2), token

    def merge(c, token):
        n = sizes[c]
        args = (pays[c], *parts[c])
        return run(
            partial(merge_kernel, n),
            "merge",
            0.5 * n,
            [loose, cols(c)] + [whole(a) for a in args],
            (token, query, *args),
            [shape((n * hd, length), f32), shape((1, length), f32)],
        )

    def gate(x, token):
        return pl.pallas_call(
            gate_kernel,
            in_specs=[loose, loose],
            out_specs=loose,
            out_shape=shape(x.shape, x.dtype),
            input_output_aliases={1: 0},
            compiler_params=params(1),
            name="gate",
        )(token, x)

    chunks = range(len(sizes))
    diag, parts, pays = [None] * 3, [None] * 3, [None] * 3
    two_back, from_even, from_odd = [None] * 3, [None] * 2, [None] * 3
    two_back[0] = shifted(pay0, 2)
    from_even[0] = even_to_odd(pay0)
    diag[0], token = own(0, token)
    one, both, q_pay, token = run(
        partial(pack_kernel, sizes, width1),
        "pack",
        3,
        [loose, hbm, whole(keep), hbm, hbm, whole(dec)],
        (token, query, keep, key, value, dec),
        [pay_shape(1), shape((length + 32, width1 + pay_shape(2).shape[1]), bf16), shape((length + 16, features), bf16)],
        [dma((7,))],
    )
    two_back[1] = shifted(one, 2)
    from_odd[0] = odd_to_even(two_back[0])
    q_far = shifted(q_pay, -2)
    diag[1], token = own(1, token, two_back[0])
    dec_rows = pl.BlockSpec((16, length), lambda *_: (2, 0))
    pay, token = run(
        partial(pack_last_kernel, sizes), "pack", 1, [loose, hbm, hbm, dec_rows], (token, key, value, dec), [pay_shape(2)], [dma((2,))]
    )
    two_back[2] = shifted(pay, 2)
    from_even[1] = even_to_odd(both)
    from_odd[1] = odd_to_even(two_back[1])
    diag[2], token = own(2, token, two_back[1])
    pays[0], token = far(0, token)
    two_back[2] = gate(two_back[2], token)
    from_odd[2] = odd_to_even(two_back[2])
    parts[0], token = near(0, token)
    pays[1], token = far(1, token)
    pays[2], token = far(2, token)
    parts[1], token = near(1, token)
    parts[2], token = near(2, token)
    mixed, total = [], None
    for c in chunks:
        m, s, token = merge(c, token)
        mixed.append(m)
        total = s if total is None else total + s
    ranks = lax.axis_size("head")
    everyone = lax.all_gather(total.reshape(length // 128, 128), "head").reshape(ranks, length)
    gain = gain[None, :]
    return pl.pallas_call(
        partial(norm_kernel, len(mixed)),
        grid=(1,),
        in_specs=[whole(m) for m in mixed] + [whole(everyone), whole(gain)],
        out_specs=whole(query),
        out_shape=shape((length, features), bf16),
        compiler_params=params(),
        name="normalize",
    )(*mixed, everyone, gain)


def solution(mesh):
    placed = (
        P("ctx", "head"),
        P("ctx", "head"),
        P("ctx", "head"),
        P("head", "ctx"),
        P(),
        P("ctx", None),
        P("head"),
    )
    return jax.shard_map(on_device, mesh=mesh, in_specs=placed, out_specs=P("ctx", "head"), check_vma=False)
```

time: 133 us -> 104 us (0.78)
  starting transfers between devices: 42.4 us -> 32.2 us
  waiting for transfers between devices: 29.9 us -> 23.4 us
  Pallas kernels: 38.7 us -> 33 us
  local copies, waits for them, and re-layouts: 11.3 us -> 5.83 us
    ppermute x9 -> x7, waiting for transfers between devices: 28.7 us -> 21.4 us  [shifted(): lax.ppermute(x, 'ctx', [(i, i + by) for i in range(n) if 0 <= i + by < n])]
    pallas_call x15 -> x17, Pallas kernels: 38.7 us -> 33 us  [the longest x15 31.4 us: run(): pl.pallas_call(kernel, grid=(1,), in_specs=specs, out_specs=out_specs, ou...]
    unnamed x65 -> x21, local copies, waits for them, and re-layouts: 11.3 us -> 5.83 us
    ppermute x9 -> x7, starting transfers between devices: 26.8 us -> 22.9 us  [shifted(): lax.ppermute(x, 'ctx', [(i, i + by) for i in range(n) if 0 <= i + by < n])]
    ppermute x4 -> x3, starting transfers between devices: 10.4 us -> 6.77 us  [odd_to_even(): return lax.ppermute(x, 'ctx', [(i, i - 1) for i in range(1, n, 2)])]
    ppermute x4 -> x2, starting transfers between devices: 5.16 us -> 2.58 us  [even_to_odd(): return lax.ppermute(x, 'ctx', [(i, i + 1) for i in range(0, n - 1, 2)])]
    ppermute x4 -> x3, waiting for transfers between devices: 0.01 us -> 1.95 us  [odd_to_even(): return lax.ppermute(x, 'ctx', [(i, i - 1) for i in range(1, n, 2)])]
  transfers between devices with their start and end apart: 17 -> 12, of which waited for: 7 -> 5; matrix products, arithmetic and copies ran while one was open for 0% -> 0% of each run, Pallas kernels for 27% -> 29%
where the time goes in v2:
time: 104 us; the launch traced here: 103 us
  Pallas kernels  33 us (32%)
  starting transfers between devices  32.2 us (31%)
  waiting for transfers between devices  23.4 us (22%)
  blocking collectives  8.09 us (8%)
  local copies, waits for them, and re-layouts  5.83 us (6%)
    pallas_call x15, Pallas kernels, run(): pl.pallas_call(kernel, grid=(1,), in_specs=specs, out_specs=out_specs, ou...  31.4 us
    ppermute x7, starting transfers between devices, shifted(): lax.ppermute(x, 'ctx', [(i, i + by) for i in range(n) if 0 <= i + by < n])  22.9 us
    ppermute x7, waiting for transfers between devices, shifted(): lax.ppermute(x, 'ctx', [(i, i + by) for i in range(n) if 0 <= i + by < n])  21.4 us
    all_gather x1, blocking collectives, on_device(): lax.all_gather(total.reshape(length // 128, 128), 'head')  8.09 us
    ppermute x3, starting transfers between devices, odd_to_even(): return lax.ppermute(x, 'ctx', [(i, i - 1) for i in range(1, n, 2)])  6.77 us
    unnamed x21, local copies, waits for them, and re-layouts  5.83 us
    ppermute x2, starting transfers between devices, even_to_odd(): return lax.ppermute(x, 'ctx', [(i, i + 1) for i in range(0, n - 1, 2)])  2.58 us
  transfers between devices with their start and end apart: 12, of which 5 were waited for; matrix products, arithmetic and copies ran while one was open for 0% of the time, Pallas kernels for 29%

profile of v2, /device:TPU:3, one launch (start us, length us, event | category | flops | bytes accessed | tf_op | source)
XLA Modules:
  0.0 102.8 jit_solution(11711050502557414755)
XLA Ops:
  0.0 0.0 copy-start
  0.0 0.0 copy-start.1
  0.0 1.3 %copy-done.1 = bf16[512,1024]{1,0:T(8,128)(2,1)S(1)} copy-done((bf16[512,1024]{1,0:T(8,128)(2,1)S(1)}, bf16[512,1024]{1,0:T(8,128)(2,1)}, u32[]{:S(2)}) %copy-start.1) | copy-done | bytes 1048600
  1.3 0.0 copy-start.3
  1.3 1.2 %copy-done.3 = bf16[512,1024]{1,0:T(8,128)(2,1)S(1)} copy-done((bf16[512,1024]{1,0:T(8,128)(2,1)S(1)}, bf16[512,1024]{1,0:T(8,128)(2,1)}, u32[]{:S(2)}) %copy-start.3) | copy-done | bytes 1048600
  2.5 0.0 copy-start.6
  2.5 0.7 copy-done.6
  3.3 0.0 copy-start.8
  3.3 0.7 copy-done.8
  3.9 0.0 copy-start.9
  3.9 0.7 copy-done.9
  4.6 0.0 copy-start.2
  4.6 0.5 prep.1
  5.1 3.3 %collective-permute-start.1 = (bf16[528,768]{1,0:T(8,128)(2,1)S(1)}, bf16[528,768]{1,0:T(8,128)(2,1)S(1)}, u32[]{:S(2)}, u32[]{:S(2)}) collective-permute-start(bf16[528,768]{1,0:T(8,128)(2,1)S(1)} %get-tuple-element.72), channel_id=1, source_target_pairs={{0,8},{4,12},{8,16},{12,20},{16,24},{20,28},{1,9},{5,13},{9,17},{1... | collective-permute-start | bytes 2433032 | tf_op jit(solution)/shard_map/ppermute | solution.py:34
  8.4 0.0 copy-done
  8.4 0.0 copy-done.2
  8.4 0.0 copy-start.4
  8.4 1.2 %copy-done.4 = bf16[512,1024]{1,0:T(8,128)(2,1)S(1)} copy-done((bf16[512,1024]{1,0:T(8,128)(2,1)S(1)}, bf16[512,1024]{1,0:T(8,128)(2,1)}, u32[]{:S(2)}) %copy-start.4) | copy-done | bytes 1048600
  9.6 0.0 copy-start.5
  9.6 3.0 %own_piece.3 = (f32[384,512]{1,0:T(8,128)S(1)}, f32[3,512]{1,0:T(4,128)S(1)}, f32[3,512]{1,0:T(4,128)S(1)}, f32[384,512]{1,0:T(8,128)S(1)}, f32[8,128]{1,0:T(8,128)S(1)}) custom-call(f32[8,128]{1,0:T(8,128)S(1)} %get-tuple-element.63.refs_0_, bf16[512,1024]{1,0:T(8,128)(2,1)S(1)} %copy-done, bf16[512,1024]{1,0:T(8,128)(2,1)S(1)} %copy-done.2, ...), custom_call_target="tpu_custom_call" | custom-call | bytes 8856000 | tf_op jit(solution)/shard_map/own_piece/pallas_call | solution.py:387
  12.6 0.0 copy-done.5
  12.7 0.4 pack.2
  13.1 3.2 %collective-permute-start = (bf16[528,768]{1,0:T(8,128)(2,1)S(1)}, bf16[528,768]{1,0:T(8,128)(2,1)S(1)}, u32[]{:S(2)}, u32[]{:S(2)}) collective-permute-start(bf16[528,768]{1,0:T(8,128)(2,1)S(1)} %get-tuple-element.71), channel_id=1, source_target_pairs={{0,8},{4,12},{8,16},{12,20},{16,24},{20,28},{1,9},{5,13},{9,17},{1... | collective-permute-start | bytes 2433032 | tf_op jit(solution)/shard_map/ppermute | solution.py:34
  16.3 1.3 %collective-permute-start.3 = (bf16[528,768]{1,0:T(8,128)(2,1)S(1)}, bf16[528,768]{1,0:T(8,128)(2,1)S(1)}, u32[]{:S(2)}, u32[]{:S(2)}) collective-permute-start(bf16[528,768]{1,0:T(8,128)(2,1)S(1)} %get-tuple-element.72), channel_id=1, source_target_pairs={{0,4},{8,12},{16,20},{24,28},{1,5},{9,13},{17,21},{25,29},{2,6},{1... | collective-permute-start | bytes 2433032 | tf_op jit(solution)/shard_map/ppermute | solution.py:39
  17.6 1.3 %collective-permute-start.2 = (bf16[528,1024]{1,0:T(8,128)(2,1)S(1)}, bf16[528,1024]{1,0:T(8,128)(2,1)S(1)}, u32[]{:S(2)}, u32[]{:S(2)}) collective-permute-start(bf16[528,1024]{1,0:T(8,128)(2,1)S(1)} %get-tuple-element.78), channel_id=1, source_target_pairs={{8,0},{12,4},{16,8},{20,12},{24,16},{28,20},{9,1},{13,5},{17,9},{2... | collective-permute-start | bytes 3244040 | tf_op jit(solution)/shard_map/ppermute | solution.py:34
  18.9 1.3 %collective-permute-start.5 = (bf16[544,1280]{1,0:T(8,128)(2,1)S(1)}, bf16[544,1280]{1,0:T(8,128)(2,1)S(1)}, u32[]{:S(2)}, u32[]{:S(2)}) collective-permute-start(bf16[544,1280]{1,0:T(8,128)(2,1)S(1)} %get-tuple-element.87), channel_id=1, source_target_pairs={{0,4},{8,12},{16,20},{24,28},{1,5},{9,13},{17,21},{25,29},{2,6},{1... | collective-permute-start | bytes 4177928 | tf_op jit(solution)/shard_map/ppermute | solution.py:39
  20.2 4.8 %collective-permute-done.1.refs_0_.two = bf16[528,768]{1,0:T(8,128)(2,1)S(1)} collective-permute-done((bf16[528,768]{1,0:T(8,128)(2,1)S(1)}, bf16[528,768]{1,0:T(8,128)(2,1)S(1)}, u32[]{:S(2)}, u32[]{:S(2)}) %collective-permute-start.1) | collective-permute-done | bytes 811040 | tf_op jit(solution)/shard_map/ppermute | solution.py:34
  25.1 2.2 %collective-permute-start.4 = (bf16[528,768]{1,0:T(8,128)(2,1)S(1)}, bf16[528,768]{1,0:T(8,128)(2,1)S(1)}, u32[]{:S(2)}, u32[]{:S(2)}) collective-permute-start(bf16[528,768]{1,0:T(8,128)(2,1)S(1)} %collective-permute-done.1.refs_0_.two), channel_id=1, source_target_pairs={{4,0},{12,8},{20,16},{28,24},{5,1},{13,9},{21,17},{29,25},{6,2},{1... | collective-permute-start | bytes 2433032 | tf_op jit(solution)/shard_map/ppermute | solution.py:44
  27.3 3.0 %own_piece.4 = (f32[384,512]{1,0:T(8,128)S(1)}, f32[3,512]{1,0:T(4,128)S(1)}, f32[3,512]{1,0:T(4,128)S(1)}, f32[384,512]{1,0:T(8,128)S(1)}, f32[8,128]{1,0:T(8,128)S(1)}) custom-call(bf16[528,768]{1,0:T(8,128)(2,1)S(1)} %collective-permute-done.1.refs_0_.two, f32[8,128]{1,0:T(8,128)S(1)} %get-tuple-element.73.refs_1_, bf16[512,1024]{1,0:T(8,128)(2,1)S(1)} %copy-done, ...), custom_call_target="tpu_custom_call" | custom-call | bytes 8856000 | tf_op jit(solution)/shard_map/own_piece/pallas_call | solution.py:387
  30.3 0.1 pack.3
  30.4 12.1 %collective-permute-done.refs_0_.two = bf16[528,768]{1,0:T(8,128)(2,1)S(1)} collective-permute-done((bf16[528,768]{1,0:T(8,128)(2,1)S(1)}, bf16[528,768]{1,0:T(8,128)(2,1)S(1)}, u32[]{:S(2)}, u32[]{:S(2)}) %collective-permute-start) | collective-permute-done | bytes 811040 | tf_op jit(solution)/shard_map/ppermute | solution.py:34
  42.4 4.1 %collective-permute-start.7 = (bf16[528,512]{1,0:T(8,128)(2,1)S(1)}, bf16[528,512]{1,0:T(8,128)(2,1)S(1)}, u32[]{:S(2)}, u32[]{:S(2)}) collective-permute-start(bf16[528,512]{1,0:T(8,128)(2,1)S(1)} %get-tuple-element.89), channel_id=1, source_target_pairs={{0,8},{4,12},{8,16},{12,20},{16,24},{20,28},{1,9},{5,13},{9,17},{1... | collective-permute-start | bytes 1622024 | tf_op jit(solution)/shard_map/ppermute | solution.py:34
  46.6 0.0 collective-permute-done.3.even
  46.6 2.4 %collective-permute-start.6 = (bf16[528,768]{1,0:T(8,128)(2,1)S(1)}, bf16[528,768]{1,0:T(8,128)(2,1)S(1)}, u32[]{:S(2)}, u32[]{:S(2)}) collective-permute-start(bf16[528,768]{1,0:T(8,128)(2,1)S(1)} %collective-permute-done.refs_0_.two), channel_id=1, source_target_pairs={{4,0},{12,8},{20,16},{28,24},{5,1},{13,9},{21,17},{29,25},{6,2},{1... | collective-permute-start | bytes 2433032 | tf_op jit(solution)/shard_map/ppermute | solution.py:44
  49.0 2.0 %own_piece.5 = (f32[256,512]{1,0:T(8,128)S(1)}, f32[2,512]{1,0:T(2,128)S(1)}, f32[2,512]{1,0:T(2,128)S(1)}, f32[256,512]{1,0:T(8,128)S(1)}, f32[8,128]{1,0:T(8,128)S(1)}) custom-call(bf16[528,768]{1,0:T(8,128)(2,1)S(1)} %collective-permute-done.refs_0_.two, f32[8,128]{1,0:T(8,128)S(1)} %get-tuple-element.75.refs_1_, bf16[512,1024]{1,0:T(8,128)(2,1)S(1)} %copy-done, ...), custom_call_target="tpu_custom_call" | custom-call | bytes 5904000 | tf_op jit(solution)/shard_map/own_piece/pallas_call | solution.py:387
  51.0 0.0 collective-permute-done.2.q_ref.keep_ref
  51.0 0.0 collective-permute-done.4.odd
  51.0 3.5 %far_pieces.3 = (bf16[432,640]{1,0:T(8,128)(2,1)S(1)}, f32[8,128]{1,0:T(8,128)S(1)}) custom-call(f32[8,128]{1,0:T(8,128)S(1)} %get-tuple-element.76.token_in, s32[8,512]{1,0:T(8,128)S(1)} %get-tuple-element.77.entry_ref, bf16[528,1024]{1,0:T(8,128)(2,1)S(1)} %collective-permute-done.2.q_ref.keep_ref, ...), custom_call_target="tpu_custom_call" | custom-call | bytes 16605000 | tf_op jit(solution)/shard_map/far_pieces/pallas_call | solution.py:387
  54.5 2.0 %collective-permute-done.7.x_in = bf16[528,512]{1,0:T(8,128)(2,1)S(1)} collective-permute-done((bf16[528,512]{1,0:T(8,128)(2,1)S(1)}, bf16[528,512]{1,0:T(8,128)(2,1)S(1)}, u32[]{:S(2)}, u32[]{:S(2)}) %collective-permute-start.7) | collective-permute-done | bytes 540704 | tf_op jit(solution)/shard_map/ppermute | solution.py:34
  56.5 2.2 %collective-permute-start.8 = (bf16[528,512]{1,0:T(8,128)(2,1)S(1)}, bf16[528,512]{1,0:T(8,128)(2,1)S(1)}, u32[]{:S(2)}, u32[]{:S(2)}) collective-permute-start(bf16[528,512]{1,0:T(8,128)(2,1)S(1)} %gate.1.two), channel_id=1, source_target_pairs={{4,0},{12,8},{20,16},{28,24},{5,1},{13,9},{21,17},{29,25},{6,2},{1... | collective-permute-start | bytes 1622024 | tf_op jit(solution)/shard_map/ppermute | solution.py:44
  58.7 4.4 %collective-permute-start.9 = (bf16[432,640]{1,0:T(8,128)(2,1)S(1)}, bf16[432,640]{1,0:T(8,128)(2,1)S(1)}, u32[]{:S(2)}, u32[]{:S(2)}) collective-permute-start(bf16[432,640]{1,0:T(8,128)(2,1)S(1)} %get-tuple-element.101), channel_id=1, source_target_pairs={{0,8},{4,12},{8,16},{12,20},{16,24},{20,28},{1,9},{5,13},{9,17},{1... | collective-permute-start | bytes 1658888 | tf_op jit(solution)/shard_map/ppermute | solution.py:34
  63.1 4.0 %near_pieces.3 = (f32[384,512]{1,0:T(8,128)S(1)}, f32[384,512]{1,0:T(8,128)S(1)}, f32[8,512]{1,0:T(8,128)S(1)}, f32[8,128]{1,0:T(8,128)S(1)}) custom-call(f32[8,128]{1,0:T(8,128)S(1)} %get-tuple-element.80.token_in, s32[8,512]{1,0:T(8,128)S(1)} %get-tuple-element.77.entry_ref, bf16[512,1024]{1,0:T(8,128)(2,1)S(1)} %copy-done, ...), custom_call_target="tpu_custom_call" | custom-call | bytes 19926000 | tf_op jit(solution)/shard_map/near_pieces/pallas_call | solution.py:387
  67.1 0.0 collective-permute-done.5.even
  67.1 0.0 collective-permute-done.6.odd
  67.2 3.6 %far_pieces.4 = (bf16[432,640]{1,0:T(8,128)(2,1)S(1)}, f32[8,128]{1,0:T(8,128)S(1)}) custom-call(f32[8,128]{1,0:T(8,128)S(1)} %get-tuple-element.86.token_in, s32[8,512]{1,0:T(8,128)S(1)} %get-tuple-element.77.entry_ref, bf16[528,1024]{1,0:T(8,128)(2,1)S(1)} %collective-permute-done.2.q_ref.keep_ref, ...), custom_call_target="tpu_custom_call" | custom-call | bytes 16605000 | tf_op jit(solution)/shard_map/far_pieces/pallas_call | solution.py:387
  70.7 3.2 %collective-permute-start.10 = (bf16[432,640]{1,0:T(8,128)(2,1)S(1)}, bf16[432,640]{1,0:T(8,128)(2,1)S(1)}, u32[]{:S(2)}, u32[]{:S(2)}) collective-permute-start(bf16[432,640]{1,0:T(8,128)(2,1)S(1)} %get-tuple-element.107), channel_id=1, source_target_pairs={{0,8},{4,12},{8,16},{12,20},{16,24},{20,28},{1,9},{5,13},{9,17},{1... | collective-permute-start | bytes 1658888 | tf_op jit(solution)/shard_map/ppermute | solution.py:34
  73.9 1.9 %collective-permute-done.8.odd = bf16[528,512]{1,0:T(8,128)(2,1)S(1)} collective-permute-done((bf16[528,512]{1,0:T(8,128)(2,1)S(1)}, bf16[528,512]{1,0:T(8,128)(2,1)S(1)}, u32[]{:S(2)}, u32[]{:S(2)}) %collective-permute-start.8) | collective-permute-done | bytes 540704 | tf_op jit(solution)/shard_map/ppermute | solution.py:44
  75.9 2.5 %far_pieces.5 = (bf16[288,640]{1,0:T(8,128)(2,1)S(1)}, f32[8,128]{1,0:T(8,128)S(1)}) custom-call(f32[8,128]{1,0:T(8,128)S(1)} %get-tuple-element.88.token_in, s32[8,512]{1,0:T(8,128)S(1)} %get-tuple-element.77.entry_ref, bf16[528,1024]{1,0:T(8,128)(2,1)S(1)} %collective-permute-done.2.q_ref.keep_ref, ...), custom_call_target="tpu_custom_call" | custom-call | bytes 11070000 | tf_op jit(solution)/shard_map/far_pieces/pallas_call | solution.py:387
  78.4 3.4 %collective-permute-start.11 = (bf16[288,640]{1,0:T(8,128)(2,1)S(1)}, bf16[288,640]{1,0:T(8,128)(2,1)S(1)}, u32[]{:S(2)}, u32[]{:S(2)}) collective-permute-start(bf16[288,640]{1,0:T(8,128)(2,1)S(1)} %get-tuple-element.113), channel_id=1, source_target_pairs={{0,8},{4,12},{8,16},{12,20},{16,24},{20,28},{1,9},{5,13},{9,17},{1... | collective-permute-start | bytes 1105928 | tf_op jit(solution)/shard_map/ppermute | solution.py:34
  81.8 4.1 %near_pieces.4 = (f32[384,512]{1,0:T(8,128)S(1)}, f32[384,512]{1,0:T(8,128)S(1)}, f32[8,512]{1,0:T(8,128)S(1)}, f32[8,128]{1,0:T(8,128)S(1)}) custom-call(f32[8,128]{1,0:T(8,128)S(1)} %get-tuple-element.90.token_in, s32[8,512]{1,0:T(8,128)S(1)} %get-tuple-element.77.entry_ref, bf16[512,1024]{1,0:T(8,128)(2,1)S(1)} %copy-done, ...), custom_call_target="tpu_custom_call" | custom-call | bytes 19926000 | tf_op jit(solution)/shard_map/near_pieces/pallas_call | solution.py:387
  85.9 2.9 %near_pieces.5 = (f32[256,512]{1,0:T(8,128)S(1)}, f32[256,512]{1,0:T(8,128)S(1)}, f32[8,512]{1,0:T(8,128)S(1)}, f32[8,128]{1,0:T(8,128)S(1)}) custom-call(f32[8,128]{1,0:T(8,128)S(1)} %get-tuple-element.95.token_in, s32[8,512]{1,0:T(8,128)S(1)} %get-tuple-element.77.entry_ref, bf16[512,1024]{1,0:T(8,128)(2,1)S(1)} %copy-done, ...), custom_call_target="tpu_custom_call" | custom-call | bytes 13284000 | tf_op jit(solution)/shard_map/near_pieces/pallas_call | solution.py:387
  88.8 0.0 collective-permute-done.9.pay_ref
  88.8 0.4 merge.3
  89.2 0.0 collective-permute-done.10.pay_ref
  89.3 0.4 merge.4
  89.7 0.0 copy-start.7
  89.7 2.5 %collective-permute-done.11.pay_ref = bf16[288,640]{1,0:T(8,128)(2,1)S(1)} collective-permute-done((bf16[288,640]{1,0:T(8,128)(2,1)S(1)}, bf16[288,640]{1,0:T(8,128)(2,1)S(1)}, u32[]{:S(2)}, u32[]{:S(2)}) %collective-permute-start.11) | collective-permute-done | bytes 368672 | tf_op jit(solution)/shard_map/ppermute | solution.py:34
  92.2 0.9 merge.5
  93.1 8.1 %all_gather.3 = f32[4,4,128]{2,1,0:T(4,128)S(1)} all-gather(f32[1,4,128]{2,1,0:T(4,128)S(1)} %bitcast.11), channel_id=1, replica_groups=mesh['ctx'=8,'head'=4] {'head'}, dimensions={0}, use_global_device_ids=true | all-gather | bytes 10240 | tf_op jit(solution)/shard_map/all_gather | solution.py:542
  101.2 0.0 copy-done.7
  101.2 1.6 %normalize.1 = bf16[512,1024]{1,0:T(8,128)(2,1)} custom-call(f32[384,512]{1,0:T(8,128)S(1)} %get-tuple-element.105.refs_0_, f32[384,512]{1,0:T(8,128)S(1)} %get-tuple-element.111.refs_1_, f32[256,512]{1,0:T(8,128)S(1)} %get-tuple-element.117.refs_2_, f32[4,512]{1,0:T(4,128)S(1)} %bitcast.7, f32[1,1024]{1,0:T(1,128)S(1)} %bitcast.8), custom_call_target="tpu_custom_call" | custom-call | tf_op jit(solution)/shard_map/normalize/pallas_call | solution.py:544
  (3 shorter events, 0.0 us)
Async XLA Ops:
  0.0 8.4 %copy-start = (bf16[512,1024]{1,0:T(8,128)(2,1)S(1)}, bf16[512,1024]{1,0:T(8,128)(2,1)}, u32[]{:S(2)}) copy-start(bf16[512,1024]{1,0:T(8,128)(2,1)} %q_ref.13) | copy-start | bytes 3145732
  0.0 1.3 %copy-start.1 = (bf16[512,1024]{1,0:T(8,128)(2,1)S(1)}, bf16[512,1024]{1,0:T(8,128)(2,1)}, u32[]{:S(2)}) copy-start(bf16[512,1024]{1,0:T(8,128)(2,1)} %refs_3_.5) | copy-start | bytes 3145732
  1.3 1.2 %copy-start.3 = (bf16[512,1024]{1,0:T(8,128)(2,1)S(1)}, bf16[512,1024]{1,0:T(8,128)(2,1)}, u32[]{:S(2)}) copy-start(bf16[512,1024]{1,0:T(8,128)(2,1)} %refs_4_.3) | copy-start | bytes 3145732
  2.5 0.7 copy-start.6
  3.3 0.7 copy-start.8
  3.9 0.7 copy-start.9
  4.6 3.8 %copy-start.2 = (bf16[512,1024]{1,0:T(8,128)(2,1)S(1)}, bf16[512,1024]{1,0:T(8,128)(2,1)}, u32[]{:S(2)}) copy-start(bf16[512,1024]{1,0:T(8,128)(2,1)} %refs_3_.5) | copy-start | bytes 3145732
  5.1 19.9 %collective-permute-start.1 = (bf16[528,768]{1,0:T(8,128)(2,1)S(1)}, bf16[528,768]{1,0:T(8,128)(2,1)S(1)}, u32[]{:S(2)}, u32[]{:S(2)}) collective-permute-start(bf16[528,768]{1,0:T(8,128)(2,1)S(1)} %get-tuple-element.72), channel_id=1, source_target_pairs={{0,8},{4,12},{8,16},{12,20},{16,24},{20,28},{1,9},{5,13},{9,17},{1... | collective-permute-start | bytes 2433032 | tf_op jit(solution)/shard_map/ppermute | solution.py:34
  8.4 1.2 %copy-start.4 = (bf16[512,1024]{1,0:T(8,128)(2,1)S(1)}, bf16[512,1024]{1,0:T(8,128)(2,1)}, u32[]{:S(2)}) copy-start(bf16[512,1024]{1,0:T(8,128)(2,1)} %refs_4_.3) | copy-start | bytes 3145732
  9.6 3.0 %copy-start.5 = (bf16[512,1024]{1,0:T(8,128)(2,1)S(1)}, bf16[512,1024]{1,0:T(8,128)(2,1)}, u32[]{:S(2)}) copy-start(bf16[512,1024]{1,0:T(8,128)(2,1)} %refs_4_.3) | copy-start | bytes 3145732
  13.1 29.3 %collective-permute-start = (bf16[528,768]{1,0:T(8,128)(2,1)S(1)}, bf16[528,768]{1,0:T(8,128)(2,1)S(1)}, u32[]{:S(2)}, u32[]{:S(2)}) collective-permute-start(bf16[528,768]{1,0:T(8,128)(2,1)S(1)} %get-tuple-element.71), channel_id=1, source_target_pairs={{0,8},{4,12},{8,16},{12,20},{16,24},{20,28},{1,9},{5,13},{9,17},{1... | collective-permute-start | bytes 2433032 | tf_op jit(solution)/shard_map/ppermute | solution.py:34
  16.3 30.3 %collective-permute-start.3 = (bf16[528,768]{1,0:T(8,128)(2,1)S(1)}, bf16[528,768]{1,0:T(8,128)(2,1)S(1)}, u32[]{:S(2)}, u32[]{:S(2)}) collective-permute-start(bf16[528,768]{1,0:T(8,128)(2,1)S(1)} %get-tuple-element.72), channel_id=1, source_target_pairs={{0,4},{8,12},{16,20},{24,28},{1,5},{9,13},{17,21},{25,29},{2,6},{1... | collective-permute-start | bytes 2433032 | tf_op jit(solution)/shard_map/ppermute | solution.py:39
  17.6 33.4 %collective-permute-start.2 = (bf16[528,1024]{1,0:T(8,128)(2,1)S(1)}, bf16[528,1024]{1,0:T(8,128)(2,1)S(1)}, u32[]{:S(2)}, u32[]{:S(2)}) collective-permute-start(bf16[528,1024]{1,0:T(8,128)(2,1)S(1)} %get-tuple-element.78), channel_id=1, source_target_pairs={{8,0},{12,4},{16,8},{20,12},{24,16},{28,20},{9,1},{13,5},{17,9},{2... | collective-permute-start | bytes 3244040 | tf_op jit(solution)/shard_map/ppermute | solution.py:34
  18.9 48.2 %collective-permute-start.5 = (bf16[544,1280]{1,0:T(8,128)(2,1)S(1)}, bf16[544,1280]{1,0:T(8,128)(2,1)S(1)}, u32[]{:S(2)}, u32[]{:S(2)}) collective-permute-start(bf16[544,1280]{1,0:T(8,128)(2,1)S(1)} %get-tuple-element.87), channel_id=1, source_target_pairs={{0,4},{8,12},{16,20},{24,28},{1,5},{9,13},{17,21},{25,29},{2,6},{1... | collective-permute-start | bytes 4177928 | tf_op jit(solution)/shard_map/ppermute | solution.py:39
  25.1 25.9 %collective-permute-start.4 = (bf16[528,768]{1,0:T(8,128)(2,1)S(1)}, bf16[528,768]{1,0:T(8,128)(2,1)S(1)}, u32[]{:S(2)}, u32[]{:S(2)}) collective-permute-start(bf16[528,768]{1,0:T(8,128)(2,1)S(1)} %collective-permute-done.1.refs_0_.two), channel_id=1, source_target_pairs={{4,0},{12,8},{20,16},{28,24},{5,1},{13,9},{21,17},{29,25},{6,2},{1... | collective-permute-start | bytes 2433032 | tf_op jit(solution)/shard_map/ppermute | solution.py:44
  42.4 14.1 %collective-permute-start.7 = (bf16[528,512]{1,0:T(8,128)(2,1)S(1)}, bf16[528,512]{1,0:T(8,128)(2,1)S(1)}, u32[]{:S(2)}, u32[]{:S(2)}) collective-permute-start(bf16[528,512]{1,0:T(8,128)(2,1)S(1)} %get-tuple-element.89), channel_id=1, source_target_pairs={{0,8},{4,12},{8,16},{12,20},{16,24},{20,28},{1,9},{5,13},{9,17},{1... | collective-permute-start | bytes 1622024 | tf_op jit(solution)/shard_map/ppermute | solution.py:34
  46.6 20.6 %collective-permute-start.6 = (bf16[528,768]{1,0:T(8,128)(2,1)S(1)}, bf16[528,768]{1,0:T(8,128)(2,1)S(1)}, u32[]{:S(2)}, u32[]{:S(2)}) collective-permute-start(bf16[528,768]{1,0:T(8,128)(2,1)S(1)} %collective-permute-done.refs_0_.two), channel_id=1, source_target_pairs={{4,0},{12,8},{20,16},{28,24},{5,1},{13,9},{21,17},{29,25},{6,2},{1... | collective-permute-start | bytes 2433032 | tf_op jit(solution)/shard_map/ppermute | solution.py:44
  56.5 19.3 %collective-permute-start.8 = (bf16[528,512]{1,0:T(8,128)(2,1)S(1)}, bf16[528,512]{1,0:T(8,128)(2,1)S(1)}, u32[]{:S(2)}, u32[]{:S(2)}) collective-permute-start(bf16[528,512]{1,0:T(8,128)(2,1)S(1)} %gate.1.two), channel_id=1, source_target_pairs={{4,0},{12,8},{20,16},{28,24},{5,1},{13,9},{21,17},{29,25},{6,2},{1... | collective-permute-start | bytes 1622024 | tf_op jit(solution)/shard_map/ppermute | solution.py:44
  58.7 30.1 %collective-permute-start.9 = (bf16[432,640]{1,0:T(8,128)(2,1)S(1)}, bf16[432,640]{1,0:T(8,128)(2,1)S(1)}, u32[]{:S(2)}, u32[]{:S(2)}) collective-permute-start(bf16[432,640]{1,0:T(8,128)(2,1)S(1)} %get-tuple-element.101), channel_id=1, source_target_pairs={{0,8},{4,12},{8,16},{12,20},{16,24},{20,28},{1,9},{5,13},{9,17},{1... | collective-permute-start | bytes 1658888 | tf_op jit(solution)/shard_map/ppermute | solution.py:34
  70.7 18.5 %collective-permute-start.10 = (bf16[432,640]{1,0:T(8,128)(2,1)S(1)}, bf16[432,640]{1,0:T(8,128)(2,1)S(1)}, u32[]{:S(2)}, u32[]{:S(2)}) collective-permute-start(bf16[432,640]{1,0:T(8,128)(2,1)S(1)} %get-tuple-element.107), channel_id=1, source_target_pairs={{0,8},{4,12},{8,16},{12,20},{16,24},{20,28},{1,9},{5,13},{9,17},{1... | collective-permute-start | bytes 1658888 | tf_op jit(solution)/shard_map/ppermute | solution.py:34
  78.4 13.8 %collective-permute-start.11 = (bf16[288,640]{1,0:T(8,128)(2,1)S(1)}, bf16[288,640]{1,0:T(8,128)(2,1)S(1)}, u32[]{:S(2)}, u32[]{:S(2)}) collective-permute-start(bf16[288,640]{1,0:T(8,128)(2,1)S(1)} %get-tuple-element.113), channel_id=1, source_target_pairs={{0,8},{4,12},{8,16},{12,20},{16,24},{20,28},{1,9},{5,13},{9,17},{1... | collective-permute-start | bytes 1105928 | tf_op jit(solution)/shard_map/ppermute | solution.py:34
  89.7 11.5 %copy-start.7 = (f32[1024]{0:T(1024)S(1)}, f32[1024]{0:T(1024)}, u32[]{:S(2)}) copy-start(f32[1024]{0:T(1024)} %param.13) | copy-start | bytes 12292

commit v3 on v2

--- a/solution.py
+++ b/solution.py
@@ -107,21 +107,45 @@
         pay_ref[dec_row : dec_row + 16, length:] = jnp.zeros((16, pay_ref.shape[1] - length), jnp.bfloat16)
 
 
+def running_sums(decays):
+    heads, length = decays.shape
+    parts = jnp.concatenate(split3(decays), axis=0).astype(jnp.bfloat16)
+    u = lax.broadcasted_iota(jnp.int32, (length, length), 0)
+    t = lax.broadcasted_iota(jnp.int32, (length, length), 1)
+    ones = jnp.where(u <= t, 1.0, 0.0).astype(jnp.bfloat16)
+    sums = dot(parts, ones, NN)
+    return sums[:heads] + sums[heads : 2 * heads] + sums[2 * heads :]
+
+
+def decay_rows(cum, first, n):
+    length = cum.shape[1]
+    last = cum[:, length - 1 :]
+    rows = []
+    for h in range(first, first + n):
+        rows += list(split2(last[h : h + 1] - cum[h : h + 1]))
+    for h in range(first, first + n):
+        rows += list(split2(last[h : h + 1] + jnp.zeros((1, length), jnp.float32)))
+    return stack_rows(rows, 16, length).astype(jnp.bfloat16)
+
+
+def first_kernel(n, ld_ref, k_ref, v_ref, pay_ref, token_ref, sems):
+    length = k_ref.shape[0]
+    copies = fetch(pay_ref, k_ref, v_ref, 0, n * 128, sems, 0)
+    fill(pay_ref, decay_rows(running_sums(ld_ref[...]), 0, n), length, length)
+    token_ref[...] = jnp.zeros_like(token_ref)
+    for copy in copies:
+        copy.wait()
+
+
 def prep_kernel(
-    divisor, sizes, docs_ref, mask_ref, ld_ref, k_ref, v_ref,
-    thr_ref, start_ref, ahead_ref, entry_ref, keep_ref, cum_ref, cumt_ref, coef_ref, dec_ref, pay_ref, token_ref, sems,
+    divisor, sizes, token_in, docs_ref, mask_ref, ld_ref,
+    thr_ref, start_ref, ahead_ref, entry_ref, keep_ref, cum_ref, cumt_ref, coef_ref, dec_ref, token_ref,
 ):
     heads, length = ld_ref.shape
-    copies = fetch(pay_ref, k_ref, v_ref, 0, sizes[0] * 128, sems, 0)
     tiles = length // BLK
     begin = lax.axis_index("ctx").astype(jnp.int32) * length
     f32, bf16 = jnp.float32, jnp.bfloat16
-    parts = jnp.concatenate(split3(ld_ref[...]), axis=0).astype(bf16)
-    u = lax.broadcasted_iota(jnp.int32, (length, length), 0)
-    t = lax.broadcasted_iota(jnp.int32, (length, length), 1)
-    ones = jnp.where(u <= t, 1.0, 0.0).astype(bf16)
-    sums = dot(parts, ones, NN)
-    cum = sums[:heads] + sums[heads : 2 * heads] + sums[2 * heads :]
+    cum = running_sums(ld_ref[...])
     cum_ref[...] = cum
     cumt_ref[...] = jnp.concatenate([cum, jnp.zeros((BLK - heads, length), f32)], axis=0).T
     pos = begin + lax.broadcasted_iota(jnp.int32, (8, length), 1)
@@ -149,22 +173,11 @@
     thr_ref[...] = jnp.where(keep, start[:1] - base, FAR_OFF)
     kept = jnp.where(picked > 0.5, 1.0, 0.0)
     keep_ref[...] = kept[0:16].astype(bf16)
-    last = cum[:, length - 1 :]
     first = 0
     for c, n in enumerate(sizes):
-        rows = []
-        for h in range(first, first + n):
-            rows += list(split2(last[h : h + 1] - cum[h : h + 1]))
-        for h in range(first, first + n):
-            rows += list(split2(last[h : h + 1] + jnp.zeros((1, length), f32)))
-        dec = stack_rows(rows, 16, length).astype(bf16)
-        dec_ref[c * 16 : (c + 1) * 16, :] = dec
-        if c == 0:
-            fill(pay_ref, dec, length, length)
+        dec_ref[c * 16 : (c + 1) * 16, :] = decay_rows(cum, first, n)
         first += n
     token_ref[...] = jnp.zeros_like(token_ref)
-    for copy in copies:
-        copy.wait()
 
 
 def pack_kernel(sizes, width1, token_in, q_ref, keep_ref, k_ref, v_ref, dec_ref, one_ref, both_ref, qpay_ref, token_ref, sems):
@@ -195,7 +208,7 @@
         copy.wait()
 
 
-def gate_kernel(token_in, x_in, x_out):
+def gate_kernel(*refs):
     pass
 
 
@@ -287,15 +300,16 @@
         base = (j - REACH * tiles) * BLK
         thr.append(jnp.where(keep[j : j + 1] > 0.5, ahead_ref[0:1, :] - base, FAR_OFF))
     thr = jnp.concatenate(thr, axis=0)
+    rows = [jnp.ones((1, length), jnp.float32)]
     for i in range(n):
         top, total, o, state = p.attend(i, q_ref[0:length, i * 128 : (i + 1) * 128], thr, scale2)
-        r = i * 144
+        r = i * 128
         out_ref[r : r + 128, 0:length] = (o * (1.0 / total)).astype(jnp.bfloat16)
         out_ref[r : r + 128, length:] = state
         lse = top + jnp.log(total) * LOG2E
-        stats = stack_rows(list(split3(lse)) + [jnp.ones_like(lse)], 16, length)
-        out_ref[r + 128 : r + 144, 0:length] = stats.astype(jnp.bfloat16)
-        out_ref[r + 128 : r + 144, length:] = jnp.zeros((16, 128), jnp.bfloat16)
+        rows += list(split3(lse))
+    out_ref[n * 128 :, 0:length] = stack_rows(rows, 16, length).astype(jnp.bfloat16)
+    out_ref[n * 128 :, length:] = jnp.zeros((16, 128), jnp.bfloat16)
     token_ref[...] = jnp.zeros_like(token_ref)
 
 
@@ -331,16 +345,15 @@
 def merge_kernel(n, token_in, q_ref, pay_ref, x_ref, on_ref, st_ref, mixed_ref, sq_ref, token_ref):
     squares = None
     length = q_ref.shape[0]
+    stats = pay_ref[n * 128 :, 0:length].astype(jnp.float32)
     for i in range(n):
         q = q_ref[:, i * 128 : (i + 1) * 128]
         rows = slice(i * 128, (i + 1) * 128)
-        r = i * 144
-        stats = pay_ref[r + 128 : r + 144, 0:length].astype(jnp.float32)
-        lse_far = join3(stats, 0)
-        far = pay_ref[r : r + 128, 0:length].astype(jnp.float32)
+        lse_far = join3(stats, 1 + 3 * i)
+        far = pay_ref[rows, 0:length].astype(jnp.float32)
         share = 1.0 / (1.0 + jnp.exp2(jnp.minimum(st_ref[i : i + 1, :] - lse_far, 120.0)))
-        share = jnp.where((lse_far > 0.5 * NEG) & (stats[3:4] > 0.5), share, 0.0)
-        lin = dot(pay_ref[r : r + 128, length:], q, NT) * st_ref[n + i : n + i + 1, :]
+        share = jnp.where((lse_far > 0.5 * NEG) & (stats[0:1] > 0.5), share, 0.0)
+        lin = dot(pay_ref[rows, length:], q, NT) * st_ref[n + i : n + i + 1, :]
         mixed = x_ref[rows, :] + share * (far - on_ref[rows, :]) + lin
         mixed_ref[rows, :] = mixed
         part = jnp.sum(mixed * mixed, axis=0, keepdims=True)
@@ -381,7 +394,7 @@
     def cols(c, rows=length):
         return pl.BlockSpec((rows, sizes[c] * hd), lambda *_: (0, firsts[c] // sizes[c]))
 
-    def run(kernel, name, us, specs, args, outs, scratch=()):
+    def run(kernel, name, us, specs, args, outs, scratch=(), limit=24):
         outs = outs + [shape((8, 128), f32)]
         out_specs = [whole(o) for o in outs]
         return pl.pallas_call(
@@ -391,7 +404,7 @@
             out_specs=out_specs,
             out_shape=outs,
             scratch_shapes=scratch,
-            compiler_params=params(),
+            compiler_params=params(limit),
             cost_estimate=pl.CostEstimate(flops=0, bytes_accessed=int(us * 3.69e6), transcendentals=0),
             name=name,
         )(*args)
@@ -410,16 +423,24 @@
         shape((length, BLK), f32),
         shape((heads, length), f32),
         shape((16 * len(sizes), length), bf16),
-        pay_shape(0),
     ]
-    thr, start, ahead, entry, keep, cum, cum_t, coef, dec, pay0, token = run(
+    pay0, token = run(
+        partial(first_kernel, sizes[0]),
+        "first_chunk",
+        1,
+        [whole(log_decay), hbm, hbm],
+        (log_decay, key, value),
+        [pay_shape(0)],
+        [dma((2,))],
+        limit=60,
+    )
+    thr, start, ahead, entry, keep, cum, cum_t, coef, dec, token = run(
         partial(prep_kernel, divisor, sizes),
         "prep",
         2,
-        [whole(docs), whole(tile_mask), whole(log_decay), hbm, hbm],
-        (docs, tile_mask, log_decay, key, value),
+        [loose, whole(docs), whole(tile_mask), whole(log_decay)],
+        (token, docs, tile_mask, log_decay),
         outs,
-        [dma((2,))],
     )
     thr_near = pl.BlockSpec((2 * tiles, length), lambda *_: (1, 0))
 
@@ -471,7 +492,7 @@
             1.5 * n,
             [loose, whole(entry), cols(c), kept, whole(ahead)] + [whole(a) for a in kv(c)],
             (token, entry, q_far, q_far, ahead, *kv(c)),
-            [shape((n * (hd + 16), length + hd), bf16)],
+            [shape((n * hd + 16, length + hd), bf16)],
         )
         return shifted(pay, 2), token
 
@@ -487,16 +508,16 @@
             [shape((n * hd, length), f32), shape((1, length), f32)],
         )
 
-    def gate(x, token):
+    def gate(x, *after):
         return pl.pallas_call(
             gate_kernel,
-            in_specs=[loose, loose],
+            in_specs=[loose] * (1 + len(after)),
             out_specs=loose,
             out_shape=shape(x.shape, x.dtype),
-            input_output_aliases={1: 0},
+            input_output_aliases={0: 0},
             compiler_params=params(1),
             name="gate",
-        )(token, x)
+        )(x, *after)
 
     chunks = range(len(sizes))
     diag, parts, pays = [None] * 3, [None] * 3, [None] * 3
@@ -524,14 +545,14 @@
     two_back[2] = shifted(pay, 2)
     from_even[1] = even_to_odd(both)
     from_odd[1] = odd_to_even(two_back[1])
-    diag[2], token = own(2, token, two_back[1])
+    diag[2], token = own(2, token)
     pays[0], token = far(0, token)
+    parts[0], token = near(0, token)
     two_back[2] = gate(two_back[2], token)
     from_odd[2] = odd_to_even(two_back[2])
-    parts[0], token = near(0, token)
     pays[1], token = far(1, token)
+    parts[1], token = near(1, token)
     pays[2], token = far(2, token)
-    parts[1], token = near(1, token)
     parts[2], token = near(2, token)
     mixed, total = [], None
     for c in chunks:

time: 104 us -> 97.6 us (0.938)
  waiting for transfers between devices: 23.4 us -> 17.7 us
  local copies, waits for them, and re-layouts: 5.83 us -> 1.92 us
  Pallas kernels: 33 us -> 35.5 us
    unnamed x21 -> x19, local copies, waits for them, and re-layouts: 5.83 us -> 1.92 us
    ppermute x7, waiting for transfers between devices: 21.4 us -> 17.7 us  [shifted(): lax.ppermute(x, 'ctx', [(i, i + by) for i in range(n) if 0 <= i + by < n])]
    pallas_call x15 -> x16, Pallas kernels: 31.4 us -> 33.9 us  [run(): pl.pallas_call(kernel, grid=(1,), in_specs=specs, out_specs=out_specs, ou...]
    ppermute x3, waiting for transfers between devices: 1.95 us -> 0.01 us  [odd_to_even(): return lax.ppermute(x, 'ctx', [(i, i - 1) for i in range(1, n, 2)])]
  transfers between devices with their start and end apart: 12 -> 12, of which waited for: 5 -> 3; matrix products, arithmetic and copies ran while one was open for 0% -> 0% of each run, Pallas kernels for 29% -> 31%
where the time goes in v3:
time: 97.6 us; the launch traced here: 96 us
  Pallas kernels  35.5 us (36%)
  starting transfers between devices  32.1 us (33%)
  waiting for transfers between devices  17.7 us (18%)
  blocking collectives  8.4 us (9%)
  local copies, waits for them, and re-layouts  1.92 us (2%)
    pallas_call x16, Pallas kernels, run(): pl.pallas_call(kernel, grid=(1,), in_specs=specs, out_specs=out_specs, ou...  33.9 us
    ppermute x7, starting transfers between devices, shifted(): lax.ppermute(x, 'ctx', [(i, i + by) for i in range(n) if 0 <= i + by < n])  23.2 us
    ppermute x7, waiting for transfers between devices, shifted(): lax.ppermute(x, 'ctx', [(i, i + by) for i in range(n) if 0 <= i + by < n])  17.7 us
    all_gather x1, blocking collectives, on_device(): lax.all_gather(total.reshape(length // 128, 128), 'head')  8.4 us
    ppermute x3, starting transfers between devices, odd_to_even(): return lax.ppermute(x, 'ctx', [(i, i - 1) for i in range(1, n, 2)])  6.35 us
    ppermute x2, starting transfers between devices, even_to_odd(): return lax.ppermute(x, 'ctx', [(i, i + 1) for i in range(0, n - 1, 2)])  2.58 us
  transfers between devices with their start and end apart: 12, of which 3 were waited for; matrix products, arithmetic and copies ran while one was open for 0% of the time, Pallas kernels for 31%

profile of v3, /device:TPU:3, one launch (start us, length us, event | category | flops | bytes accessed | tf_op | source)
XLA Modules:
  0.0 96.0 jit_solution(13678093992364594334)
XLA Ops:
  0.0 0.0 copy-start.4
  0.0 0.0 copy-start.1
  0.0 0.0 copy-start.8
  0.0 0.0 copy-start.7
  0.0 0.0 copy-start
  0.0 2.9 %first_chunk.1 = (bf16[528,768]{1,0:T(8,128)(2,1)}, f32[8,128]{1,0:T(8,128)}) custom-call(f32[8,512]{1,0:T(8,128)} %ld_ref.3, bf16[512,1024]{1,0:T(8,128)(2,1)} %refs_2_.5, bf16[512,1024]{1,0:T(8,128)(2,1)} %refs_3_.5), custom_call_target="tpu_custom_call" | custom-call | bytes 3690000 | tf_op jit(solution)/shard_map/first_chunk/pallas_call | solution.py:400
  2.9 3.3 %collective-permute-start = (bf16[528,768]{1,0:T(8,128)(2,1)}, bf16[528,768]{1,0:T(8,128)(2,1)S(1)}, u32[]{:S(2)}, u32[]{:S(2)}) collective-permute-start(bf16[528,768]{1,0:T(8,128)(2,1)} %get-tuple-element.64), channel_id=1, source_target_pairs={{0,8},{4,12},{8,16},{12,20},{16,24},{20,28},{1,9},{5,13},{9,17},{1... | collective-permute-start | bytes 2433032 | tf_op jit(solution)/shard_map/ppermute | solution.py:34
  6.2 1.3 %collective-permute-start.2 = (bf16[528,768]{1,0:T(8,128)(2,1)}, bf16[528,768]{1,0:T(8,128)(2,1)S(1)}, u32[]{:S(2)}, u32[]{:S(2)}) collective-permute-start(bf16[528,768]{1,0:T(8,128)(2,1)} %get-tuple-element.64), channel_id=1, source_target_pairs={{0,4},{8,12},{16,20},{24,28},{1,5},{9,13},{17,21},{25,29},{2,6},{1... | collective-permute-start | bytes 2433032 | tf_op jit(solution)/shard_map/ppermute | solution.py:39
  7.5 0.0 copy-done.4
  7.5 0.0 copy-done.8
  7.5 0.0 copy-done.7
  7.5 0.0 copy-start.6
  7.5 0.7 copy-done.6
  8.2 0.4 prep.1
  8.6 0.0 copy-done.1
  8.6 0.0 copy-done
  8.6 0.0 copy-start.2
  8.6 1.2 %copy-done.2 = bf16[512,1024]{1,0:T(8,128)(2,1)S(1)} copy-done((bf16[512,1024]{1,0:T(8,128)(2,1)S(1)}, bf16[512,1024]{1,0:T(8,128)(2,1)}, u32[]{:S(2)}) %copy-start.2) | copy-done | bytes 1048600
  9.8 0.0 copy-start.3
  9.8 3.0 %own_piece.3 = (f32[384,512]{1,0:T(8,128)S(1)}, f32[3,512]{1,0:T(4,128)S(1)}, f32[3,512]{1,0:T(4,128)S(1)}, f32[384,512]{1,0:T(8,128)S(1)}, f32[8,128]{1,0:T(8,128)S(1)}) custom-call(f32[8,128]{1,0:T(8,128)S(1)} %get-tuple-element.66.refs_0_, bf16[512,1024]{1,0:T(8,128)(2,1)S(1)} %copy-done, bf16[512,1024]{1,0:T(8,128)(2,1)S(1)} %copy-done.1, ...), custom_call_target="tpu_custom_call" | custom-call | bytes 8856000 | tf_op jit(solution)/shard_map/own_piece/pallas_call | solution.py:400
  12.8 0.0 copy-done.3
  12.9 0.4 pack.2
  13.3 3.2 %collective-permute-start.4 = (bf16[528,768]{1,0:T(8,128)(2,1)S(1)}, bf16[528,768]{1,0:T(8,128)(2,1)S(1)}, u32[]{:S(2)}, u32[]{:S(2)}) collective-permute-start(bf16[528,768]{1,0:T(8,128)(2,1)S(1)} %get-tuple-element.88), channel_id=1, source_target_pairs={{0,8},{4,12},{8,16},{12,20},{16,24},{20,28},{1,9},{5,13},{9,17},{1... | collective-permute-start | bytes 2433032 | tf_op jit(solution)/shard_map/ppermute | solution.py:34
  16.5 1.3 %collective-permute-start.1 = (bf16[528,1024]{1,0:T(8,128)(2,1)S(1)}, bf16[528,1024]{1,0:T(8,128)(2,1)S(1)}, u32[]{:S(2)}, u32[]{:S(2)}) collective-permute-start(bf16[528,1024]{1,0:T(8,128)(2,1)S(1)} %get-tuple-element.79), channel_id=1, source_target_pairs={{8,0},{12,4},{16,8},{20,12},{24,16},{28,20},{9,1},{13,5},{17,9},{2... | collective-permute-start | bytes 3244040 | tf_op jit(solution)/shard_map/ppermute | solution.py:34
  17.8 1.3 %collective-permute-start.5 = (bf16[544,1280]{1,0:T(8,128)(2,1)S(1)}, bf16[544,1280]{1,0:T(8,128)(2,1)S(1)}, u32[]{:S(2)}, u32[]{:S(2)}) collective-permute-start(bf16[544,1280]{1,0:T(8,128)(2,1)S(1)} %get-tuple-element.89), channel_id=1, source_target_pairs={{0,4},{8,12},{16,20},{24,28},{1,5},{9,13},{17,21},{25,29},{2,6},{1... | collective-permute-start | bytes 4177928 | tf_op jit(solution)/shard_map/ppermute | solution.py:39
  19.1 4.0 %collective-permute-done.refs_0_.two = bf16[528,768]{1,0:T(8,128)(2,1)S(1)} collective-permute-done((bf16[528,768]{1,0:T(8,128)(2,1)}, bf16[528,768]{1,0:T(8,128)(2,1)S(1)}, u32[]{:S(2)}, u32[]{:S(2)}) %collective-permute-start) | collective-permute-done | bytes 811040 | tf_op jit(solution)/shard_map/ppermute | solution.py:34
  23.2 2.2 %collective-permute-start.3 = (bf16[528,768]{1,0:T(8,128)(2,1)S(1)}, bf16[528,768]{1,0:T(8,128)(2,1)S(1)}, u32[]{:S(2)}, u32[]{:S(2)}) collective-permute-start(bf16[528,768]{1,0:T(8,128)(2,1)S(1)} %collective-permute-done.refs_0_.two), channel_id=1, source_target_pairs={{4,0},{12,8},{20,16},{28,24},{5,1},{13,9},{21,17},{29,25},{6,2},{1... | collective-permute-start | bytes 2433032 | tf_op jit(solution)/shard_map/ppermute | solution.py:44
  25.4 3.0 %own_piece.4 = (f32[384,512]{1,0:T(8,128)S(1)}, f32[3,512]{1,0:T(4,128)S(1)}, f32[3,512]{1,0:T(4,128)S(1)}, f32[384,512]{1,0:T(8,128)S(1)}, f32[8,128]{1,0:T(8,128)S(1)}) custom-call(bf16[528,768]{1,0:T(8,128)(2,1)S(1)} %collective-permute-done.refs_0_.two, f32[8,128]{1,0:T(8,128)S(1)} %get-tuple-element.74.refs_1_, bf16[512,1024]{1,0:T(8,128)(2,1)S(1)} %copy-done, ...), custom_call_target="tpu_custom_call" | custom-call | bytes 8856000 | tf_op jit(solution)/shard_map/own_piece/pallas_call | solution.py:400
  28.4 0.1 pack.3
  28.5 0.0 collective-permute-done.2.even
  28.5 4.0 %collective-permute-start.7 = (bf16[528,512]{1,0:T(8,128)(2,1)S(1)}, bf16[528,512]{1,0:T(8,128)(2,1)S(1)}, u32[]{:S(2)}, u32[]{:S(2)}) collective-permute-start(bf16[528,512]{1,0:T(8,128)(2,1)S(1)} %get-tuple-element.96), channel_id=1, source_target_pairs={{0,8},{4,12},{8,16},{12,20},{16,24},{20,28},{1,9},{5,13},{9,17},{1... | collective-permute-start | bytes 1622024 | tf_op jit(solution)/shard_map/ppermute | solution.py:34
  32.5 7.9 %collective-permute-done.4.two = bf16[528,768]{1,0:T(8,128)(2,1)S(1)} collective-permute-done((bf16[528,768]{1,0:T(8,128)(2,1)S(1)}, bf16[528,768]{1,0:T(8,128)(2,1)S(1)}, u32[]{:S(2)}, u32[]{:S(2)}) %collective-permute-start.4) | collective-permute-done | bytes 811040 | tf_op jit(solution)/shard_map/ppermute | solution.py:34
  40.4 2.4 %collective-permute-start.6 = (bf16[528,768]{1,0:T(8,128)(2,1)S(1)}, bf16[528,768]{1,0:T(8,128)(2,1)S(1)}, u32[]{:S(2)}, u32[]{:S(2)}) collective-permute-start(bf16[528,768]{1,0:T(8,128)(2,1)S(1)} %collective-permute-done.4.two), channel_id=1, source_target_pairs={{4,0},{12,8},{20,16},{28,24},{5,1},{13,9},{21,17},{29,25},{6,2},{1... | collective-permute-start | bytes 2433032 | tf_op jit(solution)/shard_map/ppermute | solution.py:44
  42.8 2.0 %own_piece.5 = (f32[256,512]{1,0:T(8,128)S(1)}, f32[2,512]{1,0:T(2,128)S(1)}, f32[2,512]{1,0:T(2,128)S(1)}, f32[256,512]{1,0:T(8,128)S(1)}, f32[8,128]{1,0:T(8,128)S(1)}) custom-call(f32[8,128]{1,0:T(8,128)S(1)} %get-tuple-element.76.refs_0_, bf16[512,1024]{1,0:T(8,128)(2,1)S(1)} %copy-done, bf16[512,1024]{1,0:T(8,128)(2,1)S(1)} %copy-done.1, ...), custom_call_target="tpu_custom_call" | custom-call | bytes 5904000 | tf_op jit(solution)/shard_map/own_piece/pallas_call | solution.py:400
  44.8 0.0 collective-permute-done.1.q_ref.keep_ref
  44.8 0.0 collective-permute-done.3.odd
  44.9 3.5 %far_pieces.3 = (bf16[400,640]{1,0:T(8,128)(2,1)S(1)}, f32[8,128]{1,0:T(8,128)S(1)}) custom-call(f32[8,128]{1,0:T(8,128)S(1)} %get-tuple-element.77.token_in, s32[8,512]{1,0:T(8,128)S(1)} %get-tuple-element.78.entry_ref, bf16[528,1024]{1,0:T(8,128)(2,1)S(1)} %collective-permute-done.1.q_ref.keep_ref, ...), custom_call_target="tpu_custom_call" | custom-call | bytes 16605000 | tf_op jit(solution)/shard_map/far_pieces/pallas_call | solution.py:400
  48.4 4.1 %near_pieces.3 = (f32[384,512]{1,0:T(8,128)S(1)}, f32[384,512]{1,0:T(8,128)S(1)}, f32[8,512]{1,0:T(8,128)S(1)}, f32[8,128]{1,0:T(8,128)S(1)}) custom-call(f32[8,128]{1,0:T(8,128)S(1)} %get-tuple-element.81.token_in, s32[8,512]{1,0:T(8,128)S(1)} %get-tuple-element.78.entry_ref, bf16[512,1024]{1,0:T(8,128)(2,1)S(1)} %copy-done, ...), custom_call_target="tpu_custom_call" | custom-call | bytes 19926000 | tf_op jit(solution)/shard_map/near_pieces/pallas_call | solution.py:400
  52.4 0.0 collective-permute-done.7.refs_0_
  52.4 1.8 %collective-permute-start.8 = (bf16[528,512]{1,0:T(8,128)(2,1)S(1)}, bf16[528,512]{1,0:T(8,128)(2,1)S(1)}, u32[]{:S(2)}, u32[]{:S(2)}) collective-permute-start(bf16[528,512]{1,0:T(8,128)(2,1)S(1)} %gate.1.two), channel_id=1, source_target_pairs={{4,0},{12,8},{20,16},{28,24},{5,1},{13,9},{21,17},{29,25},{6,2},{1... | collective-permute-start | bytes 1622024 | tf_op jit(solution)/shard_map/ppermute | solution.py:44
  54.2 4.4 %collective-permute-start.9 = (bf16[400,640]{1,0:T(8,128)(2,1)S(1)}, bf16[400,640]{1,0:T(8,128)(2,1)S(1)}, u32[]{:S(2)}, u32[]{:S(2)}) collective-permute-start(bf16[400,640]{1,0:T(8,128)(2,1)S(1)} %get-tuple-element.103), channel_id=1, source_target_pairs={{0,8},{4,12},{8,16},{12,20},{16,24},{20,28},{1,9},{5,13},{9,17},{1... | collective-permute-start | bytes 1536008 | tf_op jit(solution)/shard_map/ppermute | solution.py:34
  58.6 0.0 collective-permute-done.5.even
  58.6 0.0 collective-permute-done.6.odd
  58.6 3.5 %far_pieces.4 = (bf16[400,640]{1,0:T(8,128)(2,1)S(1)}, f32[8,128]{1,0:T(8,128)S(1)}) custom-call(f32[8,128]{1,0:T(8,128)S(1)} %get-tuple-element.87.token_in.refs_1_, s32[8,512]{1,0:T(8,128)S(1)} %get-tuple-element.78.entry_ref, bf16[528,1024]{1,0:T(8,128)(2,1)S(1)} %collective-permute-done.1.q_ref.keep_ref, ...), custom_call_target="tpu_custom_call" | custom-call | bytes 16605000 | tf_op jit(solution)/shard_map/far_pieces/pallas_call | solution.py:400
  62.1 3.2 %collective-permute-start.10 = (bf16[400,640]{1,0:T(8,128)(2,1)S(1)}, bf16[400,640]{1,0:T(8,128)(2,1)S(1)}, u32[]{:S(2)}, u32[]{:S(2)}) collective-permute-start(bf16[400,640]{1,0:T(8,128)(2,1)S(1)} %get-tuple-element.109), channel_id=1, source_target_pairs={{0,8},{4,12},{8,16},{12,20},{16,24},{20,28},{1,9},{5,13},{9,17},{1... | collective-permute-start | bytes 1536008 | tf_op jit(solution)/shard_map/ppermute | solution.py:34
  65.3 4.1 %near_pieces.4 = (f32[384,512]{1,0:T(8,128)S(1)}, f32[384,512]{1,0:T(8,128)S(1)}, f32[8,512]{1,0:T(8,128)S(1)}, f32[8,128]{1,0:T(8,128)S(1)}) custom-call(f32[8,128]{1,0:T(8,128)S(1)} %get-tuple-element.90.token_in, s32[8,512]{1,0:T(8,128)S(1)} %get-tuple-element.78.entry_ref, bf16[512,1024]{1,0:T(8,128)(2,1)S(1)} %copy-done, ...), custom_call_target="tpu_custom_call" | custom-call | bytes 19926000 | tf_op jit(solution)/shard_map/near_pieces/pallas_call | solution.py:400
  69.4 0.0 collective-permute-done.8.odd
  69.4 2.4 %far_pieces.5 = (bf16[272,640]{1,0:T(8,128)(2,1)S(1)}, f32[8,128]{1,0:T(8,128)S(1)}) custom-call(f32[8,128]{1,0:T(8,128)S(1)} %get-tuple-element.95.token_in, s32[8,512]{1,0:T(8,128)S(1)} %get-tuple-element.78.entry_ref, bf16[528,1024]{1,0:T(8,128)(2,1)S(1)} %collective-permute-done.1.q_ref.keep_ref, ...), custom_call_target="tpu_custom_call" | custom-call | bytes 11070000 | tf_op jit(solution)/shard_map/far_pieces/pallas_call | solution.py:400
  71.8 3.8 %collective-permute-start.11 = (bf16[272,640]{1,0:T(8,128)(2,1)S(1)}, bf16[272,640]{1,0:T(8,128)(2,1)S(1)}, u32[]{:S(2)}, u32[]{:S(2)}) collective-permute-start(bf16[272,640]{1,0:T(8,128)(2,1)S(1)} %get-tuple-element.115), channel_id=1, source_target_pairs={{0,8},{4,12},{8,16},{12,20},{16,24},{20,28},{1,9},{5,13},{9,17},{1... | collective-permute-start | bytes 1044488 | tf_op jit(solution)/shard_map/ppermute | solution.py:34
  75.7 2.8 %near_pieces.5 = (f32[256,512]{1,0:T(8,128)S(1)}, f32[256,512]{1,0:T(8,128)S(1)}, f32[8,512]{1,0:T(8,128)S(1)}, f32[8,128]{1,0:T(8,128)S(1)}) custom-call(f32[8,128]{1,0:T(8,128)S(1)} %get-tuple-element.97.token_in, s32[8,512]{1,0:T(8,128)S(1)} %get-tuple-element.78.entry_ref, bf16[512,1024]{1,0:T(8,128)(2,1)S(1)} %copy-done, ...), custom_call_target="tpu_custom_call" | custom-call | bytes 13284000 | tf_op jit(solution)/shard_map/near_pieces/pallas_call | solution.py:400
  78.5 0.0 collective-permute-done.9.pay_ref
  78.5 0.4 merge.3
  78.9 0.0 collective-permute-done.10.pay_ref
  78.9 0.4 merge.4
  79.4 0.0 copy-start.5
  79.4 5.8 %collective-permute-done.11.pay_ref = bf16[272,640]{1,0:T(8,128)(2,1)S(1)} collective-permute-done((bf16[272,640]{1,0:T(8,128)(2,1)S(1)}, bf16[272,640]{1,0:T(8,128)(2,1)S(1)}, u32[]{:S(2)}, u32[]{:S(2)}) %collective-permute-start.11) | collective-permute-done | bytes 348192 | tf_op jit(solution)/shard_map/ppermute | solution.py:34
  85.2 0.9 merge.5
  86.0 8.4 %all_gather.3 = f32[4,4,128]{2,1,0:T(4,128)S(1)} all-gather(f32[1,4,128]{2,1,0:T(4,128)S(1)} %bitcast.11), channel_id=1, replica_groups=mesh['ctx'=8,'head'=4] {'head'}, dimensions={0}, use_global_device_ids=true | all-gather | bytes 10240 | tf_op jit(solution)/shard_map/all_gather | solution.py:563
  94.4 0.0 copy-done.5
  94.4 1.6 %normalize.1 = bf16[512,1024]{1,0:T(8,128)(2,1)} custom-call(f32[384,512]{1,0:T(8,128)S(1)} %get-tuple-element.107.refs_0_, f32[384,512]{1,0:T(8,128)S(1)} %get-tuple-element.113.refs_1_, f32[256,512]{1,0:T(8,128)S(1)} %get-tuple-element.119.refs_2_, f32[4,512]{1,0:T(4,128)S(1)} %bitcast.7, f32[1,1024]{1,0:T(1,128)S(1)} %bitcast.8), custom_call_target="tpu_custom_call" | custom-call | tf_op jit(solution)/shard_map/normalize/pallas_call | solution.py:565
  (3 shorter events, 0.0 us)
Async XLA Ops:
  0.0 7.5 %copy-start.4 = (f32[8,512]{1,0:T(8,128)S(1)}, f32[8,512]{1,0:T(8,128)}, u32[]{:S(2)}) copy-start(f32[8,512]{1,0:T(8,128)} %ld_ref.3) | copy-start | bytes 49156
  0.0 8.6 %copy-start.1 = (bf16[512,1024]{1,0:T(8,128)(2,1)S(1)}, bf16[512,1024]{1,0:T(8,128)(2,1)}, u32[]{:S(2)}) copy-start(bf16[512,1024]{1,0:T(8,128)(2,1)} %refs_2_.5) | copy-start | bytes 3145732
  0.0 7.5 %copy-start.8 = (s32[8]{0:T(128)S(1)}, s32[8]{0:T(128)}, u32[]{:S(2)}) copy-start(s32[8]{0:T(128)} %param.11) | copy-start | bytes 100
  0.0 7.5 %copy-start.7 = (s32[4,20]{1,0:T(4,128)S(1)}, s32[4,20]{1,0:T(4,128)}, u32[]{:S(2)}) copy-start(s32[4,20]{1,0:T(4,128)} %mask_ref.1) | copy-start | bytes 964
  0.0 8.6 %copy-start = (bf16[512,1024]{1,0:T(8,128)(2,1)S(1)}, bf16[512,1024]{1,0:T(8,128)(2,1)}, u32[]{:S(2)}) copy-start(bf16[512,1024]{1,0:T(8,128)(2,1)} %q_ref.13) | copy-start | bytes 3145732
  2.9 20.2 %collective-permute-start = (bf16[528,768]{1,0:T(8,128)(2,1)}, bf16[528,768]{1,0:T(8,128)(2,1)S(1)}, u32[]{:S(2)}, u32[]{:S(2)}) collective-permute-start(bf16[528,768]{1,0:T(8,128)(2,1)} %get-tuple-element.64), channel_id=1, source_target_pairs={{0,8},{4,12},{8,16},{12,20},{16,24},{20,28},{1,9},{5,13},{9,17},{1... | collective-permute-start | bytes 2433032 | tf_op jit(solution)/shard_map/ppermute | solution.py:34
  6.2 22.3 %collective-permute-start.2 = (bf16[528,768]{1,0:T(8,128)(2,1)}, bf16[528,768]{1,0:T(8,128)(2,1)S(1)}, u32[]{:S(2)}, u32[]{:S(2)}) collective-permute-start(bf16[528,768]{1,0:T(8,128)(2,1)} %get-tuple-element.64), channel_id=1, source_target_pairs={{0,4},{8,12},{16,20},{24,28},{1,5},{9,13},{17,21},{25,29},{2,6},{1... | collective-permute-start | bytes 2433032 | tf_op jit(solution)/shard_map/ppermute | solution.py:39
  7.5 0.7 copy-start.6
  8.6 1.2 %copy-start.2 = (bf16[512,1024]{1,0:T(8,128)(2,1)S(1)}, bf16[512,1024]{1,0:T(8,128)(2,1)}, u32[]{:S(2)}) copy-start(bf16[512,1024]{1,0:T(8,128)(2,1)} %refs_3_.5) | copy-start | bytes 3145732
  9.8 3.0 %copy-start.3 = (bf16[512,1024]{1,0:T(8,128)(2,1)S(1)}, bf16[512,1024]{1,0:T(8,128)(2,1)}, u32[]{:S(2)}) copy-start(bf16[512,1024]{1,0:T(8,128)(2,1)} %refs_3_.5) | copy-start | bytes 3145732
  13.3 27.1 %collective-permute-start.4 = (bf16[528,768]{1,0:T(8,128)(2,1)S(1)}, bf16[528,768]{1,0:T(8,128)(2,1)S(1)}, u32[]{:S(2)}, u32[]{:S(2)}) collective-permute-start(bf16[528,768]{1,0:T(8,128)(2,1)S(1)} %get-tuple-element.88), channel_id=1, source_target_pairs={{0,8},{4,12},{8,16},{12,20},{16,24},{20,28},{1,9},{5,13},{9,17},{1... | collective-permute-start | bytes 2433032 | tf_op jit(solution)/shard_map/ppermute | solution.py:34
  16.5 28.3 %collective-permute-start.1 = (bf16[528,1024]{1,0:T(8,128)(2,1)S(1)}, bf16[528,1024]{1,0:T(8,128)(2,1)S(1)}, u32[]{:S(2)}, u32[]{:S(2)}) collective-permute-start(bf16[528,1024]{1,0:T(8,128)(2,1)S(1)} %get-tuple-element.79), channel_id=1, source_target_pairs={{8,0},{12,4},{16,8},{20,12},{24,16},{28,20},{9,1},{13,5},{17,9},{2... | collective-permute-start | bytes 3244040 | tf_op jit(solution)/shard_map/ppermute | solution.py:34
  17.8 40.8 %collective-permute-start.5 = (bf16[544,1280]{1,0:T(8,128)(2,1)S(1)}, bf16[544,1280]{1,0:T(8,128)(2,1)S(1)}, u32[]{:S(2)}, u32[]{:S(2)}) collective-permute-start(bf16[544,1280]{1,0:T(8,128)(2,1)S(1)} %get-tuple-element.89), channel_id=1, source_target_pairs={{0,4},{8,12},{16,20},{24,28},{1,5},{9,13},{17,21},{25,29},{2,6},{1... | collective-permute-start | bytes 4177928 | tf_op jit(solution)/shard_map/ppermute | solution.py:39
  23.2 21.7 %collective-permute-start.3 = (bf16[528,768]{1,0:T(8,128)(2,1)S(1)}, bf16[528,768]{1,0:T(8,128)(2,1)S(1)}, u32[]{:S(2)}, u32[]{:S(2)}) collective-permute-start(bf16[528,768]{1,0:T(8,128)(2,1)S(1)} %collective-permute-done.refs_0_.two), channel_id=1, source_target_pairs={{4,0},{12,8},{20,16},{28,24},{5,1},{13,9},{21,17},{29,25},{6,2},{1... | collective-permute-start | bytes 2433032 | tf_op jit(solution)/shard_map/ppermute | solution.py:44
  28.5 23.9 %collective-permute-start.7 = (bf16[528,512]{1,0:T(8,128)(2,1)S(1)}, bf16[528,512]{1,0:T(8,128)(2,1)S(1)}, u32[]{:S(2)}, u32[]{:S(2)}) collective-permute-start(bf16[528,512]{1,0:T(8,128)(2,1)S(1)} %get-tuple-element.96), channel_id=1, source_target_pairs={{0,8},{4,12},{8,16},{12,20},{16,24},{20,28},{1,9},{5,13},{9,17},{1... | collective-permute-start | bytes 1622024 | tf_op jit(solution)/shard_map/ppermute | solution.py:34
  40.4 18.2 %collective-permute-start.6 = (bf16[528,768]{1,0:T(8,128)(2,1)S(1)}, bf16[528,768]{1,0:T(8,128)(2,1)S(1)}, u32[]{:S(2)}, u32[]{:S(2)}) collective-permute-start(bf16[528,768]{1,0:T(8,128)(2,1)S(1)} %collective-permute-done.4.two), channel_id=1, source_target_pairs={{4,0},{12,8},{20,16},{28,24},{5,1},{13,9},{21,17},{29,25},{6,2},{1... | collective-permute-start | bytes 2433032 | tf_op jit(solution)/shard_map/ppermute | solution.py:44
  52.4 17.0 %collective-permute-start.8 = (bf16[528,512]{1,0:T(8,128)(2,1)S(1)}, bf16[528,512]{1,0:T(8,128)(2,1)S(1)}, u32[]{:S(2)}, u32[]{:S(2)}) collective-permute-start(bf16[528,512]{1,0:T(8,128)(2,1)S(1)} %gate.1.two), channel_id=1, source_target_pairs={{4,0},{12,8},{20,16},{28,24},{5,1},{13,9},{21,17},{29,25},{6,2},{1... | collective-permute-start | bytes 1622024 | tf_op jit(solution)/shard_map/ppermute | solution.py:44
  54.2 24.3 %collective-permute-start.9 = (bf16[400,640]{1,0:T(8,128)(2,1)S(1)}, bf16[400,640]{1,0:T(8,128)(2,1)S(1)}, u32[]{:S(2)}, u32[]{:S(2)}) collective-permute-start(bf16[400,640]{1,0:T(8,128)(2,1)S(1)} %get-tuple-element.103), channel_id=1, source_target_pairs={{0,8},{4,12},{8,16},{12,20},{16,24},{20,28},{1,9},{5,13},{9,17},{1... | collective-permute-start | bytes 1536008 | tf_op jit(solution)/shard_map/ppermute | solution.py:34
  62.1 16.8 %collective-permute-start.10 = (bf16[400,640]{1,0:T(8,128)(2,1)S(1)}, bf16[400,640]{1,0:T(8,128)(2,1)S(1)}, u32[]{:S(2)}, u32[]{:S(2)}) collective-permute-start(bf16[400,640]{1,0:T(8,128)(2,1)S(1)} %get-tuple-element.109), channel_id=1, source_target_pairs={{0,8},{4,12},{8,16},{12,20},{16,24},{20,28},{1,9},{5,13},{9,17},{1... | collective-permute-start | bytes 1536008 | tf_op jit(solution)/shard_map/ppermute | solution.py:34
  71.8 13.3 %collective-permute-start.11 = (bf16[272,640]{1,0:T(8,128)(2,1)S(1)}, bf16[272,640]{1,0:T(8,128)(2,1)S(1)}, u32[]{:S(2)}, u32[]{:S(2)}) collective-permute-start(bf16[272,640]{1,0:T(8,128)(2,1)S(1)} %get-tuple-element.115), channel_id=1, source_target_pairs={{0,8},{4,12},{8,16},{12,20},{16,24},{20,28},{1,9},{5,13},{9,17},{1... | collective-permute-start | bytes 1044488 | tf_op jit(solution)/shard_map/ppermute | solution.py:34
  79.4 15.1 %copy-start.5 = (f32[1024]{0:T(1024)S(1)}, f32[1024]{0:T(1024)}, u32[]{:S(2)}) copy-start(f32[1024]{0:T(1024)} %param.13) | copy-start | bytes 12292

commit v4 on v3

--- a/solution.py
+++ b/solution.py
@@ -128,13 +128,24 @@
     return stack_rows(rows, 16, length).astype(jnp.bfloat16)
 
 
-def first_kernel(n, ld_ref, k_ref, v_ref, pay_ref, token_ref, sems):
-    length = k_ref.shape[0]
-    copies = fetch(pay_ref, k_ref, v_ref, 0, n * 128, sems, 0)
-    fill(pay_ref, decay_rows(running_sums(ld_ref[...]), 0, n), length, length)
-    token_ref[...] = jnp.zeros_like(token_ref)
-    for copy in copies:
-        copy.wait()
+def first_kernel(n, ld_hbm, k_hbm, v_hbm, pay_hbm, token_ref, ld_ref, stage_ref, sems):
+    length = k_hbm.shape[0]
+    half = n * 128
+    decays = pltpu.make_async_copy(ld_hbm, ld_ref, sems.at[0])
+    decays.start()
+    loads = fetch(stage_ref, k_hbm, v_hbm, 0, half, sems, 1)
+    decays.wait()
+    fill(stage_ref, decay_rows(running_sums(ld_ref[...]), 0, n), length, length)
+    stores = [pltpu.make_async_copy(stage_ref.at[length : length + 16, :], pay_hbm.at[length : length + 16, :], sems.at[3])]
+    stores[-1].start()
+    for i in range(2):
+        loads[i].wait()
+        where = (slice(0, length), slice(i * half, (i + 1) * half))
+        stores.append(pltpu.make_async_copy(stage_ref.at[where], pay_hbm.at[where], sems.at[4 + i]))
+        stores[-1].start()
+    token_ref[...] = jnp.zeros_like(token_ref)
+    for store in stores:
+        store.wait()
 
 
 def prep_kernel(
@@ -250,6 +261,40 @@
     token_ref[...] = jnp.zeros_like(token_ref)
 
 
+def partial_softmax(q, groups, thr, scale2):
+    tiles = groups[0][1].shape[0] // BLK
+    row = lax.broadcasted_iota(jnp.int32, (BLK, q.shape[0]), 0)
+    parts = []
+    for first, keys, _ in groups:
+        scores = dot(keys, q, NT)
+        for j in range(tiles):
+            ok = row >= thr[first + j : first + j + 1]
+            parts.append(jnp.where(ok, scores[j * BLK : (j + 1) * BLK], NEG))
+    top, total, weights = softmax_of(parts, scale2)
+    o = None
+    for g, (_, _, values) in enumerate(groups):
+        here = dot(values, jnp.concatenate(weights[g * tiles : (g + 1) * tiles], axis=0), TN)
+        o = here if o is None else o + here
+    return top, total, o
+
+
+def earlier_kernel(scale2, n, token_in, q_ref, thr_ref, two, od_ref, topd_ref, totd_ref, o_ref, top_ref, tot_ref, token_ref):
+    length = q_ref.shape[0]
+    thr = thr_ref[...]
+    for i in range(n):
+        rows = slice(i * 128, (i + 1) * 128)
+        keys = two[0:length, i * 128 : (i + 1) * 128]
+        values = two[0:length, (n + i) * 128 : (n + i + 1) * 128]
+        top, total, o = partial_softmax(q_ref[:, rows], [(0, keys, values)], thr, scale2)
+        top_d = topd_ref[i : i + 1, :]
+        new_top = jnp.maximum(top, top_d)
+        a, b = jnp.exp2(top - new_top), jnp.exp2(top_d - new_top)
+        o_ref[rows, :] = o * a + od_ref[rows, :] * b
+        top_ref[i : i + 1, :] = new_top
+        tot_ref[i : i + 1, :] = total * a + totd_ref[i : i + 1, :] * b
+    token_ref[...] = jnp.zeros_like(token_ref)
+
+
 class Pieces:
     def __init__(self, n, two, even, odd, entry, even_at, even_dec):
         self.n, self.two, self.even, self.odd, self.even_at = n, two, even, odd, even_at
@@ -270,19 +315,12 @@
         at = slice(self.even_at + index * 128, self.even_at + (index + 1) * 128)
         return self.two[0 : self.length, cols], self.even[0 : self.length, at] + self.odd[0 : self.length, cols]
 
-    def attend(self, i, q, thr, scale2):
+    def attend(self, i, q, thr, scale2, both=True):
         tiles = self.length // BLK
         k2, k1 = self.part(i)
         v2, v1 = self.part(self.n + i)
-        row = lax.broadcasted_iota(jnp.int32, (BLK, q.shape[0]), 0)
-        parts = []
-        for first, keys in ((0, k2), (tiles, k1)):
-            scores = dot(keys, q, NT)
-            for j in range(tiles):
-                ok = row >= thr[first + j : first + j + 1]
-                parts.append(jnp.where(ok, scores[j * BLK : (j + 1) * BLK], NEG))
-        top, total, weights = softmax_of(parts, scale2)
-        o = dot(v2, jnp.concatenate(weights[:tiles], axis=0), TN) + dot(v1, jnp.concatenate(weights[tiles:], axis=0), TN)
+        groups = [(0, k2, v2), (tiles, k1, v1)] if both else [(tiles, k1, v1)]
+        top, total, o = partial_softmax(q, groups, thr, scale2)
         n = self.n
         kw1 = (k1.astype(jnp.float32) * self.weight[:, i : i + 1]).astype(jnp.bfloat16)
         kw2 = (k2.astype(jnp.float32) * self.weight[:, n + i : n + i + 1]).astype(jnp.bfloat16)
@@ -290,19 +328,43 @@
         return top, total, o, state.astype(jnp.bfloat16)
 
 
-def far_kernel(scale2, n, even_at, even_dec, token_in, entry_ref, q_ref, keep_ref, ahead_ref, two, even, odd, out_ref, token_ref):
-    p = Pieces(n, two, even, odd, entry_ref[0:1, :], even_at, even_dec)
-    length = p.length
+def far_thresholds(keep_ref, ahead_ref):
     keep = keep_ref[...].astype(jnp.float32)
-    tiles = length // BLK
+    tiles = keep.shape[1] // BLK
     thr = []
     for j in range(2 * tiles):
         base = (j - REACH * tiles) * BLK
         thr.append(jnp.where(keep[j : j + 1] > 0.5, ahead_ref[0:1, :] - base, FAR_OFF))
-    thr = jnp.concatenate(thr, axis=0)
+    return jnp.concatenate(thr, axis=0)
+
+
+def far_earlier_kernel(scale2, n, token_in, q_ref, keep_ref, ahead_ref, two, o_ref, top_ref, tot_ref, token_ref):
+    thr = far_thresholds(keep_ref, ahead_ref)
+    length = thr.shape[1]
+    for i in range(n):
+        rows = slice(i * 128, (i + 1) * 128)
+        keys = two[0:length, i * 128 : (i + 1) * 128]
+        values = two[0:length, (n + i) * 128 : (n + i + 1) * 128]
+        top, total, o = partial_softmax(q_ref[0:length, rows], [(0, keys, values)], thr, scale2)
+        o_ref[rows, :] = o
+        top_ref[i : i + 1, :] = top
+        tot_ref[i : i + 1, :] = total
+    token_ref[...] = jnp.zeros_like(token_ref)
+
+
+def far_kernel(scale2, n, both, even_at, even_dec, token_in, entry_ref, q_ref, keep_ref, ahead_ref, two, even, odd, *rest):
+    out_ref, token_ref = rest[-2:]
+    p = Pieces(n, two, even, odd, entry_ref[0:1, :], even_at, even_dec)
+    length = p.length
+    thr = far_thresholds(keep_ref, ahead_ref)
     rows = [jnp.ones((1, length), jnp.float32)]
     for i in range(n):
-        top, total, o, state = p.attend(i, q_ref[0:length, i * 128 : (i + 1) * 128], thr, scale2)
+        top, total, o, state = p.attend(i, q_ref[0:length, i * 128 : (i + 1) * 128], thr, scale2, both)
+        if not both:
+            o_e, top_e, tot_e = rest[0][i * 128 : (i + 1) * 128, :], rest[1][i : i + 1, :], rest[2][i : i + 1, :]
+            new_top = jnp.maximum(top, top_e)
+            a, b = jnp.exp2(top - new_top), jnp.exp2(top_e - new_top)
+            top, total, o = new_top, total * a + tot_e * b, o * a + o_e * b
         r = i * 128
         out_ref[r : r + 128, 0:length] = (o * (1.0 / total)).astype(jnp.bfloat16)
         out_ref[r : r + 128, length:] = state
@@ -314,7 +376,7 @@
 
 
 def near_kernel(
-    scale2, n, first, even_at, even_dec, token_in, entry_ref, q_ref, thr_ref, coef_ref, two, even, odd, od_ref, topd_ref, totd_ref, lind_ref,
+    scale2, n, first, both, even_at, even_dec, token_in, entry_ref, q_ref, thr_ref, coef_ref, two, even, odd, od_ref, topd_ref, totd_ref, lind_ref,
     x_ref, on_ref, st_ref, token_ref,
 ):
     entry = entry_ref[0:1, :]
@@ -325,7 +387,7 @@
     for i in range(n):
         q = q_ref[:, i * 128 : (i + 1) * 128]
         rows = slice(i * 128, (i + 1) * 128)
-        top, total, o, state = p.attend(i, q, thr, scale2)
+        top, total, o, state = p.attend(i, q, thr, scale2, both)
         top_d = topd_ref[i : i + 1, :]
         new_top = jnp.maximum(top, top_d)
         a, b = jnp.exp2(top - new_top), jnp.exp2(top_d - new_top)
@@ -394,9 +456,9 @@
     def cols(c, rows=length):
         return pl.BlockSpec((rows, sizes[c] * hd), lambda *_: (0, firsts[c] // sizes[c]))
 
-    def run(kernel, name, us, specs, args, outs, scratch=(), limit=24):
+    def run(kernel, name, us, specs, args, outs, scratch=(), limit=24, out_specs=None):
         outs = outs + [shape((8, 128), f32)]
-        out_specs = [whole(o) for o in outs]
+        out_specs = (out_specs or [whole(o) for o in outs[:-1]]) + [whole(outs[-1])]
         return pl.pallas_call(
             kernel,
             grid=(1,),
@@ -428,11 +490,12 @@
         partial(first_kernel, sizes[0]),
         "first_chunk",
         1,
-        [whole(log_decay), hbm, hbm],
+        [hbm, hbm, hbm],
         (log_decay, key, value),
         [pay_shape(0)],
-        [dma((2,))],
+        [pltpu.VMEM(log_decay.shape, f32), pltpu.VMEM(pay_shape(0).shape, bf16), dma((6,))],
         limit=60,
+        out_specs=[hbm],
     )
     thr, start, ahead, entry, keep, cum, cum_t, coef, dec, token = run(
         partial(prep_kernel, divisor, sizes),
@@ -474,7 +537,7 @@
         n = sizes[c]
         args = (*kv(c), *diag[c])
         x, on, st, token = run(
-            partial(near_kernel, scale2, n, firsts[c], *even_place(c)),
+            partial(near_kernel, scale2, n, firsts[c], c != 1, *even_place(c)),
             "near_pieces",
             1.8 * n,
             [loose, whole(entry), cols(c), thr_near, whole(coef)] + [whole(a) for a in args],
@@ -483,15 +546,43 @@
         )
         return (x, on, st), token
 
-    def far(c, token):
+    def earlier(c, token):
         n = sizes[c]
-        kept = pl.BlockSpec((16, length), lambda *_: (length // 16, 0))
+        args = (two_back[c], *diag[c][:3])
+        o, top, tot, token = run(
+            partial(earlier_kernel, scale2, n),
+            "earlier_piece",
+            0.8 * n,
+            [loose, cols(c), thr_near] + [whole(a) for a in args],
+            (token, query, thr, *args),
+            [shape((n * hd, length), f32), shape((n, length), f32), shape((n, length), f32)],
+        )
+        diag[c] = [o, top, tot, diag[c][3]]
+        return token
+
+    kept = pl.BlockSpec((16, length), lambda *_: (length // 16, 0))
+
+    def far_earlier(c, token):
+        n = sizes[c]
+        *first, token = run(
+            partial(far_earlier_kernel, scale2, n),
+            "far_earlier",
+            0.7 * n,
+            [loose, cols(c), kept, whole(ahead), whole(two_back[c])],
+            (token, q_far, q_far, ahead, two_back[c]),
+            [shape((n * hd, length), f32), shape((n, length), f32), shape((n, length), f32)],
+        )
+        return first, token
+
+    def far(c, token, first=()):
+        n = sizes[c]
+        args = (*kv(c), *first)
         pay, token = run(
-            partial(far_kernel, scale2, n, *even_place(c)),
+            partial(far_kernel, scale2, n, not first, *even_place(c)),
             "far_pieces",
             1.5 * n,
-            [loose, whole(entry), cols(c), kept, whole(ahead)] + [whole(a) for a in kv(c)],
-            (token, entry, q_far, q_far, ahead, *kv(c)),
+            [loose, whole(entry), cols(c), kept, whole(ahead)] + [whole(a) for a in args],
+            (token, entry, q_far, q_far, ahead, *args),
             [shape((n * hd + 16, length + hd), bf16)],
         )
         return shifted(pay, 2), token
@@ -550,7 +641,9 @@
     parts[0], token = near(0, token)
     two_back[2] = gate(two_back[2], token)
     from_odd[2] = odd_to_even(two_back[2])
-    pays[1], token = far(1, token)
+    first, token = far_earlier(1, token)
+    token = earlier(1, token)
+    pays[1], token = far(1, token, first)
     parts[1], token = near(1, token)
     pays[2], token = far(2, token)
     parts[2], token = near(2, token)

time: 97.6 us -> 97.2 us (level)
  blocking collectives: 8.4 us -> 7.19 us
  Pallas kernels: 35.5 us -> 36.5 us
    all_gather x1, blocking collectives: 8.4 us -> 7.19 us  [on_device(): lax.all_gather(total.reshape(length // 128, 128), 'head')]
    pallas_call x16 -> x18, Pallas kernels: 33.9 us -> 34.9 us  [run(): pl.pallas_call(kernel, grid=(1,), in_specs=specs, out_specs=out_specs, ou...]
  transfers between devices with their start and end apart: 12 -> 12, of which waited for: 3 -> 3; matrix products, arithmetic and copies ran while one was open for 0% -> 0% of each run, Pallas kernels for 31% -> 33%
where the time goes in v4:
time: 97.2 us; the launch traced here: 95.8 us
  Pallas kernels  36.5 us (38%)
  starting transfers between devices  31.8 us (33%)
  waiting for transfers between devices  18 us (19%)
  blocking collectives  7.19 us (7%)
  local copies, waits for them, and re-layouts  1.92 us (2%)
    pallas_call x18, Pallas kernels, run(): pl.pallas_call(kernel, grid=(1,), in_specs=specs, out_specs=out_specs, ou...  34.9 us
    ppermute x7, starting transfers between devices, shifted(): lax.ppermute(x, 'ctx', [(i, i + by) for i in range(n) if 0 <= i + by < n])  22.8 us
    ppermute x7, waiting for transfers between devices, shifted(): lax.ppermute(x, 'ctx', [(i, i + by) for i in range(n) if 0 <= i + by < n])  18 us
    all_gather x1, blocking collectives, on_device(): lax.all_gather(total.reshape(length // 128, 128), 'head')  7.19 us
    ppermute x3, starting transfers between devices, odd_to_even(): return lax.ppermute(x, 'ctx', [(i, i - 1) for i in range(1, n, 2)])  6.42 us
    ppermute x2, starting transfers between devices, even_to_odd(): return lax.ppermute(x, 'ctx', [(i, i + 1) for i in range(0, n - 1, 2)])  2.58 us
  transfers between devices with their start and end apart: 12, of which 3 were waited for; matrix products, arithmetic and copies ran while one was open for 0% of the time, Pallas kernels for 33%

profile of v4, /device:TPU:3, one launch (start us, length us, event | category | flops | bytes accessed | tf_op | source)
XLA Modules:
  0.0 95.8 jit_solution(16292730963736451262)
XLA Ops:
  0.0 0.0 copy-start.4
  0.0 0.0 copy-start.1
  0.0 0.0 copy-start.8
  0.0 0.0 copy-start.7
  0.0 0.0 copy-start
  0.0 2.7 %first_chunk.1 = (bf16[528,768]{1,0:T(8,128)(2,1)}, f32[8,128]{1,0:T(8,128)}) custom-call(f32[8,512]{1,0:T(8,128)} %ld_ref.1, bf16[512,1024]{1,0:T(8,128)(2,1)} %refs_2_.5, bf16[512,1024]{1,0:T(8,128)(2,1)} %refs_3_.5), custom_call_target="tpu_custom_call" | custom-call | bytes 3690000 | tf_op jit(solution)/shard_map/first_chunk/pallas_call | solution.py:462
  2.7 3.3 %collective-permute-start = (bf16[528,768]{1,0:T(8,128)(2,1)}, bf16[528,768]{1,0:T(8,128)(2,1)S(1)}, u32[]{:S(2)}, u32[]{:S(2)}) collective-permute-start(bf16[528,768]{1,0:T(8,128)(2,1)} %get-tuple-element.72), channel_id=1, source_target_pairs={{0,8},{4,12},{8,16},{12,20},{16,24},{20,28},{1,9},{5,13},{9,17},{1... | collective-permute-start | bytes 2433032 | tf_op jit(solution)/shard_map/ppermute | solution.py:34
  6.0 1.3 %collective-permute-start.2 = (bf16[528,768]{1,0:T(8,128)(2,1)}, bf16[528,768]{1,0:T(8,128)(2,1)S(1)}, u32[]{:S(2)}, u32[]{:S(2)}) collective-permute-start(bf16[528,768]{1,0:T(8,128)(2,1)} %get-tuple-element.72), channel_id=1, source_target_pairs={{0,4},{8,12},{16,20},{24,28},{1,5},{9,13},{17,21},{25,29},{2,6},{1... | collective-permute-start | bytes 2433032 | tf_op jit(solution)/shard_map/ppermute | solution.py:39
  7.3 0.0 copy-done.4
  7.3 0.0 copy-done.8
  7.3 0.0 copy-done.7
  7.3 0.0 copy-start.6
  7.3 0.7 copy-done.6
  8.0 0.4 prep.1
  8.4 0.0 copy-done.1
  8.4 0.0 copy-done
  8.4 0.0 copy-start.2
  8.4 1.2 %copy-done.2 = bf16[512,1024]{1,0:T(8,128)(2,1)S(1)} copy-done((bf16[512,1024]{1,0:T(8,128)(2,1)S(1)}, bf16[512,1024]{1,0:T(8,128)(2,1)}, u32[]{:S(2)}) %copy-start.2) | copy-done | bytes 1048600
  9.6 0.0 copy-start.3
  9.6 3.0 %own_piece.3 = (f32[384,512]{1,0:T(8,128)S(1)}, f32[3,512]{1,0:T(4,128)S(1)}, f32[3,512]{1,0:T(4,128)S(1)}, f32[384,512]{1,0:T(8,128)S(1)}, f32[8,128]{1,0:T(8,128)S(1)}) custom-call(f32[8,128]{1,0:T(8,128)S(1)} %get-tuple-element.74.refs_0_, bf16[512,1024]{1,0:T(8,128)(2,1)S(1)} %copy-done, bf16[512,1024]{1,0:T(8,128)(2,1)S(1)} %copy-done.1, ...), custom_call_target="tpu_custom_call" | custom-call | bytes 8856000 | tf_op jit(solution)/shard_map/own_piece/pallas_call | solution.py:462
  12.6 0.0 copy-done.3
  12.6 0.4 pack.2
  13.1 3.2 %collective-permute-start.4 = (bf16[528,768]{1,0:T(8,128)(2,1)S(1)}, bf16[528,768]{1,0:T(8,128)(2,1)S(1)}, u32[]{:S(2)}, u32[]{:S(2)}) collective-permute-start(bf16[528,768]{1,0:T(8,128)(2,1)S(1)} %get-tuple-element.96), channel_id=1, source_target_pairs={{0,8},{4,12},{8,16},{12,20},{16,24},{20,28},{1,9},{5,13},{9,17},{1... | collective-permute-start | bytes 2433032 | tf_op jit(solution)/shard_map/ppermute | solution.py:34
  16.3 1.3 %collective-permute-start.1 = (bf16[528,1024]{1,0:T(8,128)(2,1)S(1)}, bf16[528,1024]{1,0:T(8,128)(2,1)S(1)}, u32[]{:S(2)}, u32[]{:S(2)}) collective-permute-start(bf16[528,1024]{1,0:T(8,128)(2,1)S(1)} %get-tuple-element.87), channel_id=1, source_target_pairs={{8,0},{12,4},{16,8},{20,12},{24,16},{28,20},{9,1},{13,5},{17,9},{2... | collective-permute-start | bytes 3244040 | tf_op jit(solution)/shard_map/ppermute | solution.py:34
  17.6 1.3 %collective-permute-start.5 = (bf16[544,1280]{1,0:T(8,128)(2,1)S(1)}, bf16[544,1280]{1,0:T(8,128)(2,1)S(1)}, u32[]{:S(2)}, u32[]{:S(2)}) collective-permute-start(bf16[544,1280]{1,0:T(8,128)(2,1)S(1)} %get-tuple-element.102), channel_id=1, source_target_pairs={{0,4},{8,12},{16,20},{24,28},{1,5},{9,13},{17,21},{25,29},{2,6},{1... | collective-permute-start | bytes 4177928 | tf_op jit(solution)/shard_map/ppermute | solution.py:39
  18.9 4.1 %collective-permute-done.refs_0_.two = bf16[528,768]{1,0:T(8,128)(2,1)S(1)} collective-permute-done((bf16[528,768]{1,0:T(8,128)(2,1)}, bf16[528,768]{1,0:T(8,128)(2,1)S(1)}, u32[]{:S(2)}, u32[]{:S(2)}) %collective-permute-start) | collective-permute-done | bytes 811040 | tf_op jit(solution)/shard_map/ppermute | solution.py:34
  23.0 2.2 %collective-permute-start.3 = (bf16[528,768]{1,0:T(8,128)(2,1)S(1)}, bf16[528,768]{1,0:T(8,128)(2,1)S(1)}, u32[]{:S(2)}, u32[]{:S(2)}) collective-permute-start(bf16[528,768]{1,0:T(8,128)(2,1)S(1)} %collective-permute-done.refs_0_.two), channel_id=1, source_target_pairs={{4,0},{12,8},{20,16},{28,24},{5,1},{13,9},{21,17},{29,25},{6,2},{1... | collective-permute-start | bytes 2433032 | tf_op jit(solution)/shard_map/ppermute | solution.py:44
  25.2 3.0 %own_piece.4 = (f32[384,512]{1,0:T(8,128)S(1)}, f32[3,512]{1,0:T(4,128)S(1)}, f32[3,512]{1,0:T(4,128)S(1)}, f32[384,512]{1,0:T(8,128)S(1)}, f32[8,128]{1,0:T(8,128)S(1)}) custom-call(bf16[528,768]{1,0:T(8,128)(2,1)S(1)} %collective-permute-done.refs_0_.two, f32[8,128]{1,0:T(8,128)S(1)} %get-tuple-element.82.refs_1_, bf16[512,1024]{1,0:T(8,128)(2,1)S(1)} %copy-done, ...), custom_call_target="tpu_custom_call" | custom-call | bytes 8856000 | tf_op jit(solution)/shard_map/own_piece/pallas_call | solution.py:462
  28.2 0.1 pack.3
  28.3 0.0 collective-permute-done.2.even
  28.3 4.0 %collective-permute-start.7 = (bf16[528,512]{1,0:T(8,128)(2,1)S(1)}, bf16[528,512]{1,0:T(8,128)(2,1)S(1)}, u32[]{:S(2)}, u32[]{:S(2)}) collective-permute-start(bf16[528,512]{1,0:T(8,128)(2,1)S(1)} %get-tuple-element.112), channel_id=1, source_target_pairs={{0,8},{4,12},{8,16},{12,20},{16,24},{20,28},{1,9},{5,13},{9,17},{1... | collective-permute-start | bytes 1622024 | tf_op jit(solution)/shard_map/ppermute | solution.py:34
  32.3 7.9 %collective-permute-done.4.two = bf16[528,768]{1,0:T(8,128)(2,1)S(1)} collective-permute-done((bf16[528,768]{1,0:T(8,128)(2,1)S(1)}, bf16[528,768]{1,0:T(8,128)(2,1)S(1)}, u32[]{:S(2)}, u32[]{:S(2)}) %collective-permute-start.4) | collective-permute-done | bytes 811040 | tf_op jit(solution)/shard_map/ppermute | solution.py:34
  40.2 2.4 %collective-permute-start.6 = (bf16[528,768]{1,0:T(8,128)(2,1)S(1)}, bf16[528,768]{1,0:T(8,128)(2,1)S(1)}, u32[]{:S(2)}, u32[]{:S(2)}) collective-permute-start(bf16[528,768]{1,0:T(8,128)(2,1)S(1)} %collective-permute-done.4.two), channel_id=1, source_target_pairs={{4,0},{12,8},{20,16},{28,24},{5,1},{13,9},{21,17},{29,25},{6,2},{1... | collective-permute-start | bytes 2433032 | tf_op jit(solution)/shard_map/ppermute | solution.py:44
  42.6 2.0 %own_piece.5 = (f32[256,512]{1,0:T(8,128)S(1)}, f32[2,512]{1,0:T(2,128)S(1)}, f32[2,512]{1,0:T(2,128)S(1)}, f32[256,512]{1,0:T(8,128)S(1)}, f32[8,128]{1,0:T(8,128)S(1)}) custom-call(f32[8,128]{1,0:T(8,128)S(1)} %get-tuple-element.84.refs_0_, bf16[512,1024]{1,0:T(8,128)(2,1)S(1)} %copy-done, bf16[512,1024]{1,0:T(8,128)(2,1)S(1)} %copy-done.1, ...), custom_call_target="tpu_custom_call" | custom-call | bytes 5904000 | tf_op jit(solution)/shard_map/own_piece/pallas_call | solution.py:462
  44.6 0.0 collective-permute-done.1.q_ref.keep_ref
  44.6 0.0 collective-permute-done.3.odd
  44.6 3.5 %far_pieces.3 = (bf16[400,640]{1,0:T(8,128)(2,1)S(1)}, f32[8,128]{1,0:T(8,128)S(1)}) custom-call(f32[8,128]{1,0:T(8,128)S(1)} %get-tuple-element.85.token_in, s32[8,512]{1,0:T(8,128)S(1)} %get-tuple-element.86.entry_ref, bf16[528,1024]{1,0:T(8,128)(2,1)S(1)} %collective-permute-done.1.q_ref.keep_ref, ...), custom_call_target="tpu_custom_call" | custom-call | bytes 16605000 | tf_op jit(solution)/shard_map/far_pieces/pallas_call | solution.py:462
  48.1 4.0 %near_pieces.3 = (f32[384,512]{1,0:T(8,128)S(1)}, f32[384,512]{1,0:T(8,128)S(1)}, f32[8,512]{1,0:T(8,128)S(1)}, f32[8,128]{1,0:T(8,128)S(1)}) custom-call(f32[8,128]{1,0:T(8,128)S(1)} %get-tuple-element.89.token_in, s32[8,512]{1,0:T(8,128)S(1)} %get-tuple-element.86.entry_ref, bf16[512,1024]{1,0:T(8,128)(2,1)S(1)} %copy-done, ...), custom_call_target="tpu_custom_call" | custom-call | bytes 19926000 | tf_op jit(solution)/shard_map/near_pieces/pallas_call | solution.py:462
  52.1 0.0 collective-permute-done.7.refs_0_
  52.2 1.8 %collective-permute-start.8 = (bf16[528,512]{1,0:T(8,128)(2,1)S(1)}, bf16[528,512]{1,0:T(8,128)(2,1)S(1)}, u32[]{:S(2)}, u32[]{:S(2)}) collective-permute-start(bf16[528,512]{1,0:T(8,128)(2,1)S(1)} %gate.1.two), channel_id=1, source_target_pairs={{4,0},{12,8},{20,16},{28,24},{5,1},{13,9},{21,17},{29,25},{6,2},{1... | collective-permute-start | bytes 1622024 | tf_op jit(solution)/shard_map/ppermute | solution.py:44
  54.0 4.4 %collective-permute-start.9 = (bf16[400,640]{1,0:T(8,128)(2,1)S(1)}, bf16[400,640]{1,0:T(8,128)(2,1)S(1)}, u32[]{:S(2)}, u32[]{:S(2)}) collective-permute-start(bf16[400,640]{1,0:T(8,128)(2,1)S(1)} %get-tuple-element.119), channel_id=1, source_target_pairs={{0,8},{4,12},{8,16},{12,20},{16,24},{20,28},{1,9},{5,13},{9,17},{1... | collective-permute-start | bytes 1536008 | tf_op jit(solution)/shard_map/ppermute | solution.py:34
  58.4 1.9 %far_earlier.1 = (f32[384,512]{1,0:T(8,128)S(1)}, f32[3,512]{1,0:T(4,128)S(1)}, f32[3,512]{1,0:T(4,128)S(1)}, f32[8,128]{1,0:T(8,128)S(1)}) custom-call(f32[8,128]{1,0:T(8,128)S(1)} %get-tuple-element.95.token_in.refs_1_, bf16[528,1024]{1,0:T(8,128)(2,1)S(1)} %collective-permute-done.1.q_ref.keep_ref, ...), custom_call_target="tpu_custom_call" | custom-call | bytes 7748999 | tf_op jit(solution)/shard_map/far_earlier/pallas_call | solution.py:462
  60.3 1.9 %earlier_piece.1 = (f32[384,512]{1,0:T(8,128)S(1)}, f32[3,512]{1,0:T(4,128)S(1)}, f32[3,512]{1,0:T(4,128)S(1)}, f32[8,128]{1,0:T(8,128)S(1)}) custom-call(f32[8,128]{1,0:T(8,128)S(1)} %get-tuple-element.97.token_in, bf16[512,1024]{1,0:T(8,128)(2,1)S(1)} %copy-done, s32[20,512]{1,0:T(8,128)S(1)} %get-tuple-element.75.refs_4_.refs_5_.thr_ref, ...), custom_call_target="tpu_custom_call" | custom-call | bytes 8856000 | tf_op jit(solution)/shard_map/earlier_piece/pallas_call | solution.py:462
  62.2 0.0 collective-permute-done.5.even
  62.2 0.0 collective-permute-done.6.odd
  62.2 2.3 %far_pieces.4 = (bf16[400,640]{1,0:T(8,128)(2,1)S(1)}, f32[8,128]{1,0:T(8,128)S(1)}) custom-call(f32[8,128]{1,0:T(8,128)S(1)} %get-tuple-element.101.token_in, s32[8,512]{1,0:T(8,128)S(1)} %get-tuple-element.86.entry_ref, bf16[528,1024]{1,0:T(8,128)(2,1)S(1)} %collective-permute-done.1.q_ref.keep_ref, ...), custom_call_target="tpu_custom_call" | custom-call | bytes 16605000 | tf_op jit(solution)/shard_map/far_pieces/pallas_call | solution.py:462
  64.5 3.2 %collective-permute-start.10 = (bf16[400,640]{1,0:T(8,128)(2,1)S(1)}, bf16[400,640]{1,0:T(8,128)(2,1)S(1)}, u32[]{:S(2)}, u32[]{:S(2)}) collective-permute-start(bf16[400,640]{1,0:T(8,128)(2,1)S(1)} %get-tuple-element.125), channel_id=1, source_target_pairs={{0,8},{4,12},{8,16},{12,20},{16,24},{20,28},{1,9},{5,13},{9,17},{1... | collective-permute-start | bytes 1536008 | tf_op jit(solution)/shard_map/ppermute | solution.py:34
  67.7 2.7 %near_pieces.4 = (f32[384,512]{1,0:T(8,128)S(1)}, f32[384,512]{1,0:T(8,128)S(1)}, f32[8,512]{1,0:T(8,128)S(1)}, f32[8,128]{1,0:T(8,128)S(1)}) custom-call(f32[8,128]{1,0:T(8,128)S(1)} %get-tuple-element.106.token_in, s32[8,512]{1,0:T(8,128)S(1)} %get-tuple-element.86.entry_ref, bf16[512,1024]{1,0:T(8,128)(2,1)S(1)} %copy-done, ...), custom_call_target="tpu_custom_call" | custom-call | bytes 19926000 | tf_op jit(solution)/shard_map/near_pieces/pallas_call | solution.py:462
  70.5 0.0 collective-permute-done.8.odd
  70.5 2.5 %far_pieces.5 = (bf16[272,640]{1,0:T(8,128)(2,1)S(1)}, f32[8,128]{1,0:T(8,128)S(1)}) custom-call(f32[8,128]{1,0:T(8,128)S(1)} %get-tuple-element.111.token_in, s32[8,512]{1,0:T(8,128)S(1)} %get-tuple-element.86.entry_ref, bf16[528,1024]{1,0:T(8,128)(2,1)S(1)} %collective-permute-done.1.q_ref.keep_ref, ...), custom_call_target="tpu_custom_call" | custom-call | bytes 11070000 | tf_op jit(solution)/shard_map/far_pieces/pallas_call | solution.py:462
  72.9 3.5 %collective-permute-start.11 = (bf16[272,640]{1,0:T(8,128)(2,1)S(1)}, bf16[272,640]{1,0:T(8,128)(2,1)S(1)}, u32[]{:S(2)}, u32[]{:S(2)}) collective-permute-start(bf16[272,640]{1,0:T(8,128)(2,1)S(1)} %get-tuple-element.131), channel_id=1, source_target_pairs={{0,8},{4,12},{8,16},{12,20},{16,24},{20,28},{1,9},{5,13},{9,17},{1... | collective-permute-start | bytes 1044488 | tf_op jit(solution)/shard_map/ppermute | solution.py:34
  76.4 2.9 %near_pieces.5 = (f32[256,512]{1,0:T(8,128)S(1)}, f32[256,512]{1,0:T(8,128)S(1)}, f32[8,512]{1,0:T(8,128)S(1)}, f32[8,128]{1,0:T(8,128)S(1)}) custom-call(f32[8,128]{1,0:T(8,128)S(1)} %get-tuple-element.113.token_in, s32[8,512]{1,0:T(8,128)S(1)} %get-tuple-element.86.entry_ref, bf16[512,1024]{1,0:T(8,128)(2,1)S(1)} %copy-done, ...), custom_call_target="tpu_custom_call" | custom-call | bytes 13284000 | tf_op jit(solution)/shard_map/near_pieces/pallas_call | solution.py:462
  79.3 0.0 collective-permute-done.9.pay_ref
  79.3 0.4 merge.3
  79.7 0.0 collective-permute-done.10.pay_ref
  79.7 0.4 merge.4
  80.1 0.0 copy-start.5
  80.1 6.0 %collective-permute-done.11.pay_ref = bf16[272,640]{1,0:T(8,128)(2,1)S(1)} collective-permute-done((bf16[272,640]{1,0:T(8,128)(2,1)S(1)}, bf16[272,640]{1,0:T(8,128)(2,1)S(1)}, u32[]{:S(2)}, u32[]{:S(2)}) %collective-permute-start.11) | collective-permute-done | bytes 348192 | tf_op jit(solution)/shard_map/ppermute | solution.py:34
  86.2 0.9 merge.5
  87.0 7.2 %all_gather.3 = f32[4,4,128]{2,1,0:T(4,128)S(1)} all-gather(f32[1,4,128]{2,1,0:T(4,128)S(1)} %bitcast.11), channel_id=1, replica_groups=mesh['ctx'=8,'head'=4] {'head'}, dimensions={0}, use_global_device_ids=true | all-gather | bytes 10240 | tf_op jit(solution)/shard_map/all_gather | solution.py:656
  94.2 0.0 copy-done.5
  94.2 1.6 %normalize.1 = bf16[512,1024]{1,0:T(8,128)(2,1)} custom-call(f32[384,512]{1,0:T(8,128)S(1)} %get-tuple-element.123.refs_0_, f32[384,512]{1,0:T(8,128)S(1)} %get-tuple-element.129.refs_1_, f32[256,512]{1,0:T(8,128)S(1)} %get-tuple-element.135.refs_2_, f32[4,512]{1,0:T(4,128)S(1)} %bitcast.7, f32[1,1024]{1,0:T(1,128)S(1)} %bitcast.8), custom_call_target="tpu_custom_call" | custom-call | tf_op jit(solution)/shard_map/normalize/pallas_call | solution.py:658
  (3 shorter events, 0.0 us)
Async XLA Ops:
  0.0 7.3 %copy-start.4 = (f32[8,512]{1,0:T(8,128)S(1)}, f32[8,512]{1,0:T(8,128)}, u32[]{:S(2)}) copy-start(f32[8,512]{1,0:T(8,128)} %ld_ref.1) | copy-start | bytes 49156
  0.0 8.4 %copy-start.1 = (bf16[512,1024]{1,0:T(8,128)(2,1)S(1)}, bf16[512,1024]{1,0:T(8,128)(2,1)}, u32[]{:S(2)}) copy-start(bf16[512,1024]{1,0:T(8,128)(2,1)} %refs_2_.5) | copy-start | bytes 3145732
  0.0 7.3 %copy-start.8 = (s32[8]{0:T(128)S(1)}, s32[8]{0:T(128)}, u32[]{:S(2)}) copy-start(s32[8]{0:T(128)} %param.11) | copy-start | bytes 100
  0.0 7.3 %copy-start.7 = (s32[4,20]{1,0:T(4,128)S(1)}, s32[4,20]{1,0:T(4,128)}, u32[]{:S(2)}) copy-start(s32[4,20]{1,0:T(4,128)} %mask_ref.1) | copy-start | bytes 964
  0.0 8.4 %copy-start = (bf16[512,1024]{1,0:T(8,128)(2,1)S(1)}, bf16[512,1024]{1,0:T(8,128)(2,1)}, u32[]{:S(2)}) copy-start(bf16[512,1024]{1,0:T(8,128)(2,1)} %q_ref.15) | copy-start | bytes 3145732
  2.7 20.2 %collective-permute-start = (bf16[528,768]{1,0:T(8,128)(2,1)}, bf16[528,768]{1,0:T(8,128)(2,1)S(1)}, u32[]{:S(2)}, u32[]{:S(2)}) collective-permute-start(bf16[528,768]{1,0:T(8,128)(2,1)} %get-tuple-element.72), channel_id=1, source_target_pairs={{0,8},{4,12},{8,16},{12,20},{16,24},{20,28},{1,9},{5,13},{9,17},{1... | collective-permute-start | bytes 2433032 | tf_op jit(solution)/shard_map/ppermute | solution.py:34
  6.0 22.3 %collective-permute-start.2 = (bf16[528,768]{1,0:T(8,128)(2,1)}, bf16[528,768]{1,0:T(8,128)(2,1)S(1)}, u32[]{:S(2)}, u32[]{:S(2)}) collective-permute-start(bf16[528,768]{1,0:T(8,128)(2,1)} %get-tuple-element.72), channel_id=1, source_target_pairs={{0,4},{8,12},{16,20},{24,28},{1,5},{9,13},{17,21},{25,29},{2,6},{1... | collective-permute-start | bytes 2433032 | tf_op jit(solution)/shard_map/ppermute | solution.py:39
  7.3 0.7 copy-start.6
  8.4 1.2 %copy-start.2 = (bf16[512,1024]{1,0:T(8,128)(2,1)S(1)}, bf16[512,1024]{1,0:T(8,128)(2,1)}, u32[]{:S(2)}) copy-start(bf16[512,1024]{1,0:T(8,128)(2,1)} %refs_3_.5) | copy-start | bytes 3145732
  9.6 3.0 %copy-start.3 = (bf16[512,1024]{1,0:T(8,128)(2,1)S(1)}, bf16[512,1024]{1,0:T(8,128)(2,1)}, u32[]{:S(2)}) copy-start(bf16[512,1024]{1,0:T(8,128)(2,1)} %refs_3_.5) | copy-start | bytes 3145732
  13.1 27.1 %collective-permute-start.4 = (bf16[528,768]{1,0:T(8,128)(2,1)S(1)}, bf16[528,768]{1,0:T(8,128)(2,1)S(1)}, u32[]{:S(2)}, u32[]{:S(2)}) collective-permute-start(bf16[528,768]{1,0:T(8,128)(2,1)S(1)} %get-tuple-element.96), channel_id=1, source_target_pairs={{0,8},{4,12},{8,16},{12,20},{16,24},{20,28},{1,9},{5,13},{9,17},{1... | collective-permute-start | bytes 2433032 | tf_op jit(solution)/shard_map/ppermute | solution.py:34
  16.3 28.3 %collective-permute-start.1 = (bf16[528,1024]{1,0:T(8,128)(2,1)S(1)}, bf16[528,1024]{1,0:T(8,128)(2,1)S(1)}, u32[]{:S(2)}, u32[]{:S(2)}) collective-permute-start(bf16[528,1024]{1,0:T(8,128)(2,1)S(1)} %get-tuple-element.87), channel_id=1, source_target_pairs={{8,0},{12,4},{16,8},{20,12},{24,16},{28,20},{9,1},{13,5},{17,9},{2... | collective-permute-start | bytes 3244040 | tf_op jit(solution)/shard_map/ppermute | solution.py:34
  17.6 44.6 %collective-permute-start.5 = (bf16[544,1280]{1,0:T(8,128)(2,1)S(1)}, bf16[544,1280]{1,0:T(8,128)(2,1)S(1)}, u32[]{:S(2)}, u32[]{:S(2)}) collective-permute-start(bf16[544,1280]{1,0:T(8,128)(2,1)S(1)} %get-tuple-element.102), channel_id=1, source_target_pairs={{0,4},{8,12},{16,20},{24,28},{1,5},{9,13},{17,21},{25,29},{2,6},{1... | collective-permute-start | bytes 4177928 | tf_op jit(solution)/shard_map/ppermute | solution.py:39
  23.0 21.7 %collective-permute-start.3 = (bf16[528,768]{1,0:T(8,128)(2,1)S(1)}, bf16[528,768]{1,0:T(8,128)(2,1)S(1)}, u32[]{:S(2)}, u32[]{:S(2)}) collective-permute-start(bf16[528,768]{1,0:T(8,128)(2,1)S(1)} %collective-permute-done.refs_0_.two), channel_id=1, source_target_pairs={{4,0},{12,8},{20,16},{28,24},{5,1},{13,9},{21,17},{29,25},{6,2},{1... | collective-permute-start | bytes 2433032 | tf_op jit(solution)/shard_map/ppermute | solution.py:44
  28.3 23.9 %collective-permute-start.7 = (bf16[528,512]{1,0:T(8,128)(2,1)S(1)}, bf16[528,512]{1,0:T(8,128)(2,1)S(1)}, u32[]{:S(2)}, u32[]{:S(2)}) collective-permute-start(bf16[528,512]{1,0:T(8,128)(2,1)S(1)} %get-tuple-element.112), channel_id=1, source_target_pairs={{0,8},{4,12},{8,16},{12,20},{16,24},{20,28},{1,9},{5,13},{9,17},{1... | collective-permute-start | bytes 1622024 | tf_op jit(solution)/shard_map/ppermute | solution.py:34
  40.2 22.0 %collective-permute-start.6 = (bf16[528,768]{1,0:T(8,128)(2,1)S(1)}, bf16[528,768]{1,0:T(8,128)(2,1)S(1)}, u32[]{:S(2)}, u32[]{:S(2)}) collective-permute-start(bf16[528,768]{1,0:T(8,128)(2,1)S(1)} %collective-permute-done.4.two), channel_id=1, source_target_pairs={{4,0},{12,8},{20,16},{28,24},{5,1},{13,9},{21,17},{29,25},{6,2},{1... | collective-permute-start | bytes 2433032 | tf_op jit(solution)/shard_map/ppermute | solution.py:44
  52.2 18.3 %collective-permute-start.8 = (bf16[528,512]{1,0:T(8,128)(2,1)S(1)}, bf16[528,512]{1,0:T(8,128)(2,1)S(1)}, u32[]{:S(2)}, u32[]{:S(2)}) collective-permute-start(bf16[528,512]{1,0:T(8,128)(2,1)S(1)} %gate.1.two), channel_id=1, source_target_pairs={{4,0},{12,8},{20,16},{28,24},{5,1},{13,9},{21,17},{29,25},{6,2},{1... | collective-permute-start | bytes 1622024 | tf_op jit(solution)/shard_map/ppermute | solution.py:44
  54.0 25.3 %collective-permute-start.9 = (bf16[400,640]{1,0:T(8,128)(2,1)S(1)}, bf16[400,640]{1,0:T(8,128)(2,1)S(1)}, u32[]{:S(2)}, u32[]{:S(2)}) collective-permute-start(bf16[400,640]{1,0:T(8,128)(2,1)S(1)} %get-tuple-element.119), channel_id=1, source_target_pairs={{0,8},{4,12},{8,16},{12,20},{16,24},{20,28},{1,9},{5,13},{9,17},{1... | collective-permute-start | bytes 1536008 | tf_op jit(solution)/shard_map/ppermute | solution.py:34
  64.5 15.2 %collective-permute-start.10 = (bf16[400,640]{1,0:T(8,128)(2,1)S(1)}, bf16[400,640]{1,0:T(8,128)(2,1)S(1)}, u32[]{:S(2)}, u32[]{:S(2)}) collective-permute-start(bf16[400,640]{1,0:T(8,128)(2,1)S(1)} %get-tuple-element.125), channel_id=1, source_target_pairs={{0,8},{4,12},{8,16},{12,20},{16,24},{20,28},{1,9},{5,13},{9,17},{1... | collective-permute-start | bytes 1536008 | tf_op jit(solution)/shard_map/ppermute | solution.py:34
  72.9 13.2 %collective-permute-start.11 = (bf16[272,640]{1,0:T(8,128)(2,1)S(1)}, bf16[272,640]{1,0:T(8,128)(2,1)S(1)}, u32[]{:S(2)}, u32[]{:S(2)}) collective-permute-start(bf16[272,640]{1,0:T(8,128)(2,1)S(1)} %get-tuple-element.131), channel_id=1, source_target_pairs={{0,8},{4,12},{8,16},{12,20},{16,24},{20,28},{1,9},{5,13},{9,17},{1... | collective-permute-start | bytes 1044488 | tf_op jit(solution)/shard_map/ppermute | solution.py:34
  80.1 14.1 %copy-start.5 = (f32[1024]{0:T(1024)S(1)}, f32[1024]{0:T(1024)}, u32[]{:S(2)}) copy-start(f32[1024]{0:T(1024)} %param.13) | copy-start | bytes 12292

commit v5 on v4

--- a/solution.py
+++ b/solution.py
@@ -417,7 +417,7 @@
         share = jnp.where((lse_far > 0.5 * NEG) & (stats[0:1] > 0.5), share, 0.0)
         lin = dot(pay_ref[rows, length:], q, NT) * st_ref[n + i : n + i + 1, :]
         mixed = x_ref[rows, :] + share * (far - on_ref[rows, :]) + lin
-        mixed_ref[rows, :] = mixed
+        mixed_ref[:, rows] = mixed.T
         part = jnp.sum(mixed * mixed, axis=0, keepdims=True)
         squares = part if squares is None else squares + part
     sq_ref[...] = squares
@@ -427,10 +427,11 @@
 def norm_kernel(parts, *refs):
     mixed_refs, sq_ref, gain_ref, out_ref = refs[:parts], refs[parts], refs[parts + 1], refs[parts + 2]
     inverse = lax.rsqrt(jnp.sum(sq_ref[...], axis=0, keepdims=True) / D + EPSILON)
+    spread = (jnp.zeros((128, inverse.shape[1]), jnp.float32) + inverse).T
     col = 0
     for ref in mixed_refs:
-        for i in range(ref.shape[0] // 128):
-            part = (ref[i * 128 : (i + 1) * 128, :] * inverse).T
+        for i in range(ref.shape[1] // 128):
+            part = ref[:, i * 128 : (i + 1) * 128] * spread
             out_ref[:, col : col + 128] = (part * gain_ref[:, col : col + 128]).astype(jnp.bfloat16)
             col += 128
 
@@ -596,7 +597,7 @@
             0.5 * n,
             [loose, cols(c)] + [whole(a) for a in args],
             (token, query, *args),
-            [shape((n * hd, length), f32), shape((1, length), f32)],
+            [shape((length, n * hd), f32), shape((1, length), f32)],
         )
 
     def gate(x, *after):

time: 97.2 us -> 96.9 us (level)
  no operation moved by 1% of the time
where the time goes in v5:
time: 96.9 us; the launch traced here: 95.6 us
  Pallas kernels  36.5 us (38%)
  starting transfers between devices  31.8 us (33%)
  waiting for transfers between devices  17.8 us (18%)
  blocking collectives  7.19 us (7%)
  local copies, waits for them, and re-layouts  1.92 us (2%)
    pallas_call x18, Pallas kernels, run(): pl.pallas_call(kernel, grid=(1,), in_specs=specs, out_specs=out_specs, ou...  35.2 us
    ppermute x7, starting transfers between devices, shifted(): lax.ppermute(x, 'ctx', [(i, i + by) for i in range(n) if 0 <= i + by < n])  22.8 us
    ppermute x7, waiting for transfers between devices, shifted(): lax.ppermute(x, 'ctx', [(i, i + by) for i in range(n) if 0 <= i + by < n])  17.8 us
    all_gather x1, blocking collectives, on_device(): lax.all_gather(total.reshape(length // 128, 128), 'head')  7.19 us
    ppermute x3, starting transfers between devices, odd_to_even(): return lax.ppermute(x, 'ctx', [(i, i - 1) for i in range(1, n, 2)])  6.42 us
    ppermute x2, starting transfers between devices, even_to_odd(): return lax.ppermute(x, 'ctx', [(i, i + 1) for i in range(0, n - 1, 2)])  2.58 us
  transfers between devices with their start and end apart: 12, of which 3 were waited for; matrix products, arithmetic and copies ran while one was open for 0% of the time, Pallas kernels for 33%

profile of v5, /device:TPU:3, one launch (start us, length us, event | category | flops | bytes accessed | tf_op | source)
XLA Modules:
  0.0 95.6 jit_solution(2469592402748475717)
XLA Ops:
  0.0 0.0 copy-start.4
  0.0 0.0 copy-start.1
  0.0 0.0 copy-start.8
  0.0 0.0 copy-start.7
  0.0 0.0 copy-start
  0.0 2.7 %first_chunk.1 = (bf16[528,768]{1,0:T(8,128)(2,1)}, f32[8,128]{1,0:T(8,128)}) custom-call(f32[8,512]{1,0:T(8,128)} %ld_ref.1, bf16[512,1024]{1,0:T(8,128)(2,1)} %refs_2_.5, bf16[512,1024]{1,0:T(8,128)(2,1)} %refs_3_.5), custom_call_target="tpu_custom_call" | custom-call | bytes 3690000 | tf_op jit(solution)/shard_map/first_chunk/pallas_call | solution.py:463
  2.7 3.3 %collective-permute-start = (bf16[528,768]{1,0:T(8,128)(2,1)}, bf16[528,768]{1,0:T(8,128)(2,1)S(1)}, u32[]{:S(2)}, u32[]{:S(2)}) collective-permute-start(bf16[528,768]{1,0:T(8,128)(2,1)} %get-tuple-element.72), channel_id=1, source_target_pairs={{0,8},{4,12},{8,16},{12,20},{16,24},{20,28},{1,9},{5,13},{9,17},{1... | collective-permute-start | bytes 2433032 | tf_op jit(solution)/shard_map/ppermute | solution.py:34
  6.0 1.3 %collective-permute-start.2 = (bf16[528,768]{1,0:T(8,128)(2,1)}, bf16[528,768]{1,0:T(8,128)(2,1)S(1)}, u32[]{:S(2)}, u32[]{:S(2)}) collective-permute-start(bf16[528,768]{1,0:T(8,128)(2,1)} %get-tuple-element.72), channel_id=1, source_target_pairs={{0,4},{8,12},{16,20},{24,28},{1,5},{9,13},{17,21},{25,29},{2,6},{1... | collective-permute-start | bytes 2433032 | tf_op jit(solution)/shard_map/ppermute | solution.py:39
  7.3 0.0 copy-done.4
  7.3 0.0 copy-done.8
  7.3 0.0 copy-done.7
  7.3 0.0 copy-start.6
  7.3 0.7 copy-done.6
  8.0 0.4 prep.1
  8.4 0.0 copy-done.1
  8.4 0.0 copy-done
  8.4 0.0 copy-start.2
  8.4 1.2 %copy-done.2 = bf16[512,1024]{1,0:T(8,128)(2,1)S(1)} copy-done((bf16[512,1024]{1,0:T(8,128)(2,1)S(1)}, bf16[512,1024]{1,0:T(8,128)(2,1)}, u32[]{:S(2)}) %copy-start.2) | copy-done | bytes 1048600
  9.6 0.0 copy-start.3
  9.6 3.0 %own_piece.3 = (f32[384,512]{1,0:T(8,128)S(1)}, f32[3,512]{1,0:T(4,128)S(1)}, f32[3,512]{1,0:T(4,128)S(1)}, f32[384,512]{1,0:T(8,128)S(1)}, f32[8,128]{1,0:T(8,128)S(1)}) custom-call(f32[8,128]{1,0:T(8,128)S(1)} %get-tuple-element.74.refs_0_, bf16[512,1024]{1,0:T(8,128)(2,1)S(1)} %copy-done, bf16[512,1024]{1,0:T(8,128)(2,1)S(1)} %copy-done.1, ...), custom_call_target="tpu_custom_call" | custom-call | bytes 8856000 | tf_op jit(solution)/shard_map/own_piece/pallas_call | solution.py:463
  12.6 0.0 copy-done.3
  12.6 0.4 pack.2
  13.1 3.2 %collective-permute-start.4 = (bf16[528,768]{1,0:T(8,128)(2,1)S(1)}, bf16[528,768]{1,0:T(8,128)(2,1)S(1)}, u32[]{:S(2)}, u32[]{:S(2)}) collective-permute-start(bf16[528,768]{1,0:T(8,128)(2,1)S(1)} %get-tuple-element.96), channel_id=1, source_target_pairs={{0,8},{4,12},{8,16},{12,20},{16,24},{20,28},{1,9},{5,13},{9,17},{1... | collective-permute-start | bytes 2433032 | tf_op jit(solution)/shard_map/ppermute | solution.py:34
  16.3 1.3 %collective-permute-start.1 = (bf16[528,1024]{1,0:T(8,128)(2,1)S(1)}, bf16[528,1024]{1,0:T(8,128)(2,1)S(1)}, u32[]{:S(2)}, u32[]{:S(2)}) collective-permute-start(bf16[528,1024]{1,0:T(8,128)(2,1)S(1)} %get-tuple-element.87), channel_id=1, source_target_pairs={{8,0},{12,4},{16,8},{20,12},{24,16},{28,20},{9,1},{13,5},{17,9},{2... | collective-permute-start | bytes 3244040 | tf_op jit(solution)/shard_map/ppermute | solution.py:34
  17.6 1.3 %collective-permute-start.5 = (bf16[544,1280]{1,0:T(8,128)(2,1)S(1)}, bf16[544,1280]{1,0:T(8,128)(2,1)S(1)}, u32[]{:S(2)}, u32[]{:S(2)}) collective-permute-start(bf16[544,1280]{1,0:T(8,128)(2,1)S(1)} %get-tuple-element.102), channel_id=1, source_target_pairs={{0,4},{8,12},{16,20},{24,28},{1,5},{9,13},{17,21},{25,29},{2,6},{1... | collective-permute-start | bytes 4177928 | tf_op jit(solution)/shard_map/ppermute | solution.py:39
  18.9 4.1 %collective-permute-done.refs_0_.two = bf16[528,768]{1,0:T(8,128)(2,1)S(1)} collective-permute-done((bf16[528,768]{1,0:T(8,128)(2,1)}, bf16[528,768]{1,0:T(8,128)(2,1)S(1)}, u32[]{:S(2)}, u32[]{:S(2)}) %collective-permute-start) | collective-permute-done | bytes 811040 | tf_op jit(solution)/shard_map/ppermute | solution.py:34
  23.0 2.2 %collective-permute-start.3 = (bf16[528,768]{1,0:T(8,128)(2,1)S(1)}, bf16[528,768]{1,0:T(8,128)(2,1)S(1)}, u32[]{:S(2)}, u32[]{:S(2)}) collective-permute-start(bf16[528,768]{1,0:T(8,128)(2,1)S(1)} %collective-permute-done.refs_0_.two), channel_id=1, source_target_pairs={{4,0},{12,8},{20,16},{28,24},{5,1},{13,9},{21,17},{29,25},{6,2},{1... | collective-permute-start | bytes 2433032 | tf_op jit(solution)/shard_map/ppermute | solution.py:44
  25.2 3.0 %own_piece.4 = (f32[384,512]{1,0:T(8,128)S(1)}, f32[3,512]{1,0:T(4,128)S(1)}, f32[3,512]{1,0:T(4,128)S(1)}, f32[384,512]{1,0:T(8,128)S(1)}, f32[8,128]{1,0:T(8,128)S(1)}) custom-call(bf16[528,768]{1,0:T(8,128)(2,1)S(1)} %collective-permute-done.refs_0_.two, f32[8,128]{1,0:T(8,128)S(1)} %get-tuple-element.82.refs_1_, bf16[512,1024]{1,0:T(8,128)(2,1)S(1)} %copy-done, ...), custom_call_target="tpu_custom_call" | custom-call | bytes 8856000 | tf_op jit(solution)/shard_map/own_piece/pallas_call | solution.py:463
  28.2 0.1 pack.3
  28.3 0.0 collective-permute-done.2.even
  28.3 4.0 %collective-permute-start.7 = (bf16[528,512]{1,0:T(8,128)(2,1)S(1)}, bf16[528,512]{1,0:T(8,128)(2,1)S(1)}, u32[]{:S(2)}, u32[]{:S(2)}) collective-permute-start(bf16[528,512]{1,0:T(8,128)(2,1)S(1)} %get-tuple-element.112), channel_id=1, source_target_pairs={{0,8},{4,12},{8,16},{12,20},{16,24},{20,28},{1,9},{5,13},{9,17},{1... | collective-permute-start | bytes 1622024 | tf_op jit(solution)/shard_map/ppermute | solution.py:34
  32.3 7.9 %collective-permute-done.4.two = bf16[528,768]{1,0:T(8,128)(2,1)S(1)} collective-permute-done((bf16[528,768]{1,0:T(8,128)(2,1)S(1)}, bf16[528,768]{1,0:T(8,128)(2,1)S(1)}, u32[]{:S(2)}, u32[]{:S(2)}) %collective-permute-start.4) | collective-permute-done | bytes 811040 | tf_op jit(solution)/shard_map/ppermute | solution.py:34
  40.2 2.4 %collective-permute-start.6 = (bf16[528,768]{1,0:T(8,128)(2,1)S(1)}, bf16[528,768]{1,0:T(8,128)(2,1)S(1)}, u32[]{:S(2)}, u32[]{:S(2)}) collective-permute-start(bf16[528,768]{1,0:T(8,128)(2,1)S(1)} %collective-permute-done.4.two), channel_id=1, source_target_pairs={{4,0},{12,8},{20,16},{28,24},{5,1},{13,9},{21,17},{29,25},{6,2},{1... | collective-permute-start | bytes 2433032 | tf_op jit(solution)/shard_map/ppermute | solution.py:44
  42.6 2.0 %own_piece.5 = (f32[256,512]{1,0:T(8,128)S(1)}, f32[2,512]{1,0:T(2,128)S(1)}, f32[2,512]{1,0:T(2,128)S(1)}, f32[256,512]{1,0:T(8,128)S(1)}, f32[8,128]{1,0:T(8,128)S(1)}) custom-call(f32[8,128]{1,0:T(8,128)S(1)} %get-tuple-element.84.refs_0_, bf16[512,1024]{1,0:T(8,128)(2,1)S(1)} %copy-done, bf16[512,1024]{1,0:T(8,128)(2,1)S(1)} %copy-done.1, ...), custom_call_target="tpu_custom_call" | custom-call | bytes 5904000 | tf_op jit(solution)/shard_map/own_piece/pallas_call | solution.py:463
  44.6 0.0 collective-permute-done.1.q_ref.keep_ref
  44.6 0.0 collective-permute-done.3.odd
  44.6 3.5 %far_pieces.3 = (bf16[400,640]{1,0:T(8,128)(2,1)S(1)}, f32[8,128]{1,0:T(8,128)S(1)}) custom-call(f32[8,128]{1,0:T(8,128)S(1)} %get-tuple-element.85.token_in, s32[8,512]{1,0:T(8,128)S(1)} %get-tuple-element.86.entry_ref, bf16[528,1024]{1,0:T(8,128)(2,1)S(1)} %collective-permute-done.1.q_ref.keep_ref, ...), custom_call_target="tpu_custom_call" | custom-call | bytes 16605000 | tf_op jit(solution)/shard_map/far_pieces/pallas_call | solution.py:463
  48.1 4.0 %near_pieces.3 = (f32[384,512]{1,0:T(8,128)S(1)}, f32[384,512]{1,0:T(8,128)S(1)}, f32[8,512]{1,0:T(8,128)S(1)}, f32[8,128]{1,0:T(8,128)S(1)}) custom-call(f32[8,128]{1,0:T(8,128)S(1)} %get-tuple-element.89.token_in, s32[8,512]{1,0:T(8,128)S(1)} %get-tuple-element.86.entry_ref, bf16[512,1024]{1,0:T(8,128)(2,1)S(1)} %copy-done, ...), custom_call_target="tpu_custom_call" | custom-call | bytes 19926000 | tf_op jit(solution)/shard_map/near_pieces/pallas_call | solution.py:463
  52.1 0.0 collective-permute-done.7.refs_0_
  52.2 1.8 %collective-permute-start.8 = (bf16[528,512]{1,0:T(8,128)(2,1)S(1)}, bf16[528,512]{1,0:T(8,128)(2,1)S(1)}, u32[]{:S(2)}, u32[]{:S(2)}) collective-permute-start(bf16[528,512]{1,0:T(8,128)(2,1)S(1)} %gate.1.two), channel_id=1, source_target_pairs={{4,0},{12,8},{20,16},{28,24},{5,1},{13,9},{21,17},{29,25},{6,2},{1... | collective-permute-start | bytes 1622024 | tf_op jit(solution)/shard_map/ppermute | solution.py:44
  54.0 4.4 %collective-permute-start.9 = (bf16[400,640]{1,0:T(8,128)(2,1)S(1)}, bf16[400,640]{1,0:T(8,128)(2,1)S(1)}, u32[]{:S(2)}, u32[]{:S(2)}) collective-permute-start(bf16[400,640]{1,0:T(8,128)(2,1)S(1)} %get-tuple-element.119), channel_id=1, source_target_pairs={{0,8},{4,12},{8,16},{12,20},{16,24},{20,28},{1,9},{5,13},{9,17},{1... | collective-permute-start | bytes 1536008 | tf_op jit(solution)/shard_map/ppermute | solution.py:34
  58.4 1.9 %far_earlier.1 = (f32[384,512]{1,0:T(8,128)S(1)}, f32[3,512]{1,0:T(4,128)S(1)}, f32[3,512]{1,0:T(4,128)S(1)}, f32[8,128]{1,0:T(8,128)S(1)}) custom-call(f32[8,128]{1,0:T(8,128)S(1)} %get-tuple-element.95.token_in.refs_1_, bf16[528,1024]{1,0:T(8,128)(2,1)S(1)} %collective-permute-done.1.q_ref.keep_ref, ...), custom_call_target="tpu_custom_call" | custom-call | bytes 7748999 | tf_op jit(solution)/shard_map/far_earlier/pallas_call | solution.py:463
  60.3 1.9 %earlier_piece.1 = (f32[384,512]{1,0:T(8,128)S(1)}, f32[3,512]{1,0:T(4,128)S(1)}, f32[3,512]{1,0:T(4,128)S(1)}, f32[8,128]{1,0:T(8,128)S(1)}) custom-call(f32[8,128]{1,0:T(8,128)S(1)} %get-tuple-element.97.token_in, bf16[512,1024]{1,0:T(8,128)(2,1)S(1)} %copy-done, s32[20,512]{1,0:T(8,128)S(1)} %get-tuple-element.75.refs_4_.refs_5_.thr_ref, ...), custom_call_target="tpu_custom_call" | custom-call | bytes 8856000 | tf_op jit(solution)/shard_map/earlier_piece/pallas_call | solution.py:463
  62.2 0.0 collective-permute-done.5.even
  62.2 0.0 collective-permute-done.6.odd
  62.2 2.3 %far_pieces.4 = (bf16[400,640]{1,0:T(8,128)(2,1)S(1)}, f32[8,128]{1,0:T(8,128)S(1)}) custom-call(f32[8,128]{1,0:T(8,128)S(1)} %get-tuple-element.101.token_in, s32[8,512]{1,0:T(8,128)S(1)} %get-tuple-element.86.entry_ref, bf16[528,1024]{1,0:T(8,128)(2,1)S(1)} %collective-permute-done.1.q_ref.keep_ref, ...), custom_call_target="tpu_custom_call" | custom-call | bytes 16605000 | tf_op jit(solution)/shard_map/far_pieces/pallas_call | solution.py:463
  64.5 3.2 %collective-permute-start.10 = (bf16[400,640]{1,0:T(8,128)(2,1)S(1)}, bf16[400,640]{1,0:T(8,128)(2,1)S(1)}, u32[]{:S(2)}, u32[]{:S(2)}) collective-permute-start(bf16[400,640]{1,0:T(8,128)(2,1)S(1)} %get-tuple-element.125), channel_id=1, source_target_pairs={{0,8},{4,12},{8,16},{12,20},{16,24},{20,28},{1,9},{5,13},{9,17},{1... | collective-permute-start | bytes 1536008 | tf_op jit(solution)/shard_map/ppermute | solution.py:34
  67.7 2.7 %near_pieces.4 = (f32[384,512]{1,0:T(8,128)S(1)}, f32[384,512]{1,0:T(8,128)S(1)}, f32[8,512]{1,0:T(8,128)S(1)}, f32[8,128]{1,0:T(8,128)S(1)}) custom-call(f32[8,128]{1,0:T(8,128)S(1)} %get-tuple-element.106.token_in, s32[8,512]{1,0:T(8,128)S(1)} %get-tuple-element.86.entry_ref, bf16[512,1024]{1,0:T(8,128)(2,1)S(1)} %copy-done, ...), custom_call_target="tpu_custom_call" | custom-call | bytes 19926000 | tf_op jit(solution)/shard_map/near_pieces/pallas_call | solution.py:463
  70.5 0.0 collective-permute-done.8.odd
  70.5 2.5 %far_pieces.5 = (bf16[272,640]{1,0:T(8,128)(2,1)S(1)}, f32[8,128]{1,0:T(8,128)S(1)}) custom-call(f32[8,128]{1,0:T(8,128)S(1)} %get-tuple-element.111.token_in, s32[8,512]{1,0:T(8,128)S(1)} %get-tuple-element.86.entry_ref, bf16[528,1024]{1,0:T(8,128)(2,1)S(1)} %collective-permute-done.1.q_ref.keep_ref, ...), custom_call_target="tpu_custom_call" | custom-call | bytes 11070000 | tf_op jit(solution)/shard_map/far_pieces/pallas_call | solution.py:463
  72.9 3.5 %collective-permute-start.11 = (bf16[272,640]{1,0:T(8,128)(2,1)S(1)}, bf16[272,640]{1,0:T(8,128)(2,1)S(1)}, u32[]{:S(2)}, u32[]{:S(2)}) collective-permute-start(bf16[272,640]{1,0:T(8,128)(2,1)S(1)} %get-tuple-element.131), channel_id=1, source_target_pairs={{0,8},{4,12},{8,16},{12,20},{16,24},{20,28},{1,9},{5,13},{9,17},{1... | collective-permute-start | bytes 1044488 | tf_op jit(solution)/shard_map/ppermute | solution.py:34
  76.4 2.9 %near_pieces.5 = (f32[256,512]{1,0:T(8,128)S(1)}, f32[256,512]{1,0:T(8,128)S(1)}, f32[8,512]{1,0:T(8,128)S(1)}, f32[8,128]{1,0:T(8,128)S(1)}) custom-call(f32[8,128]{1,0:T(8,128)S(1)} %get-tuple-element.113.token_in, s32[8,512]{1,0:T(8,128)S(1)} %get-tuple-element.86.entry_ref, bf16[512,1024]{1,0:T(8,128)(2,1)S(1)} %copy-done, ...), custom_call_target="tpu_custom_call" | custom-call | bytes 13284000 | tf_op jit(solution)/shard_map/near_pieces/pallas_call | solution.py:463
  79.3 0.0 collective-permute-done.9.pay_ref
  79.3 0.5 merge.3
  79.8 0.0 collective-permute-done.10.pay_ref
  79.8 0.5 merge.4
  80.4 0.0 copy-start.5
  80.4 5.8 %collective-permute-done.11.pay_ref = bf16[272,640]{1,0:T(8,128)(2,1)S(1)} collective-permute-done((bf16[272,640]{1,0:T(8,128)(2,1)S(1)}, bf16[272,640]{1,0:T(8,128)(2,1)S(1)}, u32[]{:S(2)}, u32[]{:S(2)}) %collective-permute-start.11) | collective-permute-done | bytes 348192 | tf_op jit(solution)/shard_map/ppermute | solution.py:34
  86.2 0.9 merge.5
  87.1 7.2 %all_gather.3 = f32[4,4,128]{2,1,0:T(4,128)S(1)} all-gather(f32[1,4,128]{2,1,0:T(4,128)S(1)} %bitcast.11), channel_id=1, replica_groups=mesh['ctx'=8,'head'=4] {'head'}, dimensions={0}, use_global_device_ids=true | all-gather | bytes 10240 | tf_op jit(solution)/shard_map/all_gather | solution.py:657
  94.3 0.0 copy-done.5
  94.3 1.3 %normalize.1 = bf16[512,1024]{1,0:T(8,128)(2,1)} custom-call(f32[512,384]{1,0:T(8,128)S(1)} %get-tuple-element.123.refs_0_, f32[512,384]{1,0:T(8,128)S(1)} %get-tuple-element.129.refs_1_, f32[512,256]{1,0:T(8,128)S(1)} %get-tuple-element.135.refs_2_, f32[4,512]{1,0:T(4,128)S(1)} %bitcast.7, f32[1,1024]{1,0:T(1,128)S(1)} %bitcast.8), custom_call_target="tpu_custom_call" | custom-call | tf_op jit(solution)/shard_map/normalize/pallas_call | solution.py:659
  (3 shorter events, 0.0 us)
Async XLA Ops:
  0.0 7.3 %copy-start.4 = (f32[8,512]{1,0:T(8,128)S(1)}, f32[8,512]{1,0:T(8,128)}, u32[]{:S(2)}) copy-start(f32[8,512]{1,0:T(8,128)} %ld_ref.1) | copy-start | bytes 49156
  0.0 8.4 %copy-start.1 = (bf16[512,1024]{1,0:T(8,128)(2,1)S(1)}, bf16[512,1024]{1,0:T(8,128)(2,1)}, u32[]{:S(2)}) copy-start(bf16[512,1024]{1,0:T(8,128)(2,1)} %refs_2_.5) | copy-start | bytes 3145732
  0.0 7.3 %copy-start.8 = (s32[8]{0:T(128)S(1)}, s32[8]{0:T(128)}, u32[]{:S(2)}) copy-start(s32[8]{0:T(128)} %param.11) | copy-start | bytes 100
  0.0 7.3 %copy-start.7 = (s32[4,20]{1,0:T(4,128)S(1)}, s32[4,20]{1,0:T(4,128)}, u32[]{:S(2)}) copy-start(s32[4,20]{1,0:T(4,128)} %mask_ref.1) | copy-start | bytes 964
  0.0 8.4 %copy-start = (bf16[512,1024]{1,0:T(8,128)(2,1)S(1)}, bf16[512,1024]{1,0:T(8,128)(2,1)}, u32[]{:S(2)}) copy-start(bf16[512,1024]{1,0:T(8,128)(2,1)} %q_ref.15) | copy-start | bytes 3145732
  2.7 20.2 %collective-permute-start = (bf16[528,768]{1,0:T(8,128)(2,1)}, bf16[528,768]{1,0:T(8,128)(2,1)S(1)}, u32[]{:S(2)}, u32[]{:S(2)}) collective-permute-start(bf16[528,768]{1,0:T(8,128)(2,1)} %get-tuple-element.72), channel_id=1, source_target_pairs={{0,8},{4,12},{8,16},{12,20},{16,24},{20,28},{1,9},{5,13},{9,17},{1... | collective-permute-start | bytes 2433032 | tf_op jit(solution)/shard_map/ppermute | solution.py:34
  6.0 22.3 %collective-permute-start.2 = (bf16[528,768]{1,0:T(8,128)(2,1)}, bf16[528,768]{1,0:T(8,128)(2,1)S(1)}, u32[]{:S(2)}, u32[]{:S(2)}) collective-permute-start(bf16[528,768]{1,0:T(8,128)(2,1)} %get-tuple-element.72), channel_id=1, source_target_pairs={{0,4},{8,12},{16,20},{24,28},{1,5},{9,13},{17,21},{25,29},{2,6},{1... | collective-permute-start | bytes 2433032 | tf_op jit(solution)/shard_map/ppermute | solution.py:39
  7.3 0.7 copy-start.6
  8.4 1.2 %copy-start.2 = (bf16[512,1024]{1,0:T(8,128)(2,1)S(1)}, bf16[512,1024]{1,0:T(8,128)(2,1)}, u32[]{:S(2)}) copy-start(bf16[512,1024]{1,0:T(8,128)(2,1)} %refs_3_.5) | copy-start | bytes 3145732
  9.6 3.0 %copy-start.3 = (bf16[512,1024]{1,0:T(8,128)(2,1)S(1)}, bf16[512,1024]{1,0:T(8,128)(2,1)}, u32[]{:S(2)}) copy-start(bf16[512,1024]{1,0:T(8,128)(2,1)} %refs_3_.5) | copy-start | bytes 3145732
  13.1 27.1 %collective-permute-start.4 = (bf16[528,768]{1,0:T(8,128)(2,1)S(1)}, bf16[528,768]{1,0:T(8,128)(2,1)S(1)}, u32[]{:S(2)}, u32[]{:S(2)}) collective-permute-start(bf16[528,768]{1,0:T(8,128)(2,1)S(1)} %get-tuple-element.96), channel_id=1, source_target_pairs={{0,8},{4,12},{8,16},{12,20},{16,24},{20,28},{1,9},{5,13},{9,17},{1... | collective-permute-start | bytes 2433032 | tf_op jit(solution)/shard_map/ppermute | solution.py:34
  16.3 28.3 %collective-permute-start.1 = (bf16[528,1024]{1,0:T(8,128)(2,1)S(1)}, bf16[528,1024]{1,0:T(8,128)(2,1)S(1)}, u32[]{:S(2)}, u32[]{:S(2)}) collective-permute-start(bf16[528,1024]{1,0:T(8,128)(2,1)S(1)} %get-tuple-element.87), channel_id=1, source_target_pairs={{8,0},{12,4},{16,8},{20,12},{24,16},{28,20},{9,1},{13,5},{17,9},{2... | collective-permute-start | bytes 3244040 | tf_op jit(solution)/shard_map/ppermute | solution.py:34
  17.6 44.6 %collective-permute-start.5 = (bf16[544,1280]{1,0:T(8,128)(2,1)S(1)}, bf16[544,1280]{1,0:T(8,128)(2,1)S(1)}, u32[]{:S(2)}, u32[]{:S(2)}) collective-permute-start(bf16[544,1280]{1,0:T(8,128)(2,1)S(1)} %get-tuple-element.102), channel_id=1, source_target_pairs={{0,4},{8,12},{16,20},{24,28},{1,5},{9,13},{17,21},{25,29},{2,6},{1... | collective-permute-start | bytes 4177928 | tf_op jit(solution)/shard_map/ppermute | solution.py:39
  23.0 21.7 %collective-permute-start.3 = (bf16[528,768]{1,0:T(8,128)(2,1)S(1)}, bf16[528,768]{1,0:T(8,128)(2,1)S(1)}, u32[]{:S(2)}, u32[]{:S(2)}) collective-permute-start(bf16[528,768]{1,0:T(8,128)(2,1)S(1)} %collective-permute-done.refs_0_.two), channel_id=1, source_target_pairs={{4,0},{12,8},{20,16},{28,24},{5,1},{13,9},{21,17},{29,25},{6,2},{1... | collective-permute-start | bytes 2433032 | tf_op jit(solution)/shard_map/ppermute | solution.py:44
  28.3 23.9 %collective-permute-start.7 = (bf16[528,512]{1,0:T(8,128)(2,1)S(1)}, bf16[528,512]{1,0:T(8,128)(2,1)S(1)}, u32[]{:S(2)}, u32[]{:S(2)}) collective-permute-start(bf16[528,512]{1,0:T(8,128)(2,1)S(1)} %get-tuple-element.112), channel_id=1, source_target_pairs={{0,8},{4,12},{8,16},{12,20},{16,24},{20,28},{1,9},{5,13},{9,17},{1... | collective-permute-start | bytes 1622024 | tf_op jit(solution)/shard_map/ppermute | solution.py:34
  40.2 22.0 %collective-permute-start.6 = (bf16[528,768]{1,0:T(8,128)(2,1)S(1)}, bf16[528,768]{1,0:T(8,128)(2,1)S(1)}, u32[]{:S(2)}, u32[]{:S(2)}) collective-permute-start(bf16[528,768]{1,0:T(8,128)(2,1)S(1)} %collective-permute-done.4.two), channel_id=1, source_target_pairs={{4,0},{12,8},{20,16},{28,24},{5,1},{13,9},{21,17},{29,25},{6,2},{1... | collective-permute-start | bytes 2433032 | tf_op jit(solution)/shard_map/ppermute | solution.py:44
  52.2 18.3 %collective-permute-start.8 = (bf16[528,512]{1,0:T(8,128)(2,1)S(1)}, bf16[528,512]{1,0:T(8,128)(2,1)S(1)}, u32[]{:S(2)}, u32[]{:S(2)}) collective-permute-start(bf16[528,512]{1,0:T(8,128)(2,1)S(1)} %gate.1.two), channel_id=1, source_target_pairs={{4,0},{12,8},{20,16},{28,24},{5,1},{13,9},{21,17},{29,25},{6,2},{1... | collective-permute-start | bytes 1622024 | tf_op jit(solution)/shard_map/ppermute | solution.py:44
  54.0 25.3 %collective-permute-start.9 = (bf16[400,640]{1,0:T(8,128)(2,1)S(1)}, bf16[400,640]{1,0:T(8,128)(2,1)S(1)}, u32[]{:S(2)}, u32[]{:S(2)}) collective-permute-start(bf16[400,640]{1,0:T(8,128)(2,1)S(1)} %get-tuple-element.119), channel_id=1, source_target_pairs={{0,8},{4,12},{8,16},{12,20},{16,24},{20,28},{1,9},{5,13},{9,17},{1... | collective-permute-start | bytes 1536008 | tf_op jit(solution)/shard_map/ppermute | solution.py:34
  64.5 15.3 %collective-permute-start.10 = (bf16[400,640]{1,0:T(8,128)(2,1)S(1)}, bf16[400,640]{1,0:T(8,128)(2,1)S(1)}, u32[]{:S(2)}, u32[]{:S(2)}) collective-permute-start(bf16[400,640]{1,0:T(8,128)(2,1)S(1)} %get-tuple-element.125), channel_id=1, source_target_pairs={{0,8},{4,12},{8,16},{12,20},{16,24},{20,28},{1,9},{5,13},{9,17},{1... | collective-permute-start | bytes 1536008 | tf_op jit(solution)/shard_map/ppermute | solution.py:34
  72.9 13.2 %collective-permute-start.11 = (bf16[272,640]{1,0:T(8,128)(2,1)S(1)}, bf16[272,640]{1,0:T(8,128)(2,1)S(1)}, u32[]{:S(2)}, u32[]{:S(2)}) collective-permute-start(bf16[272,640]{1,0:T(8,128)(2,1)S(1)} %get-tuple-element.131), channel_id=1, source_target_pairs={{0,8},{4,12},{8,16},{12,20},{16,24},{20,28},{1,9},{5,13},{9,17},{1... | collective-permute-start | bytes 1044488 | tf_op jit(solution)/shard_map/ppermute | solution.py:34
  80.4 13.9 %copy-start.5 = (f32[1024]{0:T(1024)S(1)}, f32[1024]{0:T(1024)}, u32[]{:S(2)}) copy-start(f32[1024]{0:T(1024)} %param.13) | copy-start | bytes 12292

commit v6 on v5

--- a/solution.py
+++ b/solution.py
@@ -645,8 +645,8 @@
     first, token = far_earlier(1, token)
     token = earlier(1, token)
     pays[1], token = far(1, token, first)
+    pays[2], token = far(2, token)
     parts[1], token = near(1, token)
-    pays[2], token = far(2, token)
     parts[2], token = near(2, token)
     mixed, total = [], None
     for c in chunks:

time: 96.9 us -> 96.9 us (level)
    ppermute x7, waiting for transfers between devices: 17.8 us -> 16.2 us  [shifted(): lax.ppermute(x, 'ctx', [(i, i + by) for i in range(n) if 0 <= i + by < n])]
    ppermute x3, waiting for transfers between devices: 0.01 us -> 1.33 us  [odd_to_even(): return lax.ppermute(x, 'ctx', [(i, i - 1) for i in range(1, n, 2)])]
  transfers between devices with their start and end apart: 12 -> 12, of which waited for: 3 -> 4; matrix products, arithmetic and copies ran while one was open for 0% -> 0% of each run, Pallas kernels for 33% -> 33%
where the time goes in v6:
time: 96.9 us; the launch traced here: 95.6 us
  Pallas kernels  36.3 us (37%)
  starting transfers between devices  32.4 us (33%)
  waiting for transfers between devices  17.5 us (18%)
  blocking collectives  7.07 us (7%)
  local copies, waits for them, and re-layouts  1.92 us (2%)
    pallas_call x18, Pallas kernels, run(): pl.pallas_call(kernel, grid=(1,), in_specs=specs, out_specs=out_specs, ou...  34.9 us
    ppermute x7, starting transfers between devices, shifted(): lax.ppermute(x, 'ctx', [(i, i + by) for i in range(n) if 0 <= i + by < n])  23.5 us
    ppermute x7, waiting for transfers between devices, shifted(): lax.ppermute(x, 'ctx', [(i, i + by) for i in range(n) if 0 <= i + by < n])  16.2 us
    all_gather x1, blocking collectives, on_device(): lax.all_gather(total.reshape(length // 128, 128), 'head')  7.07 us
    ppermute x3, starting transfers between devices, odd_to_even(): return lax.ppermute(x, 'ctx', [(i, i - 1) for i in range(1, n, 2)])  6.34 us
    ppermute x2, starting transfers between devices, even_to_odd(): return lax.ppermute(x, 'ctx', [(i, i + 1) for i in range(0, n - 1, 2)])  2.58 us
  transfers between devices with their start and end apart: 12, of which 4 were waited for; matrix products, arithmetic and copies ran while one was open for 0% of the time, Pallas kernels for 33%

profile of v6, /device:TPU:3, one launch (start us, length us, event | category | flops | bytes accessed | tf_op | source)
XLA Modules:
  0.0 95.6 jit_solution(2051756422085486060)
XLA Ops:
  0.0 0.0 copy-start.4
  0.0 0.0 copy-start.1
  0.0 0.0 copy-start.8
  0.0 0.0 copy-start.7
  0.0 0.0 copy-start
  0.0 2.7 %first_chunk.1 = (bf16[528,768]{1,0:T(8,128)(2,1)}, f32[8,128]{1,0:T(8,128)}) custom-call(f32[8,512]{1,0:T(8,128)} %ld_ref.1, bf16[512,1024]{1,0:T(8,128)(2,1)} %refs_2_.5, bf16[512,1024]{1,0:T(8,128)(2,1)} %refs_3_.5), custom_call_target="tpu_custom_call" | custom-call | bytes 3690000 | tf_op jit(solution)/shard_map/first_chunk/pallas_call | solution.py:463
  2.7 3.3 %collective-permute-start = (bf16[528,768]{1,0:T(8,128)(2,1)}, bf16[528,768]{1,0:T(8,128)(2,1)S(1)}, u32[]{:S(2)}, u32[]{:S(2)}) collective-permute-start(bf16[528,768]{1,0:T(8,128)(2,1)} %get-tuple-element.72), channel_id=1, source_target_pairs={{0,8},{4,12},{8,16},{12,20},{16,24},{20,28},{1,9},{5,13},{9,17},{1... | collective-permute-start | bytes 2433032 | tf_op jit(solution)/shard_map/ppermute | solution.py:34
  6.0 1.3 %collective-permute-start.2 = (bf16[528,768]{1,0:T(8,128)(2,1)}, bf16[528,768]{1,0:T(8,128)(2,1)S(1)}, u32[]{:S(2)}, u32[]{:S(2)}) collective-permute-start(bf16[528,768]{1,0:T(8,128)(2,1)} %get-tuple-element.72), channel_id=1, source_target_pairs={{0,4},{8,12},{16,20},{24,28},{1,5},{9,13},{17,21},{25,29},{2,6},{1... | collective-permute-start | bytes 2433032 | tf_op jit(solution)/shard_map/ppermute | solution.py:39
  7.3 0.0 copy-done.4
  7.3 0.0 copy-done.8
  7.3 0.0 copy-done.7
  7.3 0.0 copy-start.6
  7.3 0.7 copy-done.6
  8.0 0.4 prep.1
  8.4 0.0 copy-done.1
  8.4 0.0 copy-done
  8.4 0.0 copy-start.2
  8.4 1.2 %copy-done.2 = bf16[512,1024]{1,0:T(8,128)(2,1)S(1)} copy-done((bf16[512,1024]{1,0:T(8,128)(2,1)S(1)}, bf16[512,1024]{1,0:T(8,128)(2,1)}, u32[]{:S(2)}) %copy-start.2) | copy-done | bytes 1048600
  9.6 0.0 copy-start.3
  9.6 3.0 %own_piece.3 = (f32[384,512]{1,0:T(8,128)S(1)}, f32[3,512]{1,0:T(4,128)S(1)}, f32[3,512]{1,0:T(4,128)S(1)}, f32[384,512]{1,0:T(8,128)S(1)}, f32[8,128]{1,0:T(8,128)S(1)}) custom-call(f32[8,128]{1,0:T(8,128)S(1)} %get-tuple-element.74.refs_0_, bf16[512,1024]{1,0:T(8,128)(2,1)S(1)} %copy-done, bf16[512,1024]{1,0:T(8,128)(2,1)S(1)} %copy-done.1, ...), custom_call_target="tpu_custom_call" | custom-call | bytes 8856000 | tf_op jit(solution)/shard_map/own_piece/pallas_call | solution.py:463
  12.6 0.0 copy-done.3
  12.6 0.4 pack.2
  13.1 3.2 %collective-permute-start.4 = (bf16[528,768]{1,0:T(8,128)(2,1)S(1)}, bf16[528,768]{1,0:T(8,128)(2,1)S(1)}, u32[]{:S(2)}, u32[]{:S(2)}) collective-permute-start(bf16[528,768]{1,0:T(8,128)(2,1)S(1)} %get-tuple-element.96), channel_id=1, source_target_pairs={{0,8},{4,12},{8,16},{12,20},{16,24},{20,28},{1,9},{5,13},{9,17},{1... | collective-permute-start | bytes 2433032 | tf_op jit(solution)/shard_map/ppermute | solution.py:34
  16.3 1.3 %collective-permute-start.1 = (bf16[528,1024]{1,0:T(8,128)(2,1)S(1)}, bf16[528,1024]{1,0:T(8,128)(2,1)S(1)}, u32[]{:S(2)}, u32[]{:S(2)}) collective-permute-start(bf16[528,1024]{1,0:T(8,128)(2,1)S(1)} %get-tuple-element.87), channel_id=1, source_target_pairs={{8,0},{12,4},{16,8},{20,12},{24,16},{28,20},{9,1},{13,5},{17,9},{2... | collective-permute-start | bytes 3244040 | tf_op jit(solution)/shard_map/ppermute | solution.py:34
  17.6 1.3 %collective-permute-start.5 = (bf16[544,1280]{1,0:T(8,128)(2,1)S(1)}, bf16[544,1280]{1,0:T(8,128)(2,1)S(1)}, u32[]{:S(2)}, u32[]{:S(2)}) collective-permute-start(bf16[544,1280]{1,0:T(8,128)(2,1)S(1)} %get-tuple-element.102), channel_id=1, source_target_pairs={{0,4},{8,12},{16,20},{24,28},{1,5},{9,13},{17,21},{25,29},{2,6},{1... | collective-permute-start | bytes 4177928 | tf_op jit(solution)/shard_map/ppermute | solution.py:39
  18.9 4.1 %collective-permute-done.refs_0_.two = bf16[528,768]{1,0:T(8,128)(2,1)S(1)} collective-permute-done((bf16[528,768]{1,0:T(8,128)(2,1)}, bf16[528,768]{1,0:T(8,128)(2,1)S(1)}, u32[]{:S(2)}, u32[]{:S(2)}) %collective-permute-start) | collective-permute-done | bytes 811040 | tf_op jit(solution)/shard_map/ppermute | solution.py:34
  23.0 2.2 %collective-permute-start.3 = (bf16[528,768]{1,0:T(8,128)(2,1)S(1)}, bf16[528,768]{1,0:T(8,128)(2,1)S(1)}, u32[]{:S(2)}, u32[]{:S(2)}) collective-permute-start(bf16[528,768]{1,0:T(8,128)(2,1)S(1)} %collective-permute-done.refs_0_.two), channel_id=1, source_target_pairs={{4,0},{12,8},{20,16},{28,24},{5,1},{13,9},{21,17},{29,25},{6,2},{1... | collective-permute-start | bytes 2433032 | tf_op jit(solution)/shard_map/ppermute | solution.py:44
  25.2 3.0 %own_piece.4 = (f32[384,512]{1,0:T(8,128)S(1)}, f32[3,512]{1,0:T(4,128)S(1)}, f32[3,512]{1,0:T(4,128)S(1)}, f32[384,512]{1,0:T(8,128)S(1)}, f32[8,128]{1,0:T(8,128)S(1)}) custom-call(bf16[528,768]{1,0:T(8,128)(2,1)S(1)} %collective-permute-done.refs_0_.two, f32[8,128]{1,0:T(8,128)S(1)} %get-tuple-element.82.refs_1_, bf16[512,1024]{1,0:T(8,128)(2,1)S(1)} %copy-done, ...), custom_call_target="tpu_custom_call" | custom-call | bytes 8856000 | tf_op jit(solution)/shard_map/own_piece/pallas_call | solution.py:463
  28.2 0.1 pack.3
  28.3 0.0 collective-permute-done.2.even
  28.3 4.0 %collective-permute-start.7 = (bf16[528,512]{1,0:T(8,128)(2,1)S(1)}, bf16[528,512]{1,0:T(8,128)(2,1)S(1)}, u32[]{:S(2)}, u32[]{:S(2)}) collective-permute-start(bf16[528,512]{1,0:T(8,128)(2,1)S(1)} %get-tuple-element.107), channel_id=1, source_target_pairs={{0,8},{4,12},{8,16},{12,20},{16,24},{20,28},{1,9},{5,13},{9,17},{1... | collective-permute-start | bytes 1622024 | tf_op jit(solution)/shard_map/ppermute | solution.py:34
  32.3 7.9 %collective-permute-done.4.two = bf16[528,768]{1,0:T(8,128)(2,1)S(1)} collective-permute-done((bf16[528,768]{1,0:T(8,128)(2,1)S(1)}, bf16[528,768]{1,0:T(8,128)(2,1)S(1)}, u32[]{:S(2)}, u32[]{:S(2)}) %collective-permute-start.4) | collective-permute-done | bytes 811040 | tf_op jit(solution)/shard_map/ppermute | solution.py:34
  40.2 2.4 %collective-permute-start.6 = (bf16[528,768]{1,0:T(8,128)(2,1)S(1)}, bf16[528,768]{1,0:T(8,128)(2,1)S(1)}, u32[]{:S(2)}, u32[]{:S(2)}) collective-permute-start(bf16[528,768]{1,0:T(8,128)(2,1)S(1)} %collective-permute-done.4.two), channel_id=1, source_target_pairs={{4,0},{12,8},{20,16},{28,24},{5,1},{13,9},{21,17},{29,25},{6,2},{1... | collective-permute-start | bytes 2433032 | tf_op jit(solution)/shard_map/ppermute | solution.py:44
  42.6 2.0 %own_piece.5 = (f32[256,512]{1,0:T(8,128)S(1)}, f32[2,512]{1,0:T(2,128)S(1)}, f32[2,512]{1,0:T(2,128)S(1)}, f32[256,512]{1,0:T(8,128)S(1)}, f32[8,128]{1,0:T(8,128)S(1)}) custom-call(f32[8,128]{1,0:T(8,128)S(1)} %get-tuple-element.84.refs_0_, bf16[512,1024]{1,0:T(8,128)(2,1)S(1)} %copy-done, bf16[512,1024]{1,0:T(8,128)(2,1)S(1)} %copy-done.1, ...), custom_call_target="tpu_custom_call" | custom-call | bytes 5904000 | tf_op jit(solution)/shard_map/own_piece/pallas_call | solution.py:463
  44.6 0.0 collective-permute-done.1.q_ref.keep_ref
  44.6 0.0 collective-permute-done.3.odd
  44.6 3.5 %far_pieces.3 = (bf16[400,640]{1,0:T(8,128)(2,1)S(1)}, f32[8,128]{1,0:T(8,128)S(1)}) custom-call(f32[8,128]{1,0:T(8,128)S(1)} %get-tuple-element.85.token_in, s32[8,512]{1,0:T(8,128)S(1)} %get-tuple-element.86.entry_ref, bf16[528,1024]{1,0:T(8,128)(2,1)S(1)} %collective-permute-done.1.q_ref.keep_ref, ...), custom_call_target="tpu_custom_call" | custom-call | bytes 16605000 | tf_op jit(solution)/shard_map/far_pieces/pallas_call | solution.py:463
  48.2 4.1 %near_pieces.3 = (f32[384,512]{1,0:T(8,128)S(1)}, f32[384,512]{1,0:T(8,128)S(1)}, f32[8,512]{1,0:T(8,128)S(1)}, f32[8,128]{1,0:T(8,128)S(1)}) custom-call(f32[8,128]{1,0:T(8,128)S(1)} %get-tuple-element.89.token_in, s32[8,512]{1,0:T(8,128)S(1)} %get-tuple-element.86.entry_ref, bf16[512,1024]{1,0:T(8,128)(2,1)S(1)} %copy-done, ...), custom_call_target="tpu_custom_call" | custom-call | bytes 19926000 | tf_op jit(solution)/shard_map/near_pieces/pallas_call | solution.py:463
  52.2 0.0 collective-permute-done.7.refs_0_
  52.2 1.8 %collective-permute-start.8 = (bf16[528,512]{1,0:T(8,128)(2,1)S(1)}, bf16[528,512]{1,0:T(8,128)(2,1)S(1)}, u32[]{:S(2)}, u32[]{:S(2)}) collective-permute-start(bf16[528,512]{1,0:T(8,128)(2,1)S(1)} %gate.1.two), channel_id=1, source_target_pairs={{4,0},{12,8},{20,16},{28,24},{5,1},{13,9},{21,17},{29,25},{6,2},{1... | collective-permute-start | bytes 1622024 | tf_op jit(solution)/shard_map/ppermute | solution.py:44
  54.0 4.4 %collective-permute-start.9 = (bf16[400,640]{1,0:T(8,128)(2,1)S(1)}, bf16[400,640]{1,0:T(8,128)(2,1)S(1)}, u32[]{:S(2)}, u32[]{:S(2)}) collective-permute-start(bf16[400,640]{1,0:T(8,128)(2,1)S(1)} %get-tuple-element.119), channel_id=1, source_target_pairs={{0,8},{4,12},{8,16},{12,20},{16,24},{20,28},{1,9},{5,13},{9,17},{1... | collective-permute-start | bytes 1536008 | tf_op jit(solution)/shard_map/ppermute | solution.py:34
  58.4 1.9 %far_earlier.1 = (f32[384,512]{1,0:T(8,128)S(1)}, f32[3,512]{1,0:T(4,128)S(1)}, f32[3,512]{1,0:T(4,128)S(1)}, f32[8,128]{1,0:T(8,128)S(1)}) custom-call(f32[8,128]{1,0:T(8,128)S(1)} %get-tuple-element.95.token_in.refs_1_, bf16[528,1024]{1,0:T(8,128)(2,1)S(1)} %collective-permute-done.1.q_ref.keep_ref, ...), custom_call_target="tpu_custom_call" | custom-call | bytes 7748999 | tf_op jit(solution)/shard_map/far_earlier/pallas_call | solution.py:463
  60.2 1.9 %earlier_piece.1 = (f32[384,512]{1,0:T(8,128)S(1)}, f32[3,512]{1,0:T(4,128)S(1)}, f32[3,512]{1,0:T(4,128)S(1)}, f32[8,128]{1,0:T(8,128)S(1)}) custom-call(f32[8,128]{1,0:T(8,128)S(1)} %get-tuple-element.97.token_in, bf16[512,1024]{1,0:T(8,128)(2,1)S(1)} %copy-done, s32[20,512]{1,0:T(8,128)S(1)} %get-tuple-element.75.refs_4_.refs_5_.thr_ref, ...), custom_call_target="tpu_custom_call" | custom-call | bytes 8856000 | tf_op jit(solution)/shard_map/earlier_piece/pallas_call | solution.py:463
  62.1 0.0 collective-permute-done.5.even
  62.1 0.0 collective-permute-done.6.odd
  62.1 2.2 %far_pieces.4 = (bf16[400,640]{1,0:T(8,128)(2,1)S(1)}, f32[8,128]{1,0:T(8,128)S(1)}) custom-call(f32[8,128]{1,0:T(8,128)S(1)} %get-tuple-element.101.token_in, s32[8,512]{1,0:T(8,128)S(1)} %get-tuple-element.86.entry_ref, bf16[528,1024]{1,0:T(8,128)(2,1)S(1)} %collective-permute-done.1.q_ref.keep_ref, ...), custom_call_target="tpu_custom_call" | custom-call | bytes 16605000 | tf_op jit(solution)/shard_map/far_pieces/pallas_call | solution.py:463
  64.3 3.2 %collective-permute-start.10 = (bf16[400,640]{1,0:T(8,128)(2,1)S(1)}, bf16[400,640]{1,0:T(8,128)(2,1)S(1)}, u32[]{:S(2)}, u32[]{:S(2)}) collective-permute-start(bf16[400,640]{1,0:T(8,128)(2,1)S(1)} %get-tuple-element.125), channel_id=1, source_target_pairs={{0,8},{4,12},{8,16},{12,20},{16,24},{20,28},{1,9},{5,13},{9,17},{1... | collective-permute-start | bytes 1536008 | tf_op jit(solution)/shard_map/ppermute | solution.py:34
  67.5 1.3 %collective-permute-done.8.odd = bf16[528,512]{1,0:T(8,128)(2,1)S(1)} collective-permute-done((bf16[528,512]{1,0:T(8,128)(2,1)S(1)}, bf16[528,512]{1,0:T(8,128)(2,1)S(1)}, u32[]{:S(2)}, u32[]{:S(2)}) %collective-permute-start.8) | collective-permute-done | bytes 540704 | tf_op jit(solution)/shard_map/ppermute | solution.py:44
  68.8 2.4 %far_pieces.5 = (bf16[272,640]{1,0:T(8,128)(2,1)S(1)}, f32[8,128]{1,0:T(8,128)S(1)}) custom-call(f32[8,128]{1,0:T(8,128)S(1)} %get-tuple-element.106.token_in, s32[8,512]{1,0:T(8,128)S(1)} %get-tuple-element.86.entry_ref, bf16[528,1024]{1,0:T(8,128)(2,1)S(1)} %collective-permute-done.1.q_ref.keep_ref, ...), custom_call_target="tpu_custom_call" | custom-call | bytes 11070000 | tf_op jit(solution)/shard_map/far_pieces/pallas_call | solution.py:463
  71.3 4.2 %collective-permute-start.11 = (bf16[272,640]{1,0:T(8,128)(2,1)S(1)}, bf16[272,640]{1,0:T(8,128)(2,1)S(1)}, u32[]{:S(2)}, u32[]{:S(2)}) collective-permute-start(bf16[272,640]{1,0:T(8,128)(2,1)S(1)} %get-tuple-element.131), channel_id=1, source_target_pairs={{0,8},{4,12},{8,16},{12,20},{16,24},{20,28},{1,9},{5,13},{9,17},{1... | collective-permute-start | bytes 1044488 | tf_op jit(solution)/shard_map/ppermute | solution.py:34
  75.5 2.7 %near_pieces.4 = (f32[384,512]{1,0:T(8,128)S(1)}, f32[384,512]{1,0:T(8,128)S(1)}, f32[8,512]{1,0:T(8,128)S(1)}, f32[8,128]{1,0:T(8,128)S(1)}) custom-call(f32[8,128]{1,0:T(8,128)S(1)} %get-tuple-element.108.token_in, s32[8,512]{1,0:T(8,128)S(1)} %get-tuple-element.86.entry_ref, bf16[512,1024]{1,0:T(8,128)(2,1)S(1)} %copy-done, ...), custom_call_target="tpu_custom_call" | custom-call | bytes 19926000 | tf_op jit(solution)/shard_map/near_pieces/pallas_call | solution.py:463
  78.1 2.8 %near_pieces.5 = (f32[256,512]{1,0:T(8,128)S(1)}, f32[256,512]{1,0:T(8,128)S(1)}, f32[8,512]{1,0:T(8,128)S(1)}, f32[8,128]{1,0:T(8,128)S(1)}) custom-call(f32[8,128]{1,0:T(8,128)S(1)} %get-tuple-element.113.token_in, s32[8,512]{1,0:T(8,128)S(1)} %get-tuple-element.86.entry_ref, bf16[512,1024]{1,0:T(8,128)(2,1)S(1)} %copy-done, ...), custom_call_target="tpu_custom_call" | custom-call | bytes 13284000 | tf_op jit(solution)/shard_map/near_pieces/pallas_call | solution.py:463
  81.0 0.0 collective-permute-done.9.pay_ref
  81.0 0.5 merge.3
  81.5 0.0 collective-permute-done.10.pay_ref
  81.5 0.5 merge.4
  82.1 0.0 copy-start.5
  82.1 4.2 %collective-permute-done.11.pay_ref = bf16[272,640]{1,0:T(8,128)(2,1)S(1)} collective-permute-done((bf16[272,640]{1,0:T(8,128)(2,1)S(1)}, bf16[272,640]{1,0:T(8,128)(2,1)S(1)}, u32[]{:S(2)}, u32[]{:S(2)}) %collective-permute-start.11) | collective-permute-done | bytes 348192 | tf_op jit(solution)/shard_map/ppermute | solution.py:34
  86.3 0.9 merge.5
  87.2 7.1 %all_gather.3 = f32[4,4,128]{2,1,0:T(4,128)S(1)} all-gather(f32[1,4,128]{2,1,0:T(4,128)S(1)} %bitcast.11), channel_id=1, replica_groups=mesh['ctx'=8,'head'=4] {'head'}, dimensions={0}, use_global_device_ids=true | all-gather | bytes 10240 | tf_op jit(solution)/shard_map/all_gather | solution.py:657
  94.3 0.0 copy-done.5
  94.3 1.3 %normalize.1 = bf16[512,1024]{1,0:T(8,128)(2,1)} custom-call(f32[512,384]{1,0:T(8,128)S(1)} %get-tuple-element.123.refs_0_, f32[512,384]{1,0:T(8,128)S(1)} %get-tuple-element.129.refs_1_, f32[512,256]{1,0:T(8,128)S(1)} %get-tuple-element.135.refs_2_, f32[4,512]{1,0:T(4,128)S(1)} %bitcast.7, f32[1,1024]{1,0:T(1,128)S(1)} %bitcast.8), custom_call_target="tpu_custom_call" | custom-call | tf_op jit(solution)/shard_map/normalize/pallas_call | solution.py:659
  (3 shorter events, 0.0 us)
Async XLA Ops:
  0.0 7.3 %copy-start.4 = (f32[8,512]{1,0:T(8,128)S(1)}, f32[8,512]{1,0:T(8,128)}, u32[]{:S(2)}) copy-start(f32[8,512]{1,0:T(8,128)} %ld_ref.1) | copy-start | bytes 49156
  0.0 8.4 %copy-start.1 = (bf16[512,1024]{1,0:T(8,128)(2,1)S(1)}, bf16[512,1024]{1,0:T(8,128)(2,1)}, u32[]{:S(2)}) copy-start(bf16[512,1024]{1,0:T(8,128)(2,1)} %refs_2_.5) | copy-start | bytes 3145732
  0.0 7.3 %copy-start.8 = (s32[8]{0:T(128)S(1)}, s32[8]{0:T(128)}, u32[]{:S(2)}) copy-start(s32[8]{0:T(128)} %param.11) | copy-start | bytes 100
  0.0 7.3 %copy-start.7 = (s32[4,20]{1,0:T(4,128)S(1)}, s32[4,20]{1,0:T(4,128)}, u32[]{:S(2)}) copy-start(s32[4,20]{1,0:T(4,128)} %mask_ref.1) | copy-start | bytes 964
  0.0 8.4 %copy-start = (bf16[512,1024]{1,0:T(8,128)(2,1)S(1)}, bf16[512,1024]{1,0:T(8,128)(2,1)}, u32[]{:S(2)}) copy-start(bf16[512,1024]{1,0:T(8,128)(2,1)} %q_ref.15) | copy-start | bytes 3145732
  2.7 20.2 %collective-permute-start = (bf16[528,768]{1,0:T(8,128)(2,1)}, bf16[528,768]{1,0:T(8,128)(2,1)S(1)}, u32[]{:S(2)}, u32[]{:S(2)}) collective-permute-start(bf16[528,768]{1,0:T(8,128)(2,1)} %get-tuple-element.72), channel_id=1, source_target_pairs={{0,8},{4,12},{8,16},{12,20},{16,24},{20,28},{1,9},{5,13},{9,17},{1... | collective-permute-start | bytes 2433032 | tf_op jit(solution)/shard_map/ppermute | solution.py:34
  6.0 22.3 %collective-permute-start.2 = (bf16[528,768]{1,0:T(8,128)(2,1)}, bf16[528,768]{1,0:T(8,128)(2,1)S(1)}, u32[]{:S(2)}, u32[]{:S(2)}) collective-permute-start(bf16[528,768]{1,0:T(8,128)(2,1)} %get-tuple-element.72), channel_id=1, source_target_pairs={{0,4},{8,12},{16,20},{24,28},{1,5},{9,13},{17,21},{25,29},{2,6},{1... | collective-permute-start | bytes 2433032 | tf_op jit(solution)/shard_map/ppermute | solution.py:39
  7.3 0.7 copy-start.6
  8.4 1.2 %copy-start.2 = (bf16[512,1024]{1,0:T(8,128)(2,1)S(1)}, bf16[512,1024]{1,0:T(8,128)(2,1)}, u32[]{:S(2)}) copy-start(bf16[512,1024]{1,0:T(8,128)(2,1)} %refs_3_.5) | copy-start | bytes 3145732
  9.6 3.0 %copy-start.3 = (bf16[512,1024]{1,0:T(8,128)(2,1)S(1)}, bf16[512,1024]{1,0:T(8,128)(2,1)}, u32[]{:S(2)}) copy-start(bf16[512,1024]{1,0:T(8,128)(2,1)} %refs_3_.5) | copy-start | bytes 3145732
  13.1 27.1 %collective-permute-start.4 = (bf16[528,768]{1,0:T(8,128)(2,1)S(1)}, bf16[528,768]{1,0:T(8,128)(2,1)S(1)}, u32[]{:S(2)}, u32[]{:S(2)}) collective-permute-start(bf16[528,768]{1,0:T(8,128)(2,1)S(1)} %get-tuple-element.96), channel_id=1, source_target_pairs={{0,8},{4,12},{8,16},{12,20},{16,24},{20,28},{1,9},{5,13},{9,17},{1... | collective-permute-start | bytes 2433032 | tf_op jit(solution)/shard_map/ppermute | solution.py:34
  16.3 28.3 %collective-permute-start.1 = (bf16[528,1024]{1,0:T(8,128)(2,1)S(1)}, bf16[528,1024]{1,0:T(8,128)(2,1)S(1)}, u32[]{:S(2)}, u32[]{:S(2)}) collective-permute-start(bf16[528,1024]{1,0:T(8,128)(2,1)S(1)} %get-tuple-element.87), channel_id=1, source_target_pairs={{8,0},{12,4},{16,8},{20,12},{24,16},{28,20},{9,1},{13,5},{17,9},{2... | collective-permute-start | bytes 3244040 | tf_op jit(solution)/shard_map/ppermute | solution.py:34
  17.6 44.5 %collective-permute-start.5 = (bf16[544,1280]{1,0:T(8,128)(2,1)S(1)}, bf16[544,1280]{1,0:T(8,128)(2,1)S(1)}, u32[]{:S(2)}, u32[]{:S(2)}) collective-permute-start(bf16[544,1280]{1,0:T(8,128)(2,1)S(1)} %get-tuple-element.102), channel_id=1, source_target_pairs={{0,4},{8,12},{16,20},{24,28},{1,5},{9,13},{17,21},{25,29},{2,6},{1... | collective-permute-start | bytes 4177928 | tf_op jit(solution)/shard_map/ppermute | solution.py:39
  23.0 21.7 %collective-permute-start.3 = (bf16[528,768]{1,0:T(8,128)(2,1)S(1)}, bf16[528,768]{1,0:T(8,128)(2,1)S(1)}, u32[]{:S(2)}, u32[]{:S(2)}) collective-permute-start(bf16[528,768]{1,0:T(8,128)(2,1)S(1)} %collective-permute-done.refs_0_.two), channel_id=1, source_target_pairs={{4,0},{12,8},{20,16},{28,24},{5,1},{13,9},{21,17},{29,25},{6,2},{1... | collective-permute-start | bytes 2433032 | tf_op jit(solution)/shard_map/ppermute | solution.py:44
  28.3 23.9 %collective-permute-start.7 = (bf16[528,512]{1,0:T(8,128)(2,1)S(1)}, bf16[528,512]{1,0:T(8,128)(2,1)S(1)}, u32[]{:S(2)}, u32[]{:S(2)}) collective-permute-start(bf16[528,512]{1,0:T(8,128)(2,1)S(1)} %get-tuple-element.107), channel_id=1, source_target_pairs={{0,8},{4,12},{8,16},{12,20},{16,24},{20,28},{1,9},{5,13},{9,17},{1... | collective-permute-start | bytes 1622024 | tf_op jit(solution)/shard_map/ppermute | solution.py:34
  40.2 21.9 %collective-permute-start.6 = (bf16[528,768]{1,0:T(8,128)(2,1)S(1)}, bf16[528,768]{1,0:T(8,128)(2,1)S(1)}, u32[]{:S(2)}, u32[]{:S(2)}) collective-permute-start(bf16[528,768]{1,0:T(8,128)(2,1)S(1)} %collective-permute-done.4.two), channel_id=1, source_target_pairs={{4,0},{12,8},{20,16},{28,24},{5,1},{13,9},{21,17},{29,25},{6,2},{1... | collective-permute-start | bytes 2433032 | tf_op jit(solution)/shard_map/ppermute | solution.py:44
  52.2 16.6 %collective-permute-start.8 = (bf16[528,512]{1,0:T(8,128)(2,1)S(1)}, bf16[528,512]{1,0:T(8,128)(2,1)S(1)}, u32[]{:S(2)}, u32[]{:S(2)}) collective-permute-start(bf16[528,512]{1,0:T(8,128)(2,1)S(1)} %gate.1.two), channel_id=1, source_target_pairs={{4,0},{12,8},{20,16},{28,24},{5,1},{13,9},{21,17},{29,25},{6,2},{1... | collective-permute-start | bytes 1622024 | tf_op jit(solution)/shard_map/ppermute | solution.py:44
  54.0 26.9 %collective-permute-start.9 = (bf16[400,640]{1,0:T(8,128)(2,1)S(1)}, bf16[400,640]{1,0:T(8,128)(2,1)S(1)}, u32[]{:S(2)}, u32[]{:S(2)}) collective-permute-start(bf16[400,640]{1,0:T(8,128)(2,1)S(1)} %get-tuple-element.119), channel_id=1, source_target_pairs={{0,8},{4,12},{8,16},{12,20},{16,24},{20,28},{1,9},{5,13},{9,17},{1... | collective-permute-start | bytes 1536008 | tf_op jit(solution)/shard_map/ppermute | solution.py:34
  64.3 17.2 %collective-permute-start.10 = (bf16[400,640]{1,0:T(8,128)(2,1)S(1)}, bf16[400,640]{1,0:T(8,128)(2,1)S(1)}, u32[]{:S(2)}, u32[]{:S(2)}) collective-permute-start(bf16[400,640]{1,0:T(8,128)(2,1)S(1)} %get-tuple-element.125), channel_id=1, source_target_pairs={{0,8},{4,12},{8,16},{12,20},{16,24},{20,28},{1,9},{5,13},{9,17},{1... | collective-permute-start | bytes 1536008 | tf_op jit(solution)/shard_map/ppermute | solution.py:34
  71.3 15.0 %collective-permute-start.11 = (bf16[272,640]{1,0:T(8,128)(2,1)S(1)}, bf16[272,640]{1,0:T(8,128)(2,1)S(1)}, u32[]{:S(2)}, u32[]{:S(2)}) collective-permute-start(bf16[272,640]{1,0:T(8,128)(2,1)S(1)} %get-tuple-element.131), channel_id=1, source_target_pairs={{0,8},{4,12},{8,16},{12,20},{16,24},{20,28},{1,9},{5,13},{9,17},{1... | collective-permute-start | bytes 1044488 | tf_op jit(solution)/shard_map/ppermute | solution.py:34
  82.1 12.2 %copy-start.5 = (f32[1024]{0:T(1024)S(1)}, f32[1024]{0:T(1024)}, u32[]{:S(2)}) copy-start(f32[1024]{0:T(1024)} %param.13) | copy-start | bytes 12292
